TPU v7x, 32 devices: a whole 2x2x4 slice. The times are simulated.
32 devices in a mesh: group: 2 (over x), expert: 4 (over y, core), tensor: 4 (over z).
Axes of the slice: x: 2, y: 2, z: 4, core: 2. Of those that a mesh axis runs over, the one named last changes fastest.
Arguments:
- x_tokens: bfloat16 [256, 3072], P(('group', 'expert', 'tensor')), parts along dimension 0, may hold values from -6 to 6
- grad_values: bfloat16 [256, 3072], P(('group', 'expert', 'tensor')), parts along dimension 0, may hold values from -6 to 6
- grad_scale: float32 [256], P(('group', 'expert', 'tensor')), parts along dimension 0, may hold values from 0.05 to 1
- combine: float32 [256, 2], P(('group', 'expert', 'tensor')), parts along dimension 0, may hold values from 0.1 to 0.9
- routes: int32 [256, 2], P(('group', 'expert', 'tensor')), parts along dimension 0, may hold values from 0 to 3, all different within a row; in each aligned block of 8 rows (0 to 7, 8 to 15, ...) at most 5 rows name the same one
- pattern: int32 [4, 768], replicated, may hold values from 0 to 5
- w_gate: bfloat16 [1536, 32768], P(None, ('expert', 'tensor')), may hold values from -0.15625 to 0.15625
- w_up: bfloat16 [1536, 32768], P(None, ('expert', 'tensor')), may hold values from -0.15625 to 0.15625
- w_down: bfloat16 [32768, 1536], P(('expert', 'tensor')), may hold values from -0.0625 to 0.0625
Outputs:
- grad_tokens: bfloat16 [256, 3072], P(('group', 'expert', 'tensor')), parts along dimension 0
- grad_gate: bfloat16 [3072, 32768], P('group', ('expert', 'tensor')), parts along dimension 0
- grad_up: bfloat16 [3072, 32768], P('group', ('expert', 'tensor')), parts along dimension 0
- grad_down: bfloat16 [32768, 3072], P(('expert', 'tensor'), 'group'), parts along dimension 1
There are 2 independent parts, one for each index of `group`. A program takes and returns all parts, laid end to end along the dimension named above; an argument that names none is the same for every part. Nothing has to cross between parts.
Inputs may be any that keep to these rules, and one draw needn't show every extreme that they name: `routes`: in the rows of one device (8 aligned rows), no expert is named by more than 5 rows, and some device's rows name one expert exactly 5 times; a token's two experts differ.
All inputs are finite; a program needn't handle non-finite values.
Results may differ from a plain program's by a relative error of at most 0.0058.
Values may be sent and summed in bfloat16 or wider, within the bound.
No kernel may reach another device: no remote copies, remote signals or barrier semaphores. Data moves between devices by JAX's collectives and lax.ppermute only.
A program may use at most 128 MiB of HBM per device.

v0:
```python
import jax
import jax.numpy as jnp
from jax import lax
from jax.sharding import PartitionSpec as P

MOST = 5


def kept_columns(pattern):
    pattern_codes = jnp.arange(6, dtype=jnp.int32)
    onehot = (pattern[..., None] == pattern_codes).astype(jnp.int32)
    first_pos = jnp.sum(
        onehot * jnp.array([0, 0, 0, 1, 1, 2], dtype=jnp.int32), axis=-1, dtype=jnp.int32
    )
    second_pos = jnp.sum(
        onehot * jnp.array([1, 2, 3, 2, 3, 3], dtype=jnp.int32), axis=-1, dtype=jnp.int32
    )
    group_base = 4 * jnp.arange(pattern.shape[-1], dtype=jnp.int32)
    kept_pairs = jnp.stack([group_base + first_pos, group_base + second_pos], axis=-1)
    return kept_pairs.reshape(pattern.shape[0], -1)


def contract(left, right, dims):
    return lax.dot_general(left, right, dims, preferred_element_type=jnp.float32)


def expert_rows(rows_in, rows_grad, w_gate, w_up, w_down):
    contract_last = (((1,), (1,)), ((), ()))
    contract_first = (((0,), (0,)), ((), ()))
    plain = (((1,), (0,)), ((), ()))
    gate_pre = contract(rows_in, w_gate, plain)
    up_pre = contract(rows_in, w_up, plain)
    sigmoid_gate = jax.nn.sigmoid(gate_pre)
    silu_gate = gate_pre * sigmoid_gate
    hidden = (silu_gate * up_pre).astype(jnp.bfloat16)
    grad_hidden = contract(rows_grad, w_down, contract_last)
    grad_gate_pre = (
        grad_hidden * up_pre * sigmoid_gate * (1.0 + gate_pre * (1.0 - sigmoid_gate))
    ).astype(jnp.bfloat16)
    grad_up_pre = (grad_hidden * silu_gate).astype(jnp.bfloat16)
    part_gate = contract(rows_in, grad_gate_pre, contract_first)
    part_up = contract(rows_in, grad_up_pre, contract_first)
    part_down = contract(hidden, rows_grad, contract_first)
    back_rows = contract(grad_gate_pre, w_gate, contract_last)
    back_rows = back_rows + contract(grad_up_pre, w_up, contract_last)
    return ((part_gate, part_up, part_down), back_rows)


def body(x_tokens, grad_values, grad_scale, combine, routes, pattern, w_gate, w_up, w_down):
    tokens_here = x_tokens.shape[0]
    experts = pattern.shape[0]
    kept_width = w_gate.shape[0]
    capacity = MOST
    expert_count = lax.axis_size("expert")
    tensor_count = lax.axis_size("tensor")
    holders = expert_count // experts
    kept = kept_columns(pattern)
    slot_ids = jnp.arange(capacity, dtype=jnp.int32)
    token_ids = jnp.arange(tokens_here, dtype=jnp.int32)
    send_in = []
    send_grad = []
    send_tokens = []
    for expert in range(experts):
        chosen_pair = routes == expert
        chosen = jnp.any(chosen_pair, axis=1)
        weight = jnp.sum(chosen_pair.astype(jnp.float32) * combine, axis=1) * grad_scale
        position = jnp.cumsum(chosen.astype(jnp.int32), dtype=jnp.int32) - 1
        matches = chosen[None, :] & (position[None, :] == slot_ids[:, None])
        filled = jnp.any(matches, axis=1)
        token_slot = jnp.sum(jnp.where(matches, token_ids[None, :], 0), axis=1, dtype=jnp.int32)
        columns = kept[expert]
        picked_in = jnp.take(x_tokens[token_slot], columns, axis=1)
        picked_in = jnp.where(filled[:, None], picked_in, jnp.zeros_like(picked_in))
        picked_grad = weight[token_slot][:, None] * jnp.take(
            grad_values[token_slot], columns, axis=1
        ).astype(jnp.float32)
        picked_grad = jnp.where(filled[:, None], picked_grad, 0.0).astype(jnp.bfloat16)
        send_in.append(picked_in)
        send_grad.append(picked_grad)
        send_tokens.append(jnp.where(filled, token_slot, tokens_here))
    send_in = jnp.stack(send_in, axis=0)
    send_grad = jnp.stack(send_grad, axis=0)
    spread = holders * tensor_count
    out_in = jnp.repeat(send_in, spread, axis=0)
    out_grad = jnp.repeat(send_grad, spread, axis=0)
    recv_in, recv_grad = (
        lax.all_to_all(out_in, ("expert", "tensor"), split_axis=0, concat_axis=0, tiled=True),
        lax.all_to_all(out_grad, ("expert", "tensor"), split_axis=0, concat_axis=0, tiled=True),
    )
    parts, back_rows = expert_rows(
        recv_in.reshape(-1, kept_width), recv_grad.reshape(-1, kept_width), w_gate, w_up, w_down
    )
    part_gate, part_up, part_down = parts
    returned = lax.all_to_all(
        back_rows.reshape(recv_in.shape),
        ("expert", "tensor"),
        split_axis=0,
        concat_axis=0,
        tiled=True,
    )
    partial_value = returned.reshape(experts, spread, capacity, kept_width).sum(axis=1)
    grad_sum = jnp.zeros((tokens_here, x_tokens.shape[1]), jnp.float32)
    for expert in range(experts):
        grad_sum = grad_sum.at[send_tokens[expert][:, None], kept[expert][None, :]].add(
            partial_value[expert], mode="drop"
        )
    grad_tokens = grad_sum.astype(jnp.bfloat16)
    return (
        grad_tokens,
        part_gate.astype(jnp.bfloat16),
        part_up.astype(jnp.bfloat16),
        part_down.astype(jnp.bfloat16),
    )


def solution(mesh):
    in_specs = (
        P(("group", "expert", "tensor"), None),
        P(("group", "expert", "tensor"), None),
        P(("group", "expert", "tensor")),
        P(("group", "expert", "tensor"), None),
        P(("group", "expert", "tensor"), None),
        P(),
        P(None, ("expert", "tensor")),
        P(None, ("expert", "tensor")),
        P(("expert", "tensor"), None),
    )
    out_specs = (
        P(("group", "expert", "tensor"), None),
        P("group", ("expert", "tensor")),
        P("group", ("expert", "tensor")),
        P(("expert", "tensor"), "group"),
    )
    return jax.shard_map(body, mesh=mesh, in_specs=in_specs, out_specs=out_specs, check_vma=False)
```

profile of v0, /device:TPU:0, one launch (start us, length us, event | category | flops | bytes accessed | tf_op | source)
XLA Modules:
  0.0 328.2 jit_solution(16544565453471960643)
XLA Ops:
  0.6 0.7 fusion.28
  2.8 0.8 select_reduce_fusion
  5.5 0.6 gather_fusion.11
  6.1 0.6 gather_fusion.10
  6.7 0.6 gather_fusion.9
  7.3 0.6 gather_fusion.8
  7.9 0.4 copy.70
  8.3 0.4 copy.71
  8.7 0.4 copy.72
  9.2 0.4 copy.73
  9.6 4.1 %gather_fusion.16 = bf16[1536,5]{1,0:T(8,128)(2,1)} fusion(bf16[5,3072]{0,1:T(8,128)(2,1)S(1)} %copy.70, s32[2048]{0:T(1024)S(1)} %pad_clamp_fusion.3), kind=kCustom, calls=%fused_computation.4.clone | custom fusion | bytes 36864 | tf_op jit(solution)/shard_map/jit(_take)/gather | solution.py:72
  13.7 3.2 gather_fusion.17
  16.9 3.2 gather_fusion.18
  20.1 3.2 gather_fusion.19
  23.3 1.3 fusion.8
  24.6 0.3 fusion.7
  25.5 0.4 pad_maximum_fusion.1
  25.9 0.7 copy.74
  26.6 0.8 broadcast_in_dim.208
  27.4 7.4 %all-to-all-start.1 = ((bf16[16,5,1536]{2,1,0:T(8,128)(2,1)}), bf16[16,5,1536]{2,1,0:T(8,128)(2,1)S(1)}, u32[]{:S(2)}, u32[]{:S(2)}) async-start(bf16[16,5,1536]{2,1,0:T(8,128)(2,1)} %bitcast.35), calls=%async_computation.1 | async-start | bytes 786432 | tf_op jit(solution)/shard_map/all_to_all | solution.py:87
  34.8 0.6 gather_fusion.7
  35.4 0.6 gather_fusion.5
  36.0 0.6 gather_fusion.3
  36.6 0.6 gather_fusion.1
  37.2 0.6 gather_fusion
  37.9 0.6 gather_fusion.2
  38.5 0.6 gather_fusion.4
  39.2 0.6 gather_fusion.6
  40.3 0.6 and_reduce_fusion
  40.9 0.5 multiply_reduce_fusion
  41.3 0.4 copy.62
  41.7 3.2 gather_fusion.12
  45.0 0.4 copy.64
  45.4 3.2 gather_fusion.13
  48.6 0.4 copy.66
  49.0 4.1 %gather_fusion.14 = bf16[1536,5]{1,0:T(8,128)(2,1)} fusion(bf16[5,3072]{0,1:T(8,128)(2,1)S(1)} %copy.66, s32[2048]{0:T(1024)S(1)} %pad_clamp_fusion.1), kind=kCustom, calls=%fused_computation.2.clone | custom fusion | bytes 36864 | tf_op jit(solution)/shard_map/jit(_take)/gather | solution.py:74
  53.1 0.4 copy.68
  53.5 4.1 %gather_fusion.15 = bf16[1536,5]{1,0:T(8,128)(2,1)} fusion(bf16[5,3072]{0,1:T(8,128)(2,1)S(1)} %copy.68, s32[2048]{0:T(1024)S(1)} %pad_clamp_fusion), kind=kCustom, calls=%fused_computation.3.clone | custom fusion | bytes 36864 | tf_op jit(solution)/shard_map/jit(_take)/gather | solution.py:74
  57.9 0.3 fusion.2
  58.2 1.3 fusion.3
  59.4 2.0 fusion.4
  61.5 0.6 reshape.609
  62.1 1.4 pad_maximum_fusion
  63.5 0.7 copy.69
  64.3 0.8 broadcast_in_dim.207
  65.1 6.0 %all-to-all-start = ((bf16[16,5,1536]{2,1,0:T(8,128)(2,1)}), bf16[16,5,1536]{2,1,0:T(8,128)(2,1)S(1)}, u32[]{:S(2)}, u32[]{:S(2)}) async-start(bf16[16,5,1536]{2,1,0:T(8,128)(2,1)} %bitcast.26), calls=%async_computation | async-start | bytes 786432 | tf_op jit(solution)/shard_map/all_to_all | solution.py:88
  71.2 4.0 %fusion.35 = f32[80,2048]{1,0:T(8,128)S(1)} fusion(bf16[80,1536]{1,0:T(8,128)(2,1)S(1)} %reshape.422, bf16[1536,2048]{1,0:T(8,128)(2,1)} %param.19), kind=kOutput, calls=%fused_computation.154 | convolution fusion | flops 503316480 | bytes 7192576 | tf_op jit(solution)/shard_map/dot_general | solution.py:24
  75.2 5.0 %fusion.34 = f32[80,2048]{1,0:T(8,128)} fusion(bf16[80,1536]{1,0:T(8,128)(2,1)S(1)} %reshape.422, bf16[1536,2048]{1,0:T(8,128)(2,1)} %param.20), kind=kOutput, calls=%fused_computation.153 | convolution fusion | flops 503316480 | bytes 7192576 | tf_op jit(solution)/shard_map/dot_general | solution.py:24
  80.2 3.8 %all-to-all-done = bf16[16,5,1536]{2,1,0:T(8,128)(2,1)S(1)} async-done(((bf16[16,5,1536]{2,1,0:T(8,128)(2,1)}), bf16[16,5,1536]{2,1,0:T(8,128)(2,1)S(1)}, u32[]{:S(2)}, u32[]{:S(2)}) %all-to-all-start) | async-done | bytes 245792 | tf_op jit(solution)/shard_map/all_to_all | solution.py:88
  83.9 0.8 reshape.420
  84.8 5.2 %multiply_convert_fusion.1 = (bf16[80,2048]{1,0:T(8,128)(2,1)S(1)}, bf16[80,2048]{1,0:T(8,128)(2,1)S(1)}) fusion(f32[80,2048]{1,0:T(8,128)S(1)} %fusion.35, f32[80,2048]{1,0:T(8,128)} %fusion.34, bf16[80,1536]{1,0:T(8,128)(2,1)} %reshape.420, bf16[2048,1536]{1,0:T(8,128)(2,1)} %param.21), kind=kOutput, calls=%fused_computation.36 | convolution fusion | flops 505446400 | bytes 8503296 | tf_op jit(solution)/shard_map/dot_general | solution.py:24
  90.0 2.0 fusion.36
  92.0 4.8 %convolution_add_fusion = f32[80,1536]{1,0:T(8,128)S(1)} fusion(f32[80,1536]{1,0:T(8,128)S(1)} %fusion.36, bf16[80,2048]{1,0:T(8,128)(2,1)S(1)} %get-tuple-element.23, bf16[1536,2048]{1,0:T(8,128)(2,1)} %param.20), kind=kOutput, calls=%fused_computation.27 | convolution fusion | flops 503439360 | bytes 7602176 | tf_op jit(solution)/shard_map/dot_general | solution.py:24
  96.8 1.0 reshape.423
  97.8 3.9 %all-to-all-start.2 = ((f32[16,5,1536]{2,1,0:T(8,128)}), f32[16,5,1536]{2,1,0:T(8,128)S(1)}, u32[]{:S(2)}, u32[]{:S(2)}) async-start(f32[16,5,1536]{2,1,0:T(8,128)} %reshape.423), calls=%async_computation.2 | async-start | bytes 1572864 | tf_op jit(solution)/shard_map/all_to_all | solution.py:94
  101.7 5.5 %convolution_convert_fusion.1 = bf16[1536,2048]{1,0:T(8,128)(2,1)} fusion(bf16[80,1536]{1,0:T(8,128)(2,1)S(1)} %reshape.422, bf16[80,2048]{1,0:T(8,128)(2,1)} %copy-done.3), kind=kOutput, calls=%fused_computation.25 | convolution fusion | flops 506462208 | bytes 6864896 | tf_op jit(solution)/shard_map/dot_general | solution.py:24
  107.2 4.5 %convolution_convert_fusion.2 = bf16[1536,2048]{1,0:T(8,128)(2,1)} fusion(bf16[80,1536]{1,0:T(8,128)(2,1)S(1)} %reshape.422, bf16[80,2048]{1,0:T(8,128)(2,1)S(1)} %get-tuple-element.24), kind=kOutput, calls=%fused_computation.26 | convolution fusion | flops 506462208 | bytes 6864896 | tf_op jit(solution)/shard_map/dot_general | solution.py:24
  111.7 4.6 %convolution_convert_fusion = bf16[2048,1536]{1,0:T(8,128)(2,1)} fusion(bf16[80,1536]{1,0:T(8,128)(2,1)S(1)} %copy-done.4, f32[80,2048]{1,0:T(8,128)S(1)} %copy-done.2, f32[80,2048]{1,0:T(8,128)S(1)} %fusion.35), kind=kOutput, calls=%fused_computation.24 | convolution fusion | flops 507445248 | bytes 7847936 | tf_op jit(solution)/shard_map/dot_general | solution.py:24
  116.3 6.4 %all-to-all-done.2 = f32[16,5,1536]{2,1,0:T(8,128)S(1)} async-done(((f32[16,5,1536]{2,1,0:T(8,128)}), f32[16,5,1536]{2,1,0:T(8,128)S(1)}, u32[]{:S(2)}, u32[]{:S(2)}) %all-to-all-start.2) | async-done | bytes 491552 | tf_op jit(solution)/shard_map/all_to_all | solution.py:94
  122.8 51.1 %scatter_custom_fusion = f32[24576]{0:T(1024)S(1)} fusion(s32[7680]{0:T(1024)} %reshape.609, f32[7680]{0:T(1024)S(1)} %reshape.611, f32[]{:T(128)} %constant.21.clone.1), kind=kCustom, calls=%fused_computation.67 | custom fusion | flops 7680 | bytes 98816
  174.0 46.3 %scatter_fusion = f32[24576]{0:T(1024)S(1)} fusion(f32[24576]{0:T(1024)S(1)} %scatter_custom_fusion, s32[7680]{0:T(1024)S(1)} %reshape.615, f32[7680]{0:T(1024)S(1)} %reshape.617), kind=kCustom, calls=%fused_computation.21 | custom fusion | flops 7680 | bytes 122880
  220.3 53.6 %scatter_fusion.1 = f32[24576]{0:T(1024)S(1)} fusion(f32[24576]{0:T(1024)S(1)} %scatter_fusion, s32[7680]{0:T(1024)S(1)} %reshape.621, f32[7680]{0:T(1024)S(1)} %reshape.623), kind=kCustom, calls=%fused_computation.22 | custom fusion | flops 7680 | bytes 122880
  273.9 53.6 %scatter_fusion.2 = f32[24576]{0:T(1024)S(1)} fusion(f32[24576]{0:T(1024)S(1)} %scatter_fusion.1, s32[7680]{0:T(1024)S(1)} %reshape.627, f32[7680]{0:T(1024)S(1)} %reshape.629), kind=kCustom, calls=%fused_computation.23 | custom fusion | flops 7680 | bytes 122880
  327.5 0.6 reshape.448
  (105 shorter events, 4.8 us)
Async XLA Ops:
  0.6 4.9 %copy-start = (bf16[8,3072]{1,0:T(8,128)(2,1)S(1)}, bf16[8,3072]{1,0:T(8,128)(2,1)}, u32[]{:S(2)}) copy-start(bf16[8,3072]{1,0:T(8,128)(2,1)} %param.13) | copy-start | bytes 147460
  8.3 26.5 %copy-start.1 = (bf16[8,3072]{1,0:T(8,128)(2,1)S(1)}, bf16[8,3072]{1,0:T(8,128)(2,1)}, u32[]{:S(2)}) copy-start(bf16[8,3072]{1,0:T(8,128)(2,1)} %param.14) | copy-start | bytes 147460
  9.2 28.0 %copy-start.5 = (s32[8,2]{0,1:T(2,128)S(1)}, s32[8,2]{0,1:T(2,128)}, u32[]{:S(2)}) copy-start(s32[8,2]{0,1:T(2,128)} %param.17) | copy-start | bytes 196
  9.2 28.0 %copy-start.6 = (f32[8,2]{0,1:T(2,128)S(1)}, f32[8,2]{0,1:T(2,128)}, u32[]{:S(2)}) copy-start(f32[8,2]{0,1:T(2,128)} %param.16) | copy-start | bytes 196
  9.2 28.0 %copy-start.8 = (f32[8]{0:T(128)S(1)}, f32[8]{0:T(128)}, u32[]{:S(2)}) copy-start(f32[8]{0:T(128)} %param.15) | copy-start | bytes 100
  24.6 15.7 %copy-start.7 = (s32[2]{0:T(128)S(1)}, s32[2]{0:T(128)}, u32[]{:S(2)}) copy-start(s32[2]{0:T(128)} %constant.71) | copy-start | bytes 28
  24.6 16.2 %copy-start.9 = (s32[2]{0:T(128)S(1)}, s32[2]{0:T(128)}, u32[]{:S(2)}) copy-start(s32[2]{0:T(128)} %constant.68) | copy-start | bytes 28
  27.4 36.9 %all-to-all-start.1 = ((bf16[16,5,1536]{2,1,0:T(8,128)(2,1)}), bf16[16,5,1536]{2,1,0:T(8,128)(2,1)S(1)}, u32[]{:S(2)}, u32[]{:S(2)}) async-start(bf16[16,5,1536]{2,1,0:T(8,128)(2,1)} %bitcast.35), calls=%async_computation.1 | async-start | bytes 786432 | tf_op jit(solution)/shard_map/all_to_all | solution.py:87
  65.1 18.9 %all-to-all-start = ((bf16[16,5,1536]{2,1,0:T(8,128)(2,1)}), bf16[16,5,1536]{2,1,0:T(8,128)(2,1)S(1)}, u32[]{:S(2)}, u32[]{:S(2)}) async-start(bf16[16,5,1536]{2,1,0:T(8,128)(2,1)} %bitcast.26), calls=%async_computation | async-start | bytes 786432 | tf_op jit(solution)/shard_map/all_to_all | solution.py:88
  75.2 14.8 %slice-start = ((s8[6291456]{0:T(1024)(128)(4,1)}), s8[2097152]{0:T(1024)(128)(4,1)S(1)}, s32[]{:S(2)}) async-start(s8[6291456]{0:T(1024)(128)(4,1)} %bitcast.95), calls=%async_computation.3 | async-start | bytes 4194304
  84.8 5.2 %slice-start.1 = ((s8[6291456]{0:T(1024)(128)(4,1)}), s8[4194304]{0:T(1024)(128)(4,1)S(1)}, s32[]{:S(2)}) async-start(s8[6291456]{0:T(1024)(128)(4,1)} %bitcast.95), calls=%async_computation.4 | async-start | bytes 8388608
  89.9 2.1 copy-start.3
  97.8 24.9 %all-to-all-start.2 = ((f32[16,5,1536]{2,1,0:T(8,128)}), f32[16,5,1536]{2,1,0:T(8,128)S(1)}, u32[]{:S(2)}, u32[]{:S(2)}) async-start(f32[16,5,1536]{2,1,0:T(8,128)} %reshape.423), calls=%async_computation.2 | async-start | bytes 1572864 | tf_op jit(solution)/shard_map/all_to_all | solution.py:94
  107.2 4.5 %copy-start.2 = (f32[80,2048]{1,0:T(8,128)S(1)}, f32[80,2048]{1,0:T(8,128)}, u32[]{:S(2)}) copy-start(f32[80,2048]{1,0:T(8,128)} %fusion.34) | copy-start | bytes 1966084
  107.2 4.5 %copy-start.4 = (bf16[80,1536]{1,0:T(8,128)(2,1)S(1)}, bf16[80,1536]{1,0:T(8,128)(2,1)}, u32[]{:S(2)}) copy-start(bf16[80,1536]{1,0:T(8,128)(2,1)} %reshape.420) | copy-start | bytes 737284
where the time goes:
time: 329 us; the launch traced here: 328 us
  other arithmetic  217 us (66%)
  local copies, waits for them, and re-layouts  47.1 us (14%)
  matrix products  35.6 us (11%)
  starting transfers between devices  17.3 us (5%)
  waiting for transfers between devices  10.2 us (3%)
    unnamed x11, other arithmetic  206 us
    dot_general x8, matrix products, contract(): lax.dot_general(left, right, dims, preferred_element_type=jnp.float32)  35.6 us
    gather x12, local copies, waits for them, and re-layouts, body(): picked_in = jnp.take(x_tokens[token_slot], columns, axis=1)  17.6 us
    gather x4, local copies, waits for them, and re-layouts, body(): jnp.take(grad_values[token_slot], columns, axis=1).astype(jnp.float32)  14.5 us
    all_to_all x1, starting transfers between devices, body(): lax.all_to_all(out_in, ('expert', 'tensor'), split_axis=0, concat_axis=0,...  7.39 us
  transfers between devices with their start and end apart: 3, of which 2 were waited for; matrix products, arithmetic and copies ran while one was open for 16% of the time, Pallas kernels for 0%

commit v1 on v0

v1 whole, which is shorter than its diff:
```python
import functools

import jax
import jax.numpy as jnp
from jax import lax
from jax.experimental import pallas as pl
from jax.experimental.pallas import tpu as pltpu
from jax.sharding import PartitionSpec as P

MOST = 5
LANES = 128
SUB = 8
F32 = jnp.float32
BF16 = jnp.bfloat16
VMEM = pl.BlockSpec(memory_space=pltpu.VMEM)
SMEM = pl.BlockSpec(memory_space=pltpu.SMEM)
ANY = pl.BlockSpec(memory_space=pl.ANY)


def vmem(shape, dtype):
    return pltpu.VMEM(shape, dtype)


def params(mib=48):
    return pltpu.CompilerParams(vmem_limit_bytes=mib << 20)


def cost(flops, bytes_accessed):
    return pl.CostEstimate(flops=int(flops), bytes_accessed=int(bytes_accessed), transcendentals=0)


def block_rows(chunks):
    return -(-((chunks - 1) * MOST + SUB) // 16) * 16


def iotas():
    lane = lax.broadcasted_iota(jnp.int32, (SUB, LANES), 1)
    sub = lax.broadcasted_iota(jnp.int32, (SUB, LANES), 0)
    return lane, sub


def lanes_of(values, index):
    return jnp.take_along_axis(values, index, axis=1, mode="promise_in_bounds")


def rows_of(values, index):
    return jnp.take_along_axis(values, index, axis=0, mode="promise_in_bounds")


def positions(code):
    first = (code >= 3).astype(jnp.int32) + (code >= 5).astype(jnp.int32)
    second = jnp.where(code < 3, code + 1, jnp.where(code < 5, code - 1, 3))
    return first, second


def expert_pattern(pattern_ref, expert, chunks):
    parts = []
    for part in range(-(-chunks // 2)):
        at = slice(part * LANES, (part + 1) * LANES)
        row = pattern_ref[0:1, at]
        for other in range(1, pattern_ref.shape[0]):
            row = jnp.where(expert == other, pattern_ref[other : other + 1, at], row)
        parts.append(jnp.broadcast_to(row, (SUB, LANES)))
    return parts


def hits(routes_ref, token, expert):
    first = routes_ref[token, 0] == expert
    second = routes_ref[token, 1] == expert
    return first, jnp.logical_or(first, second)


def dispatch_kernel(
    routes_ref, combine_ref, scale_ref, pattern_ref, x_ref, g_ref, *rest, n_e, holders, chunks
):
    outs, (slot_token, slot_weight, stage) = rest[:n_e], rest[n_e:]
    toks = x_ref.shape[0]
    block = block_rows(chunks)
    me = lax.axis_index("expert")
    lane, sub = iotas()
    stage[block - SUB : block, :] = jnp.zeros((SUB, LANES), F32)
    stage[2 * block - SUB : 2 * block, :] = jnp.zeros((SUB, LANES), F32)
    for k in range(n_e):
        expert = jnp.bitwise_xor(me, k) // holders
        count = jnp.int32(0)
        for token in range(toks):
            first, hit = hits(routes_ref, token, expert)
            weight = jnp.where(first, combine_ref[token, 0], combine_ref[token, 1])
            slot_token[count] = jnp.int32(token)
            slot_weight[count] = weight * scale_ref[token]
            count = count + hit.astype(jnp.int32)
        index = jnp.zeros((SUB, LANES), jnp.int32)
        weight = jnp.zeros((SUB, LANES), F32)
        for slot in range(MOST):
            filled = slot < count
            token = jnp.where(filled, slot_token[slot], 0)
            coef = jnp.where(filled, slot_weight[slot], 0.0)
            index = jnp.where(sub == slot, token, index)
            weight = jnp.where(sub == slot, coef, weight)
        valid = sub < count
        codes = expert_pattern(pattern_ref, expert, chunks)
        for c in range(chunks):
            code = lanes_of(
                codes[c // 2], lane // 2 + (c % 2) * (LANES // 2)
            )
            first, second = positions(code)
            source = 4 * (lane // 2) + jnp.where(lane % 2 == 0, first, second)
            local = jnp.bitwise_and(source, LANES - 1)
            low = lane < LANES // 2
            for ref, base in ((x_ref, 0), (g_ref, block)):
                left = ref[:, 2 * c * LANES : (2 * c + 1) * LANES].astype(F32)
                right = ref[:, (2 * c + 1) * LANES : (2 * c + 2) * LANES].astype(F32)
                picked = jnp.where(low, lanes_of(left, local), lanes_of(right, local))
                picked = rows_of(picked, index)
                if base:
                    picked = picked * weight
                picked = jnp.where(valid, picked, 0.0)
                stage[base + c * MOST : base + c * MOST + SUB, :] = picked
        outs[k][...] = stage[...].astype(BF16)


def dispatch(routes, combine, scale, pattern, x, g, n_e, holders, chunks):
    block = block_rows(chunks)
    toks = x.shape[0]
    return pl.pallas_call(
        functools.partial(dispatch_kernel, n_e=n_e, holders=holders, chunks=chunks),
        out_shape=[vmem((2 * block, LANES), BF16)] * n_e,
        in_specs=[SMEM, SMEM, SMEM, VMEM, VMEM, VMEM],
        out_specs=[VMEM] * n_e,
        scratch_shapes=[
            pltpu.SMEM((toks + 1,), jnp.int32),
            pltpu.SMEM((toks + 1,), F32),
            pltpu.VMEM((2 * block, LANES), F32),
        ],
        compiler_params=params(8),
        name="dispatch",
    )(routes, combine, scale, pattern, x, g)


def join_kernel(*refs, n_e, block):
    ins, (zx, zg) = refs[:n_e], refs[n_e:]
    for k in range(n_e):
        zx[k * block : (k + 1) * block, :] = ins[k][:block, :]
        zg[k * block : (k + 1) * block, :] = ins[k][block:, :]


def join(parts, block):
    n_e = len(parts)
    return pl.pallas_call(
        functools.partial(join_kernel, n_e=n_e, block=block),
        out_shape=[vmem((n_e * block, LANES), BF16)] * 2,
        in_specs=[VMEM] * n_e,
        out_specs=[VMEM] * 2,
        compiler_params=params(8),
        name="join",
    )(*parts)


def load_kernel(wg, wu, wd, after, og, ou, od, sems):
    pieces = 4
    copies = []
    for a, (source, target) in enumerate(((wg, og), (wu, ou), (wd, od))):
        rows = source.shape[0] // pieces
        for i in range(pieces):
            at = pl.ds(i * rows, rows)
            copies.append(pltpu.make_async_copy(source.at[at], target.at[at], sems.at[a, i]))
    for copy in copies:
        copy.start()
    for copy in copies:
        copy.wait()


def load_weights(wg, wu, wd, after):
    size = sum(w.size * 2 for w in (wg, wu, wd))
    return pl.pallas_call(
        load_kernel,
        out_shape=[vmem(w.shape, w.dtype) for w in (wg, wu, wd)],
        in_specs=[ANY] * 4,
        out_specs=[VMEM] * 3,
        scratch_shapes=[pltpu.SemaphoreType.DMA((3, 4))],
        compiler_params=params(32),
        cost_estimate=cost(0, size),
        name="load_weights",
    )(wg, wu, wd, after)


def unpack_rows(arrays, stage, rows_ref, n_e, block, chunks):
    sources = n_e * len(arrays)
    for i, ref in enumerate(arrays):
        stage[i * n_e * block : (i + 1) * n_e * block, :] = ref[...].astype(F32)
    for c in range(chunks):
        for slot in range(MOST):
            picked = stage[pl.ds(c * MOST + slot, sources, stride=block), :]
            rows_ref[slot * sources : (slot + 1) * sources, c * LANES : (c + 1) * LANES] = (
                picked.astype(BF16)
            )


def tile_of(size, most):
    return min(size, most)


def forward_kernel(*refs, n_t, n_e, block, chunks):
    arrays, (wg, wu, rows, hidden, slope, silu_out, stage) = refs[:n_t], refs[n_t:]
    unpack_rows(arrays, stage, rows, n_e, block, chunks)
    x = rows[...]
    hid = wg.shape[1]
    tile = tile_of(hid, 256)
    for i in range(hid // tile):
        at = slice(i * tile, (i + 1) * tile)
        gate = jnp.dot(x, wg[:, at], preferred_element_type=F32)
        up = jnp.dot(x, wu[:, at], preferred_element_type=F32)
        sig = jax.nn.sigmoid(gate)
        silu = gate * sig
        hidden[:, at] = (silu * up).astype(BF16)
        slope[:, at] = up * sig * (1.0 + gate * (1.0 - sig))
        silu_out[:, at] = silu


def forward(arrays, wg, wu, n_e, block, chunks):
    n_t = len(arrays)
    count = MOST * n_e * n_t
    kept, hid = wg.shape
    return pl.pallas_call(
        functools.partial(forward_kernel, n_t=n_t, n_e=n_e, block=block, chunks=chunks),
        out_shape=[
            vmem((count, kept), BF16),
            vmem((count, hid), BF16),
            vmem((count, hid), F32),
            vmem((count, hid), F32),
        ],
        in_specs=[VMEM] * (n_t + 2),
        out_specs=[VMEM] * 4,
        scratch_shapes=[pltpu.VMEM((n_t * n_e * block, LANES), F32)],
        compiler_params=params(),
        cost_estimate=cost(4 * 4 * count * kept * hid, 4 * kept * hid),
        name="forward",
    )(*arrays, wg, wu)


def backward_kernel(*refs, n_t, n_e, block, chunks):
    arrays, (slope, silu, wg, wu, wd), rest = refs[:n_t], refs[n_t : n_t + 5], refs[n_t + 5 :]
    (rows, d_gate, d_up), outs, (stage, total) = rest[:3], rest[3 : 3 + n_t], rest[3 + n_t :]
    unpack_rows(arrays, stage, rows, n_e, block, chunks)
    last = (((1,), (1,)), ((), ()))
    hid, kept = wd.shape
    tile = tile_of(hid, 256)
    g = rows[...]
    for i in range(hid // tile):
        at = slice(i * tile, (i + 1) * tile)
        grad = lax.dot_general(g, wd[at, :], last, preferred_element_type=F32)
        d_gate[:, at] = (grad * slope[:, at]).astype(BF16)
        d_up[:, at] = (grad * silu[:, at]).astype(BF16)
    sources = n_e * n_t
    for row in range(chunks * MOST, block):
        stage[pl.ds(row, sources, stride=block), :] = jnp.zeros((sources, LANES), F32)
    dg, du = d_gate[...], d_up[...]
    width = 2 * LANES if kept % (2 * LANES) == 0 else LANES
    for i in range(kept // width):
        at = slice(i * width, (i + 1) * width)
        back = lax.dot_general(dg, wg[at, :], last, preferred_element_type=F32)
        back = back + lax.dot_general(du, wu[at, :], last, preferred_element_type=F32)
        for half in range(width // LANES):
            c = i * (width // LANES) + half
            for slot in range(MOST):
                stage[pl.ds(c * MOST + slot, sources, stride=block), :] = back[
                    slot * sources : (slot + 1) * sources, half * LANES : (half + 1) * LANES
                ]
    for i in range(n_t):
        outs[i][...] = stage[i * n_e * block : (i + 1) * n_e * block, :].astype(BF16)


def backward(arrays, slope, silu, wg, wu, wd, n_e, block, chunks):
    n_t = len(arrays)
    count = MOST * n_e * n_t
    kept, hid = wg.shape
    return pl.pallas_call(
        functools.partial(backward_kernel, n_t=n_t, n_e=n_e, block=block, chunks=chunks),
        out_shape=[
            vmem((count, kept), BF16),
            vmem((count, hid), BF16),
            vmem((count, hid), BF16),
        ]
        + [vmem((n_e * block, LANES), BF16)] * n_t,
        in_specs=[VMEM] * (n_t + 5),
        out_specs=[VMEM] * (3 + n_t),
        scratch_shapes=[
            pltpu.VMEM((n_t * n_e * block, LANES), F32),
            pltpu.VMEM((SUB, LANES), F32),
        ],
        compiler_params=params(),
        cost_estimate=cost(6 * 4 * count * kept * hid, 6 * kept * hid),
        name="backward",
    )(*arrays, slope, silu, wg, wu, wd)


def outer_kernel(left, *refs):
    rights, outs = refs[: len(refs) // 2], refs[len(refs) // 2 :]
    first = (((0,), (0,)), ((), ()))
    for right, out in zip(rights, outs):
        out[...] = lax.dot_general(left[...], right[...], first, preferred_element_type=F32).astype(
            BF16
        )


def outer(left, rights, name):
    count, m = left.shape
    n = rights[0].shape[1]
    tile = tile_of(m, 256)
    return pl.pallas_call(
        outer_kernel,
        grid=(m // tile,),
        out_shape=[jax.ShapeDtypeStruct((m, n), BF16)] * len(rights),
        in_specs=[pl.BlockSpec((count, tile), lambda i: (0, i))]
        + [pl.BlockSpec((count, n), lambda i: (0, 0))] * len(rights),
        out_specs=[pl.BlockSpec((tile, n), lambda i: (i, 0))] * len(rights),
        compiler_params=params(24),
        cost_estimate=cost(2 * 256 * m * n * len(rights), 2 * m * n * len(rights)),
        name=name,
    )(left, *rights)


def sum_kernel(*refs, n_t, n_e, block):
    ins, outs = refs[:n_t], refs[n_t:]
    for k in range(n_e):
        at = slice(k * block, (k + 1) * block)
        total = ins[0][at, :].astype(F32)
        for ref in ins[1:]:
            total = total + ref[at, :].astype(F32)
        outs[k][...] = total.astype(BF16)


def sum_parts(arrays, n_e, block):
    n_t = len(arrays)
    return pl.pallas_call(
        functools.partial(sum_kernel, n_t=n_t, n_e=n_e, block=block),
        out_shape=[vmem((block, LANES), BF16)] * n_e,
        in_specs=[VMEM] * n_t,
        out_specs=[VMEM] * n_e,
        compiler_params=params(8),
        name="sum_parts",
    )(*arrays)


def combine_kernel(routes_ref, pattern_ref, *rest, n_e, holders, chunks):
    ins, (out, stage, total) = rest[:n_e], rest[n_e:]
    toks = out.shape[0]
    me = lax.axis_index("expert")
    lane, sub = iotas()
    for k in range(n_e):
        expert = jnp.bitwise_xor(me, k) // holders
        stage[...] = ins[k][...].astype(F32)
        count = jnp.int32(0)
        slot = jnp.full((SUB, LANES), MOST, jnp.int32)
        for token in range(toks):
            _, hit = hits(routes_ref, token, expert)
            slot = jnp.where(sub == token, jnp.where(hit, count, MOST), slot)
            count = count + hit.astype(jnp.int32)
        valid = slot < MOST
        index = jnp.where(valid, slot, 0)
        codes = expert_pattern(pattern_ref, expert, chunks)
        for c in range(chunks):
            rows = stage[c * MOST : c * MOST + SUB, :]
            rows = jnp.where(valid, rows_of(rows, index), 0.0)
            for half in range(2):
                m = 2 * c + half
                code = lanes_of(
                    codes[m // 4], lane // 4 + (m % 4) * (LANES // 4)
                )
                first, second = positions(code)
                place = lane % 4
                later = place == second
                keep = jnp.logical_or(place == first, later)
                local = half * (LANES // 2) + 2 * (lane // 4) + later.astype(jnp.int32)
                spread = jnp.where(keep, lanes_of(rows, local), 0.0)
                at = slice(m * LANES, (m + 1) * LANES)
                if k == 0:
                    total[:, at] = spread
                elif k < n_e - 1:
                    total[:, at] += spread
                else:
                    out[:, at] = (total[:, at] + spread).astype(BF16)


def combine_rows(routes, pattern, arrays, toks, width, holders, chunks):
    n_e = len(arrays)
    block = arrays[0].shape[0]
    return pl.pallas_call(
        functools.partial(combine_kernel, n_e=n_e, holders=holders, chunks=chunks),
        out_shape=jax.ShapeDtypeStruct((toks, width), BF16),
        in_specs=[SMEM, VMEM] + [VMEM] * n_e,
        out_specs=VMEM,
        scratch_shapes=[pltpu.VMEM((block, LANES), F32), pltpu.VMEM((toks, width), F32)],
        compiler_params=params(8),
        name="combine_rows",
    )(routes, pattern, *arrays)


def swap(value, axis, k):
    size = lax.axis_size(axis)
    return lax.ppermute(value, axis, [(i, i ^ k) for i in range(size)])


def body(x_tokens, grad_values, grad_scale, combine, routes, pattern, w_gate, w_up, w_down):
    n_e = lax.axis_size("expert")
    n_t = lax.axis_size("tensor")
    experts = pattern.shape[0]
    holders = n_e // experts
    toks, width = x_tokens.shape
    chunks = w_gate.shape[0] // LANES
    block = block_rows(chunks)

    sent = dispatch(
        routes, combine, grad_scale, pattern, x_tokens, grad_values, n_e, holders, chunks
    )
    parts = [sent[0]] + [swap(sent[k], "expert", k) for k in range(1, n_e)]
    zx, zg = join(parts, block)
    all_x = [zx] + [swap(zx, "tensor", k) for k in range(1, n_t)]
    all_g = [zg] + [swap(zg, "tensor", k) for k in range(1, n_t)]
    wg, wu, wd = load_weights(w_gate, w_up, w_down, zx)
    rows_in, hidden, slope, silu = forward(all_x, wg, wu, n_e, block, chunks)
    rows_grad, d_gate, d_up, *back = backward(all_g, slope, silu, wg, wu, wd, n_e, block, chunks)
    back = [back[0]] + [swap(back[k], "tensor", k) for k in range(1, n_t)]
    part_gate, part_up = outer(rows_in, [d_gate, d_up], "grads_in")
    summed = sum_parts(back, n_e, block)
    summed = [summed[0]] + [swap(summed[k], "expert", k) for k in range(1, n_e)]
    (part_down,) = outer(hidden, [rows_grad], "grads_out")
    grad_tokens = combine_rows(routes, pattern, summed, toks, width, holders, chunks)
    return grad_tokens, part_gate, part_up, part_down


def solution(mesh):
    in_specs = (
        P(("group", "expert", "tensor"), None),
        P(("group", "expert", "tensor"), None),
        P(("group", "expert", "tensor")),
        P(("group", "expert", "tensor"), None),
        P(("group", "expert", "tensor"), None),
        P(),
        P(None, ("expert", "tensor")),
        P(None, ("expert", "tensor")),
        P(("expert", "tensor"), None),
    )
    out_specs = (
        P(("group", "expert", "tensor"), None),
        P("group", ("expert", "tensor")),
        P("group", ("expert", "tensor")),
        P(("expert", "tensor"), "group"),
    )
    return jax.shard_map(body, mesh=mesh, in_specs=in_specs, out_specs=out_specs, check_vma=False)
```

time: 329 us -> 79.5 us (0.24)
  other arithmetic: 217 us -> 0 us
  Pallas kernels: 0 us -> 44.1 us
  matrix products: 35.6 us -> 0 us
  local copies, waits for them, and re-layouts: 47.1 us -> 12.6 us
  waiting for transfers between devices: 10.2 us -> 3.31 us
    unnamed x11 -> x0, other arithmetic: 206 us -> none
    pallas_call x0 -> x9, Pallas kernels: none -> 44.1 us  [the longest x1 12.5 us: backward(): pl.pallas_call(functools.partial(backward_kernel, n_t=n_t, n_e=n_e, block...]
    gather x28 -> x0, local copies, waits for them, and re-layouts: 38.7 us -> none  [the longest x12 17.6 us: body(): picked_in = jnp.take(x_tokens[token_slot], columns, axis=1)]
    dot_general x8 -> x0, matrix products: 35.6 us -> none  [contract(): lax.dot_general(left, right, dims, preferred_element_type=jnp.float32)]
    ppermute x0 -> x15, starting transfers between devices: none -> 18.4 us  [swap(): return lax.ppermute(value, axis, [(i, i ^ k) for i in range(size)])]
    all_to_all x3 -> x0, starting transfers between devices: 17.3 us -> none  [the longest x1 7.39 us: body(): lax.all_to_all(out_in, ('expert', 'tensor'), split_axis=0, concat_axis=0,...]
    unnamed x28 -> x18, local copies, waits for them, and re-layouts: 0.71 us -> 12.6 us
    all_to_all x3 -> x0, waiting for transfers between devices: 10.2 us -> none  [the longest x1 6.44 us: body(): lax.all_to_all(back_rows.reshape(recv_in.shape), ('expert', 'tensor'), sp...]
  transfers between devices with their start and end apart: 3 -> 15, of which waited for: 2 -> 2; matrix products, arithmetic and copies ran while one was open for 16% -> 0% of each run, Pallas kernels for 0% -> 32%
where the time goes in v1:
time: 79.5 us; the launch traced here: 79.2 us
  Pallas kernels  44.1 us (55%)
  starting transfers between devices  18.4 us (23%)
  local copies, waits for them, and re-layouts  12.6 us (16%)
  waiting for transfers between devices  3.31 us (4%)
    ppermute x15, starting transfers between devices, swap(): return lax.ppermute(value, axis, [(i, i ^ k) for i in range(size)])  18.4 us
    unnamed x18, local copies, waits for them, and re-layouts  12.6 us
    pallas_call x1, Pallas kernels, backward(): pl.pallas_call(functools.partial(backward_kernel, n_t=n_t, n_e=n_e, block...  12.5 us
    pallas_call x2, Pallas kernels, outer(): pl.pallas_call(outer_kernel, grid=(m // tile,), out_shape=[jax.ShapeDtype...  11.5 us
    pallas_call x1, Pallas kernels, forward(): pl.pallas_call(functools.partial(forward_kernel, n_t=n_t, n_e=n_e, block=...  7.14 us
    pallas_call x1, Pallas kernels, load_weights(): pl.pallas_call(load_kernel, out_shape=[vmem(w.shape, w.dtype) for w in (w...  6.52 us
    pallas_call x1, Pallas kernels, combine_rows(): pl.pallas_call(functools.partial(combine_kernel, n_e=n_e, holders=holders...  3.93 us
    ppermute x15, waiting for transfers between devices, swap(): return lax.ppermute(value, axis, [(i, i ^ k) for i in range(size)])  3.31 us
  transfers between devices with their start and end apart: 15, of which 2 were waited for; matrix products, arithmetic and copies ran while one was open for 0% of the time, Pallas kernels for 32%

profile of v1, /device:TPU:0, one launch (start us, length us, event | category | flops | bytes accessed | tf_op | source)
XLA Modules:
  0.0 79.2 jit_solution(14289240357485023434)
XLA Ops:
  0.6 0.8 copy.15.routes_ref
  1.4 0.8 copy.14.combine_ref
  2.1 0.0 copy-start
  2.1 0.7 copy-done
  2.8 0.0 copy-start.2
  2.8 0.8 %copy-done.2 = bf16[8,3072]{1,0:T(8,128)(2,1)S(1)} copy-done((bf16[8,3072]{1,0:T(8,128)(2,1)S(1)}, bf16[8,3072]{1,0:T(8,128)(2,1)}, u32[]{:S(2)}) %copy-start.2) | copy-done | bytes 49176
  3.6 0.0 copy-start.3
  3.6 0.8 %copy-done.3 = bf16[8,3072]{1,0:T(8,128)(2,1)S(1)} copy-done((bf16[8,3072]{1,0:T(8,128)(2,1)S(1)}, bf16[8,3072]{1,0:T(8,128)(2,1)}, u32[]{:S(2)}) %copy-start.3) | copy-done | bytes 49176
  4.4 0.0 copy-start.4
  4.4 0.7 copy-done.4
  5.1 2.5 %dispatch.1 = (bf16[128,128]{1,0:T(8,128)(2,1)S(1)}, bf16[128,128]{1,0:T(8,128)(2,1)S(1)}, bf16[128,128]{1,0:T(8,128)(2,1)S(1)}, bf16[128,128]{1,0:T(8,128)(2,1)S(1)}) custom-call(s32[8,2]{1,0:T(8,128)S(1)} %copy.15.routes_ref, f32[8,2]{1,0:T(8,128)S(1)} %copy.14.combine_ref, f32[8]{0:T(128)S(1)} %copy-done.4, s32[4,768]{1,0:T(4,128)S(1)} %copy-done, ...), custom_call_target="tpu_custom_call" | custom-call | tf_op jit(solution)/shard_map/dispatch/pallas_call | solution.py:125
  7.6 0.5 collective-permute-start
  8.1 2.6 %collective-permute-start.1 = (bf16[128,128]{1,0:T(8,128)(2,1)S(1)}, bf16[128,128]{1,0:T(8,128)(2,1)S(1)}, u32[]{:S(2)}, u32[]{:S(2)}) collective-permute-start(bf16[128,128]{1,0:T(8,128)(2,1)S(1)} %get-tuple-element.32), channel_id=1, source_target_pairs={{0,8},{4,12},{8,0},{12,4},{1,9},{5,13},{9,1},{13,5},{2,10},{6,14},... | collective-permute-start | bytes 98312 | tf_op jit(solution)/shard_map/ppermute | solution.py:401
  10.7 0.1 collective-permute-start.2
  10.8 0.0 collective-permute-done.refs_1_
  10.8 1.9 %collective-permute-done.1.refs_2_ = bf16[128,128]{1,0:T(8,128)(2,1)S(1)} collective-permute-done((bf16[128,128]{1,0:T(8,128)(2,1)S(1)}, bf16[128,128]{1,0:T(8,128)(2,1)S(1)}, u32[]{:S(2)}, u32[]{:S(2)}) %collective-permute-start.1) | collective-permute-done | bytes 32800 | tf_op jit(solution)/shard_map/ppermute | solution.py:401
  12.7 1.4 %collective-permute-done.2.refs_3_ = bf16[128,128]{1,0:T(8,128)(2,1)S(1)} collective-permute-done((bf16[128,128]{1,0:T(8,128)(2,1)S(1)}, bf16[128,128]{1,0:T(8,128)(2,1)S(1)}, u32[]{:S(2)}, u32[]{:S(2)}) %collective-permute-start.2) | collective-permute-done | bytes 32800 | tf_op jit(solution)/shard_map/ppermute | solution.py:401
  14.0 3.7 %collective-permute-start.8 = (bf16[256,128]{1,0:T(8,128)(2,1)S(1)}, bf16[256,128]{1,0:T(8,128)(2,1)S(1)}, u32[]{:S(2)}, u32[]{:S(2)}) collective-permute-start(bf16[256,128]{1,0:T(8,128)(2,1)S(1)} %get-tuple-element.35.after.refs_0_), channel_id=1, source_target_pairs={{0,3},{1,2},{2,1},{3,0},{4,7},{5,6},{6,5},{7,4},{8,11},{9,10},{10,... | collective-permute-start | bytes 196616 | tf_op jit(solution)/shard_map/ppermute | solution.py:401
  17.7 0.0 collective-permute-start.7
  17.7 0.8 collective-permute-start.6
  18.5 3.6 %collective-permute-start.5 = (bf16[256,128]{1,0:T(8,128)(2,1)S(1)}, bf16[256,128]{1,0:T(8,128)(2,1)S(1)}, u32[]{:S(2)}, u32[]{:S(2)}) collective-permute-start(bf16[256,128]{1,0:T(8,128)(2,1)S(1)} %get-tuple-element.34.refs_0_), channel_id=1, source_target_pairs={{0,3},{1,2},{2,1},{3,0},{4,7},{5,6},{6,5},{7,4},{8,11},{9,10},{10,... | collective-permute-start | bytes 196616 | tf_op jit(solution)/shard_map/ppermute | solution.py:401
  22.1 0.0 collective-permute-start.4
  22.1 6.5 %load_weights.1 = (bf16[1536,2048]{1,0:T(8,128)(2,1)S(1)}, bf16[1536,2048]{1,0:T(8,128)(2,1)S(1)}, bf16[2048,1536]{1,0:T(8,128)(2,1)S(1)}) custom-call(bf16[1536,2048]{1,0:T(8,128)(2,1)} %wg.1, bf16[1536,2048]{1,0:T(8,128)(2,1)} %wu.1, bf16[2048,1536]{1,0:T(8,128)(2,1)} %wd.1, bf16[256,128]{1,0:T(8,128)(2,1)S(1)} %get-tuple-element.35.after.refs_0_), custom_call_target="tpu_custom_call" | custom-call | bytes 18874368 | tf_op jit(solution)/shard_map/load_weights/pallas_call | solution.py:175
  28.6 0.0 copy-start.5
  28.6 2.7 %copy-done.5 = bf16[1536,2048]{1,0:T(8,128)(2,1)} copy-done((bf16[1536,2048]{1,0:T(8,128)(2,1)}, bf16[1536,2048]{1,0:T(8,128)(2,1)S(1)}, u32[]{:S(2)}) %copy-start.5) | copy-done | bytes 6291480
  31.3 0.0 copy-start.6
  31.3 2.7 %copy-done.6 = bf16[1536,2048]{1,0:T(8,128)(2,1)} copy-done((bf16[1536,2048]{1,0:T(8,128)(2,1)}, bf16[1536,2048]{1,0:T(8,128)(2,1)S(1)}, u32[]{:S(2)}) %copy-start.6) | copy-done | bytes 6291480
  34.0 0.0 copy-start.7
  34.0 2.7 %copy-done.7 = bf16[2048,1536]{1,0:T(8,128)(2,1)} copy-done((bf16[2048,1536]{1,0:T(8,128)(2,1)}, bf16[2048,1536]{1,0:T(8,128)(2,1)S(1)}, u32[]{:S(2)}) %copy-start.7) | copy-done | bytes 6291480
  36.7 0.0 collective-permute-done.8.refs_3_
  36.7 0.8 collective-permute-start.3
  37.5 0.0 collective-permute-done.7.refs_2_
  37.5 0.0 collective-permute-done.6.refs_1_
  37.5 7.1 %forward.1 = (bf16[80,1536]{1,0:T(8,128)(2,1)S(1)}, bf16[80,2048]{1,0:T(8,128)(2,1)S(1)}, f32[80,2048]{1,0:T(8,128)S(1)}, f32[80,2048]{1,0:T(8,128)S(1)}) custom-call(bf16[256,128]{1,0:T(8,128)(2,1)S(1)} %get-tuple-element.35.after.refs_0_, bf16[256,128]{1,0:T(8,128)(2,1)S(1)} %collective-permute-done.6.refs_1_, ...), custom_call_target="tpu_custom_call" | custom-call | flops 4026531840 | bytes 12582912 | tf_op jit(solution)/shard_map/forward/pallas_call | solution.py:224
  44.7 0.0 collective-permute-done.5.refs_3_
  44.7 0.0 collective-permute-done.4.refs_2_
  44.7 0.0 collective-permute-done.3.refs_1_
  44.7 12.5 %backward.1 = (bf16[80,1536]{1,0:T(8,128)(2,1)S(1)}, bf16[80,2048]{1,0:T(8,128)(2,1)S(1)}, bf16[80,2048]{1,0:T(8,128)(2,1)S(1)}, bf16[256,128]{1,0:T(8,128)(2,1)...) custom-call(bf16[256,128]{1,0:T(8,128)(2,1)S(1)} %get-tuple-element.34.refs_0_, ...), custom_call_target="tpu_custom_call" | custom-call | flops 6039797760 | bytes 18874368 | tf_op jit(solution)/shard_map/backward/pallas_call | solution.py:277
  57.2 1.3 %collective-permute-start.9 = (bf16[256,128]{1,0:T(8,128)(2,1)S(1)}, bf16[256,128]{1,0:T(8,128)(2,1)S(1)}, u32[]{:S(2)}, u32[]{:S(2)}) collective-permute-start(bf16[256,128]{1,0:T(8,128)(2,1)S(1)} %get-tuple-element.42), channel_id=1, source_target_pairs={{0,1},{1,0},{2,3},{3,2},{4,5},{5,4},{6,7},{7,6},{8,9},{9,8},{10,11... | collective-permute-start | bytes 196616 | tf_op jit(solution)/shard_map/ppermute | solution.py:401
  58.5 2.9 %collective-permute-start.10 = (bf16[256,128]{1,0:T(8,128)(2,1)S(1)}, bf16[256,128]{1,0:T(8,128)(2,1)S(1)}, u32[]{:S(2)}, u32[]{:S(2)}) collective-permute-start(bf16[256,128]{1,0:T(8,128)(2,1)S(1)} %get-tuple-element.43), channel_id=1, source_target_pairs={{0,2},{1,3},{2,0},{3,1},{4,6},{5,7},{6,4},{7,5},{8,10},{9,11},{10,... | collective-permute-start | bytes 196616 | tf_op jit(solution)/shard_map/ppermute | solution.py:401
  61.5 0.2 collective-permute-start.11
  61.7 6.0 %grads_in.1 = (bf16[1536,2048]{1,0:T(8,128)(2,1)}, bf16[1536,2048]{1,0:T(8,128)(2,1)}) custom-call(bf16[80,1536]{1,0:T(8,128)(2,1)S(1)} %get-tuple-element.49.left, bf16[80,2048]{1,0:T(8,128)(2,1)S(1)} %get-tuple-element.50.refs_0_, bf16[80,2048]{1,0:T(8,128)(2,1)S(1)} %get-tuple-element.51.refs_1_), custom_call_target="tpu_custom_call" | custom-call | flops 3221225472 | bytes 12582912 | tf_op jit(solution)/shard_map/grads_in/pallas_call | solution.py:310
  67.7 0.0 copy-start.1
  67.7 0.0 collective-permute-done.9.refs_1_
  67.7 0.0 collective-permute-done.10.refs_2_
  67.7 0.0 collective-permute-done.11.refs_3_
  67.8 0.1 collective-permute-start.12
  67.8 0.8 %collective-permute-start.13 = (bf16[64,128]{1,0:T(8,128)(2,1)S(1)}, bf16[64,128]{1,0:T(8,128)(2,1)S(1)}, u32[]{:S(2)}, u32[]{:S(2)}) collective-permute-start(bf16[64,128]{1,0:T(8,128)(2,1)S(1)} %get-tuple-element.47), channel_id=1, source_target_pairs={{0,8},{4,12},{8,0},{12,4},{1,9},{5,13},{9,1},{13,5},{2,10},{6,14},... | collective-permute-start | bytes 49160 | tf_op jit(solution)/shard_map/ppermute | solution.py:401
  68.7 1.0 %collective-permute-start.14 = (bf16[64,128]{1,0:T(8,128)(2,1)S(1)}, bf16[64,128]{1,0:T(8,128)(2,1)S(1)}, u32[]{:S(2)}, u32[]{:S(2)}) collective-permute-start(bf16[64,128]{1,0:T(8,128)(2,1)S(1)} %get-tuple-element.48), channel_id=1, source_target_pairs={{0,12},{4,8},{8,4},{12,0},{1,13},{5,9},{9,5},{13,1},{2,14},{6,10},... | collective-permute-start | bytes 49160 | tf_op jit(solution)/shard_map/ppermute | solution.py:401
  69.7 5.5 %grads_out.1 = bf16[2048,1536]{1,0:T(8,128)(2,1)} custom-call(bf16[80,2048]{1,0:T(8,128)(2,1)S(1)} %get-tuple-element.54.left, bf16[80,1536]{1,0:T(8,128)(2,1)S(1)} %get-tuple-element.55.refs_0_), custom_call_target="tpu_custom_call" | custom-call | flops 1610612736 | bytes 6291456 | tf_op jit(solution)/shard_map/grads_out/pallas_call | solution.py:310
  75.2 0.0 collective-permute-done.12.rest_1_
  75.2 0.0 collective-permute-done.13.rest_2_
  75.2 0.0 collective-permute-done.14.rest_3_
  75.2 0.0 copy-done.1
  75.2 3.9 %combine_rows.1 = bf16[8,3072]{1,0:T(8,128)(2,1)} custom-call(s32[8,2]{1,0:T(8,128)S(1)} %copy.15.routes_ref, s32[4,768]{1,0:T(4,128)S(1)} %copy-done.1, bf16[64,128]{1,0:T(8,128)(2,1)S(1)} %get-tuple-element.45.rest_0_, bf16[64,128]{1,0:T(8,128)(2,1)S(1)} %collective-permute-done.12.rest_1_, bf16[64,128]{1,0:T(8,128)(2,1)S(1)} %collective-permute-done.13.rest_2_, ...), custom_call_target="tpu_custom_call" | custom-call | tf_op jit(solution)/shard_map/combine_rows/pallas_call | solution.py:388
  (2 shorter events, 0.0 us)
Async XLA Ops:
  2.1 0.7 copy-start
  2.8 0.8 %copy-start.2 = (bf16[8,3072]{1,0:T(8,128)(2,1)S(1)}, bf16[8,3072]{1,0:T(8,128)(2,1)}, u32[]{:S(2)}) copy-start(bf16[8,3072]{1,0:T(8,128)(2,1)} %x_ref.1) | copy-start | bytes 147460
  3.6 0.8 %copy-start.3 = (bf16[8,3072]{1,0:T(8,128)(2,1)S(1)}, bf16[8,3072]{1,0:T(8,128)(2,1)}, u32[]{:S(2)}) copy-start(bf16[8,3072]{1,0:T(8,128)(2,1)} %g_ref.1) | copy-start | bytes 147460
  4.4 0.7 copy-start.4
  7.6 3.2 %collective-permute-start = (bf16[128,128]{1,0:T(8,128)(2,1)S(1)}, bf16[128,128]{1,0:T(8,128)(2,1)S(1)}, u32[]{:S(2)}, u32[]{:S(2)}) collective-permute-start(bf16[128,128]{1,0:T(8,128)(2,1)S(1)} %get-tuple-element.31), channel_id=1, source_target_pairs={{0,4},{4,0},{8,12},{12,8},{1,5},{5,1},{9,13},{13,9},{2,6},{6,2},{1... | collective-permute-start | bytes 98312 | tf_op jit(solution)/shard_map/ppermute | solution.py:401
  8.1 4.6 %collective-permute-start.1 = (bf16[128,128]{1,0:T(8,128)(2,1)S(1)}, bf16[128,128]{1,0:T(8,128)(2,1)S(1)}, u32[]{:S(2)}, u32[]{:S(2)}) collective-permute-start(bf16[128,128]{1,0:T(8,128)(2,1)S(1)} %get-tuple-element.32), channel_id=1, source_target_pairs={{0,8},{4,12},{8,0},{12,4},{1,9},{5,13},{9,1},{13,5},{2,10},{6,14},... | collective-permute-start | bytes 98312 | tf_op jit(solution)/shard_map/ppermute | solution.py:401
  10.7 3.3 %collective-permute-start.2 = (bf16[128,128]{1,0:T(8,128)(2,1)S(1)}, bf16[128,128]{1,0:T(8,128)(2,1)S(1)}, u32[]{:S(2)}, u32[]{:S(2)}) collective-permute-start(bf16[128,128]{1,0:T(8,128)(2,1)S(1)} %get-tuple-element.33), channel_id=1, source_target_pairs={{0,12},{4,8},{8,4},{12,0},{1,13},{5,9},{9,5},{13,1},{2,14},{6,10},... | collective-permute-start | bytes 98312 | tf_op jit(solution)/shard_map/ppermute | solution.py:401
  14.0 22.7 %collective-permute-start.8 = (bf16[256,128]{1,0:T(8,128)(2,1)S(1)}, bf16[256,128]{1,0:T(8,128)(2,1)S(1)}, u32[]{:S(2)}, u32[]{:S(2)}) collective-permute-start(bf16[256,128]{1,0:T(8,128)(2,1)S(1)} %get-tuple-element.35.after.refs_0_), channel_id=1, source_target_pairs={{0,3},{1,2},{2,1},{3,0},{4,7},{5,6},{6,5},{7,4},{8,11},{9,10},{10,... | collective-permute-start | bytes 196616 | tf_op jit(solution)/shard_map/ppermute | solution.py:401
  17.7 19.8 %collective-permute-start.7 = (bf16[256,128]{1,0:T(8,128)(2,1)S(1)}, bf16[256,128]{1,0:T(8,128)(2,1)S(1)}, u32[]{:S(2)}, u32[]{:S(2)}) collective-permute-start(bf16[256,128]{1,0:T(8,128)(2,1)S(1)} %get-tuple-element.35.after.refs_0_), channel_id=1, source_target_pairs={{0,2},{1,3},{2,0},{3,1},{4,6},{5,7},{6,4},{7,5},{8,10},{9,11},{10,... | collective-permute-start | bytes 196616 | tf_op jit(solution)/shard_map/ppermute | solution.py:401
  17.7 19.8 %collective-permute-start.6 = (bf16[256,128]{1,0:T(8,128)(2,1)S(1)}, bf16[256,128]{1,0:T(8,128)(2,1)S(1)}, u32[]{:S(2)}, u32[]{:S(2)}) collective-permute-start(bf16[256,128]{1,0:T(8,128)(2,1)S(1)} %get-tuple-element.35.after.refs_0_), channel_id=1, source_target_pairs={{0,1},{1,0},{2,3},{3,2},{4,5},{5,4},{6,7},{7,6},{8,9},{9,8},{10,11... | collective-permute-start | bytes 196616 | tf_op jit(solution)/shard_map/ppermute | solution.py:401
  18.5 26.2 %collective-permute-start.5 = (bf16[256,128]{1,0:T(8,128)(2,1)S(1)}, bf16[256,128]{1,0:T(8,128)(2,1)S(1)}, u32[]{:S(2)}, u32[]{:S(2)}) collective-permute-start(bf16[256,128]{1,0:T(8,128)(2,1)S(1)} %get-tuple-element.34.refs_0_), channel_id=1, source_target_pairs={{0,3},{1,2},{2,1},{3,0},{4,7},{5,6},{6,5},{7,4},{8,11},{9,10},{10,... | collective-permute-start | bytes 196616 | tf_op jit(solution)/shard_map/ppermute | solution.py:401
  22.1 22.6 %collective-permute-start.4 = (bf16[256,128]{1,0:T(8,128)(2,1)S(1)}, bf16[256,128]{1,0:T(8,128)(2,1)S(1)}, u32[]{:S(2)}, u32[]{:S(2)}) collective-permute-start(bf16[256,128]{1,0:T(8,128)(2,1)S(1)} %get-tuple-element.34.refs_0_), channel_id=1, source_target_pairs={{0,2},{1,3},{2,0},{3,1},{4,6},{5,7},{6,4},{7,5},{8,10},{9,11},{10,... | collective-permute-start | bytes 196616 | tf_op jit(solution)/shard_map/ppermute | solution.py:401
  28.6 2.7 %copy-start.5 = (bf16[1536,2048]{1,0:T(8,128)(2,1)}, bf16[1536,2048]{1,0:T(8,128)(2,1)S(1)}, u32[]{:S(2)}) copy-start(bf16[1536,2048]{1,0:T(8,128)(2,1)S(1)} %get-tuple-element.36.refs_4_.refs_6_) | copy-start | bytes 18874372
  31.3 2.7 %copy-start.6 = (bf16[1536,2048]{1,0:T(8,128)(2,1)}, bf16[1536,2048]{1,0:T(8,128)(2,1)S(1)}, u32[]{:S(2)}) copy-start(bf16[1536,2048]{1,0:T(8,128)(2,1)S(1)} %get-tuple-element.37.refs_5_.refs_7_) | copy-start | bytes 18874372
  34.0 2.7 %copy-start.7 = (bf16[2048,1536]{1,0:T(8,128)(2,1)}, bf16[2048,1536]{1,0:T(8,128)(2,1)S(1)}, u32[]{:S(2)}) copy-start(bf16[2048,1536]{1,0:T(8,128)(2,1)S(1)} %get-tuple-element.40.refs_8_) | copy-start | bytes 18874372
  36.7 8.0 %collective-permute-start.3 = (bf16[256,128]{1,0:T(8,128)(2,1)S(1)}, bf16[256,128]{1,0:T(8,128)(2,1)S(1)}, u32[]{:S(2)}, u32[]{:S(2)}) collective-permute-start(bf16[256,128]{1,0:T(8,128)(2,1)S(1)} %get-tuple-element.34.refs_0_), channel_id=1, source_target_pairs={{0,1},{1,0},{2,3},{3,2},{4,5},{5,4},{6,7},{7,6},{8,9},{9,8},{10,11... | collective-permute-start | bytes 196616 | tf_op jit(solution)/shard_map/ppermute | solution.py:401
  57.2 10.5 %collective-permute-start.9 = (bf16[256,128]{1,0:T(8,128)(2,1)S(1)}, bf16[256,128]{1,0:T(8,128)(2,1)S(1)}, u32[]{:S(2)}, u32[]{:S(2)}) collective-permute-start(bf16[256,128]{1,0:T(8,128)(2,1)S(1)} %get-tuple-element.42), channel_id=1, source_target_pairs={{0,1},{1,0},{2,3},{3,2},{4,5},{5,4},{6,7},{7,6},{8,9},{9,8},{10,11... | collective-permute-start | bytes 196616 | tf_op jit(solution)/shard_map/ppermute | solution.py:401
  58.5 9.2 %collective-permute-start.10 = (bf16[256,128]{1,0:T(8,128)(2,1)S(1)}, bf16[256,128]{1,0:T(8,128)(2,1)S(1)}, u32[]{:S(2)}, u32[]{:S(2)}) collective-permute-start(bf16[256,128]{1,0:T(8,128)(2,1)S(1)} %get-tuple-element.43), channel_id=1, source_target_pairs={{0,2},{1,3},{2,0},{3,1},{4,6},{5,7},{6,4},{7,5},{8,10},{9,11},{10,... | collective-permute-start | bytes 196616 | tf_op jit(solution)/shard_map/ppermute | solution.py:401
  61.5 6.3 %collective-permute-start.11 = (bf16[256,128]{1,0:T(8,128)(2,1)S(1)}, bf16[256,128]{1,0:T(8,128)(2,1)S(1)}, u32[]{:S(2)}, u32[]{:S(2)}) collective-permute-start(bf16[256,128]{1,0:T(8,128)(2,1)S(1)} %get-tuple-element.44), channel_id=1, source_target_pairs={{0,3},{1,2},{2,1},{3,0},{4,7},{5,6},{6,5},{7,4},{8,11},{9,10},{10,... | collective-permute-start | bytes 196616 | tf_op jit(solution)/shard_map/ppermute | solution.py:401
  67.7 7.5 %copy-start.1 = (s32[4,768]{1,0:T(4,128)S(1)}, s32[4,768]{1,0:T(4,128)}, u32[]{:S(2)}) copy-start(s32[4,768]{1,0:T(4,128)} %pattern_ref.3) | copy-start | bytes 36868
  67.8 7.4 %collective-permute-start.12 = (bf16[64,128]{1,0:T(8,128)(2,1)S(1)}, bf16[64,128]{1,0:T(8,128)(2,1)S(1)}, u32[]{:S(2)}, u32[]{:S(2)}) collective-permute-start(bf16[64,128]{1,0:T(8,128)(2,1)S(1)} %get-tuple-element.46), channel_id=1, source_target_pairs={{0,4},{4,0},{8,12},{12,8},{1,5},{5,1},{9,13},{13,9},{2,6},{6,2},{1... | collective-permute-start | bytes 49160 | tf_op jit(solution)/shard_map/ppermute | solution.py:401
  67.8 7.4 %collective-permute-start.13 = (bf16[64,128]{1,0:T(8,128)(2,1)S(1)}, bf16[64,128]{1,0:T(8,128)(2,1)S(1)}, u32[]{:S(2)}, u32[]{:S(2)}) collective-permute-start(bf16[64,128]{1,0:T(8,128)(2,1)S(1)} %get-tuple-element.47), channel_id=1, source_target_pairs={{0,8},{4,12},{8,0},{12,4},{1,9},{5,13},{9,1},{13,5},{2,10},{6,14},... | collective-permute-start | bytes 49160 | tf_op jit(solution)/shard_map/ppermute | solution.py:401
  68.7 6.5 %collective-permute-start.14 = (bf16[64,128]{1,0:T(8,128)(2,1)S(1)}, bf16[64,128]{1,0:T(8,128)(2,1)S(1)}, u32[]{:S(2)}, u32[]{:S(2)}) collective-permute-start(bf16[64,128]{1,0:T(8,128)(2,1)S(1)} %get-tuple-element.48), channel_id=1, source_target_pairs={{0,12},{4,8},{8,4},{12,0},{1,13},{5,9},{9,5},{13,1},{2,14},{6,10},... | collective-permute-start | bytes 49160 | tf_op jit(solution)/shard_map/ppermute | solution.py:401

commit v2 on v1

v2 whole, which is shorter than its diff:
```python
import functools

import jax
import jax.numpy as jnp
from jax import lax
from jax.experimental import pallas as pl
from jax.experimental.pallas import tpu as pltpu
from jax.sharding import PartitionSpec as P

MOST = 5
LANES = 128
SUB = 8
PIECES = 4
DISPATCH_MIB = 56
F32 = jnp.float32
BF16 = jnp.bfloat16
VMEM = pl.BlockSpec(memory_space=pltpu.VMEM)
SMEM = pl.BlockSpec(memory_space=pltpu.SMEM)
ANY = pl.BlockSpec(memory_space=pl.ANY)


def vmem(shape, dtype):
    return pltpu.VMEM(shape, dtype)


def params(mib=48):
    return pltpu.CompilerParams(vmem_limit_bytes=mib << 20)


def cost(flops, bytes_accessed):
    return pl.CostEstimate(flops=int(flops), bytes_accessed=int(bytes_accessed), transcendentals=0)


def block_rows(chunks):
    return -(-((chunks - 1) * MOST + SUB) // 16) * 16


def iotas():
    lane = lax.broadcasted_iota(jnp.int32, (SUB, LANES), 1)
    sub = lax.broadcasted_iota(jnp.int32, (SUB, LANES), 0)
    return lane, sub


def lanes_of(values, index):
    return jnp.take_along_axis(values, index, axis=1, mode="promise_in_bounds")


def positions(code):
    first = (code >= 3).astype(jnp.int32) + (code >= 5).astype(jnp.int32)
    second = jnp.where(code < 3, code + 1, jnp.where(code < 5, code - 1, 3))
    return first, second


def pattern_rows(pattern_ref, table, parts):
    experts = pattern_ref.shape[0]
    table[...] = jnp.zeros(table.shape, table.dtype)
    for part in range(parts):
        table[part * SUB : part * SUB + experts, :] = pattern_ref[
            :, part * LANES : (part + 1) * LANES
        ]


def row_copies(source, target, sems):
    rows = source.shape[0] // PIECES
    return [
        pltpu.make_async_copy(
            source.at[pl.ds(i * rows, rows)], target.at[pl.ds(i * rows, rows)], sems.at[i]
        )
        for i in range(PIECES)
    ]


def load_kernel(w_ref, after, w_out, sems):
    loads = row_copies(w_ref, w_out, sems)
    for load in loads:
        load.start()
    for load in loads:
        load.wait()


def load_weights(weights, after):
    return pl.pallas_call(
        load_kernel,
        out_shape=vmem(weights.shape, weights.dtype),
        in_specs=[ANY] * 2,
        out_specs=VMEM,
        scratch_shapes=[pltpu.SemaphoreType.DMA((PIECES,))],
        compiler_params=params(4),
        cost_estimate=cost(0, 2 * weights.size),
        name="load_weights",
    )(weights, after)


def dispatch_kernel(
    routes_any, combine_any, scale_any, pattern_any, x_any, g_any, w_any, *rest, n_e, holders, chunks
):
    outs, rest = rest[:n_e], rest[n_e:]
    w_out, routes, weights, scale, count, pattern, x_in, g_in, codes = rest[:9]
    x_rows, g_rows, index, stage, in_sems, sems = rest[9:]
    moves = [
        pltpu.make_async_copy(source, target, in_sems.at[i])
        for i, (source, target) in enumerate(
            (
                (pattern_any, pattern),
                (routes_any, routes),
                (combine_any, weights),
                (scale_any, scale),
                (x_any, x_in),
                (g_any, g_in),
            )
        )
    ]
    for move in moves:
        move.start()
    loads = row_copies(w_any, w_out, sems)
    for load in loads:
        load.start()
    experts, toks = pattern.shape[0], x_in.shape[0]
    parts = chunks // 2
    block, region = block_rows(chunks), region_rows()
    me = lax.axis_index("expert")
    lane, _ = iotas()
    stage[...] = jnp.zeros(stage.shape, F32)
    moves[0].wait()
    pattern_rows(pattern, codes, parts)
    for expert in range(experts):
        count[expert] = jnp.int32(0)
        own = codes[pl.ds(expert, SUB, stride=SUB), :]
        for odd in range(2):
            first, second = positions(lanes_of(own, lane // 2 + odd * (LANES // 2)))
            source = 4 * (lane // 2) + jnp.where(lane % 2 == 0, first, second)
            index[expert * 2 + odd] = jnp.bitwise_and(source, LANES - 1)
    for move in moves[1:]:
        move.wait()
    for ref, rows in ((x_in, x_rows), (g_in, g_rows)):
        for m in range(2 * chunks):
            rows[m * SUB : (m + 1) * SUB, :] = ref[:, m * LANES : (m + 1) * LANES].astype(F32)
        rows[2 * chunks * SUB :, :] = jnp.zeros((rows.shape[0] - 2 * chunks * SUB, LANES), F32)
    low = lane < LANES // 2
    for token in range(toks):
        for choice in range(2):
            expert = routes[choice, token]
            slot = count[expert]
            count[expert] = slot + 1
            weight = weights[choice, token] * scale[token]
            for odd in range(2):
                local = index[expert * 2 + odd]
                for array, rows in ((0, x_rows), (1, g_rows)):
                    left = rows[pl.ds(2 * odd * SUB + token, SUB, stride=4 * SUB), :]
                    right = rows[pl.ds((2 * odd + 1) * SUB + token, SUB, stride=4 * SUB), :]
                    picked = jnp.where(low, lanes_of(left, local), lanes_of(right, local))
                    if array:
                        picked = picked * weight
                    at = (expert * 2 + array) * region + slot + odd * MOST
                    stage[pl.ds(at, SUB, stride=2 * MOST), :] = picked
    for k in range(n_e):
        expert = jnp.bitwise_xor(me, k) // holders
        for array in range(2):
            at = pl.multiple_of((expert * 2 + array) * region, 16)
            outs[k][array * block : (array + 1) * block, :] = stage[pl.ds(at, block), :].astype(
                BF16
            )
    for load in loads:
        load.wait()


def region_rows():
    return -(-((SUB - 1) * 2 * MOST + 2 * MOST) // 16) * 16


def dispatch(routes, combine, scale, pattern, x, g, weights, n_e, holders, chunks):
    block, region = block_rows(chunks), region_rows()
    experts, toks = pattern.shape[0], x.shape[0]
    return pl.pallas_call(
        functools.partial(dispatch_kernel, n_e=n_e, holders=holders, chunks=chunks),
        out_shape=[vmem((2 * block, LANES), BF16)] * n_e + [vmem(weights.shape, weights.dtype)],
        in_specs=[ANY] * 7,
        out_specs=[VMEM] * (n_e + 1),
        scratch_shapes=[
            pltpu.SMEM(routes.shape, jnp.int32),
            pltpu.SMEM(combine.shape, F32),
            pltpu.SMEM(scale.shape, F32),
            pltpu.SMEM((experts,), jnp.int32),
            pltpu.VMEM(pattern.shape, jnp.int32),
            pltpu.VMEM(x.shape, BF16),
            pltpu.VMEM(g.shape, BF16),
            pltpu.VMEM((SUB * SUB, LANES), jnp.int32),
            pltpu.VMEM((4 * SUB * SUB, LANES), F32),
            pltpu.VMEM((4 * SUB * SUB, LANES), F32),
            pltpu.VMEM((experts * 2, SUB, LANES), jnp.int32),
            pltpu.VMEM((experts * 2 * region, LANES), F32),
            pltpu.SemaphoreType.DMA((6,)),
            pltpu.SemaphoreType.DMA((PIECES,)),
        ],
        compiler_params=params(DISPATCH_MIB),
        name="dispatch",
    )(routes, combine, scale, pattern, x, g, weights)


def join_kernel(*refs, n_e, block):
    ins, (zx, zg) = refs[:n_e], refs[n_e:]
    for k in range(n_e):
        zx[k * block : (k + 1) * block, :] = ins[k][:block, :]
        zg[k * block : (k + 1) * block, :] = ins[k][block:, :]


def join(parts, block):
    n_e = len(parts)
    return pl.pallas_call(
        functools.partial(join_kernel, n_e=n_e, block=block),
        out_shape=[vmem((n_e * block, LANES), BF16)] * 2,
        in_specs=[VMEM] * n_e,
        out_specs=[VMEM] * 2,
        compiler_params=params(8),
        name="join",
    )(*parts)


def unpack_rows(arrays, stage, rows_ref, n_e, block, chunks):
    sources = n_e * len(arrays)
    for i, ref in enumerate(arrays):
        stage[i * n_e * block : (i + 1) * n_e * block, :] = ref[...].astype(F32)
    for c in range(chunks):
        for slot in range(MOST):
            picked = stage[pl.ds(c * MOST + slot, sources, stride=block), :]
            rows_ref[slot * sources : (slot + 1) * sources, c * LANES : (c + 1) * LANES] = (
                picked.astype(BF16)
            )


def tile_of(size, most):
    return min(size, most)


def forward_kernel(*refs, n_t, n_e, block, chunks):
    arrays, (wg, wu, wd, rows, hidden, slope, silu_out, wd_out, stage, sems) = refs[:n_t], refs[n_t:]
    loads = row_copies(wd, wd_out, sems)
    for load in loads:
        load.start()
    unpack_rows(arrays, stage, rows, n_e, block, chunks)
    x = rows[...]
    hid = wg.shape[1]
    tile = tile_of(hid, 256)
    for i in range(hid // tile):
        at = slice(i * tile, (i + 1) * tile)
        gate = jnp.dot(x, wg[:, at], preferred_element_type=F32)
        up = jnp.dot(x, wu[:, at], preferred_element_type=F32)
        sig = jax.nn.sigmoid(gate)
        silu = gate * sig
        hidden[:, at] = (silu * up).astype(BF16)
        slope[:, at] = up * sig * (1.0 + gate * (1.0 - sig))
        silu_out[:, at] = silu
    for load in loads:
        load.wait()


def forward(arrays, wg, wu, wd, n_e, block, chunks):
    n_t = len(arrays)
    count = MOST * n_e * n_t
    kept, hid = wg.shape
    return pl.pallas_call(
        functools.partial(forward_kernel, n_t=n_t, n_e=n_e, block=block, chunks=chunks),
        out_shape=[
            vmem((count, kept), BF16),
            vmem((count, hid), BF16),
            vmem((count, hid), F32),
            vmem((count, hid), F32),
            vmem(wd.shape, wd.dtype),
        ],
        in_specs=[VMEM] * (n_t + 2) + [ANY],
        out_specs=[VMEM] * 5,
        scratch_shapes=[
            pltpu.VMEM((n_t * n_e * block, LANES), F32),
            pltpu.SemaphoreType.DMA((PIECES,)),
        ],
        compiler_params=params(12),
        cost_estimate=cost(4 * 4 * count * kept * hid, 4 * kept * hid),
        name="forward",
    )(*arrays, wg, wu, wd)


def backward_kernel(*refs, n_t, n_e, block, chunks):
    arrays, (slope, silu, wg, wu, wd), rest = refs[:n_t], refs[n_t : n_t + 5], refs[n_t + 5 :]
    (rows, d_gate, d_up), outs, (stage, total) = rest[:3], rest[3 : 3 + n_t], rest[3 + n_t :]
    unpack_rows(arrays, stage, rows, n_e, block, chunks)
    last = (((1,), (1,)), ((), ()))
    hid, kept = wd.shape
    tile = tile_of(hid, 256)
    g = rows[...]
    for i in range(hid // tile):
        at = slice(i * tile, (i + 1) * tile)
        grad = lax.dot_general(g, wd[at, :], last, preferred_element_type=F32)
        d_gate[:, at] = (grad * slope[:, at]).astype(BF16)
        d_up[:, at] = (grad * silu[:, at]).astype(BF16)
    sources = n_e * n_t
    for row in range(chunks * MOST, block):
        stage[pl.ds(row, sources, stride=block), :] = jnp.zeros((sources, LANES), F32)
    dg, du = d_gate[...], d_up[...]
    width = 2 * LANES if kept % (2 * LANES) == 0 else LANES
    for i in range(kept // width):
        at = slice(i * width, (i + 1) * width)
        back = lax.dot_general(dg, wg[at, :], last, preferred_element_type=F32)
        back = back + lax.dot_general(du, wu[at, :], last, preferred_element_type=F32)
        for half in range(width // LANES):
            c = i * (width // LANES) + half
            for slot in range(MOST):
                stage[pl.ds(c * MOST + slot, sources, stride=block), :] = back[
                    slot * sources : (slot + 1) * sources, half * LANES : (half + 1) * LANES
                ]
    for i in range(n_t):
        outs[i][...] = stage[i * n_e * block : (i + 1) * n_e * block, :].astype(BF16)


def backward(arrays, slope, silu, wg, wu, wd, n_e, block, chunks):
    n_t = len(arrays)
    count = MOST * n_e * n_t
    kept, hid = wg.shape
    return pl.pallas_call(
        functools.partial(backward_kernel, n_t=n_t, n_e=n_e, block=block, chunks=chunks),
        out_shape=[
            vmem((count, kept), BF16),
            vmem((count, hid), BF16),
            vmem((count, hid), BF16),
        ]
        + [vmem((n_e * block, LANES), BF16)] * n_t,
        in_specs=[VMEM] * (n_t + 5),
        out_specs=[VMEM] * (3 + n_t),
        scratch_shapes=[
            pltpu.VMEM((n_t * n_e * block, LANES), F32),
            pltpu.VMEM((SUB, LANES), F32),
        ],
        compiler_params=params(12),
        cost_estimate=cost(6 * 4 * count * kept * hid, 6 * kept * hid),
        name="backward",
    )(*arrays, slope, silu, wg, wu, wd)


def outer_kernel(left, *refs):
    rights, outs = refs[: len(refs) // 2], refs[len(refs) // 2 :]
    first = (((0,), (0,)), ((), ()))
    for right, out in zip(rights, outs):
        out[...] = lax.dot_general(left[...], right[...], first, preferred_element_type=F32).astype(
            BF16
        )


def outer(left, rights, tile, name):
    count, m = left.shape
    n = rights[0].shape[1]
    tile = tile_of(m, tile)
    return pl.pallas_call(
        outer_kernel,
        grid=(m // tile,),
        out_shape=[jax.ShapeDtypeStruct((m, n), BF16)] * len(rights),
        in_specs=[pl.BlockSpec((count, tile), lambda i: (0, i))]
        + [pl.BlockSpec((count, n), lambda i: (0, 0))] * len(rights),
        out_specs=[pl.BlockSpec((tile, n), lambda i: (i, 0))] * len(rights),
        compiler_params=params(20),
        cost_estimate=cost(2 * 256 * m * n * len(rights), 2 * m * n * len(rights)),
        name=name,
    )(left, *rights)


def sum_kernel(*refs, n_t, n_e, block):
    ins, outs = refs[:n_t], refs[n_t:]
    for k in range(n_e):
        at = slice(k * block, (k + 1) * block)
        total = ins[0][at, :].astype(F32)
        for ref in ins[1:]:
            total = total + ref[at, :].astype(F32)
        outs[k][...] = total.astype(BF16)


def sum_parts(arrays, n_e, block):
    n_t = len(arrays)
    return pl.pallas_call(
        functools.partial(sum_kernel, n_t=n_t, n_e=n_e, block=block),
        out_shape=[vmem((block, LANES), BF16)] * n_e,
        in_specs=[VMEM] * n_t,
        out_specs=[VMEM] * n_e,
        compiler_params=params(8),
        name="sum_parts",
    )(*arrays)


def combine_kernel(routes, pattern, *rest, n_e, holders, chunks):
    ins, (out, count, codes, index, stage, spread) = rest[:n_e], rest[n_e:]
    experts, toks = pattern.shape[0], out.shape[0]
    block = ins[0].shape[0]
    me = lax.axis_index("expert")
    lane, _ = iotas()
    for k in range(n_e):
        stage[k * block : (k + 1) * block, :] = ins[k][...].astype(F32)
    tail = stage.shape[0] - n_e * block
    stage[n_e * block :, :] = jnp.zeros((tail, LANES), F32)
    pattern_rows(pattern, codes, chunks // 2)
    for expert in range(experts):
        count[expert] = jnp.int32(0)
        own = codes[pl.ds(expert, SUB, stride=SUB), :]
        for quarter in range(4):
            first, second = positions(lanes_of(own, lane // 4 + quarter * (LANES // 4)))
            place = lane % 4
            later = place == second
            local = (quarter % 2) * (LANES // 2) + 2 * (lane // 4) + later.astype(jnp.int32)
            keep = jnp.logical_or(place == first, later)
            index[expert * 4 + quarter] = jnp.where(keep, local, -1)
    for token in range(toks):
        total = [None] * 4
        for choice in range(2):
            expert = routes[choice, token]
            slot = count[expert]
            count[expert] = slot + 1
            for odd in range(2):
                row = None
                for holder in range(holders):
                    k = jnp.bitwise_xor(me, expert * holders + holder)
                    part = stage[pl.ds(k * block + slot + odd * MOST, SUB, stride=2 * MOST), :]
                    row = part if row is None else row + part
                for half in range(2):
                    quarter = 2 * odd + half
                    local = index[expert * 4 + quarter]
                    value = lanes_of(row, jnp.bitwise_and(local, LANES - 1))
                    value = jnp.where(local >= 0, value, 0.0)
                    total[quarter] = value if choice == 0 else total[quarter] + value
        for quarter in range(4):
            spread[pl.ds(quarter * SUB + token, SUB, stride=4 * SUB), :] = total[quarter]
    for m in range(2 * chunks):
        out[:, m * LANES : (m + 1) * LANES] = spread[m * SUB : (m + 1) * SUB, :].astype(BF16)


def combine_rows(routes, pattern, arrays, toks, width, holders, chunks):
    n_e = len(arrays)
    block = arrays[0].shape[0]
    experts = pattern.shape[0]
    return pl.pallas_call(
        functools.partial(combine_kernel, n_e=n_e, holders=holders, chunks=chunks),
        out_shape=jax.ShapeDtypeStruct((toks, width), BF16),
        in_specs=[SMEM, VMEM] + [VMEM] * n_e,
        out_specs=VMEM,
        scratch_shapes=[
            pltpu.SMEM((experts,), jnp.int32),
            pltpu.VMEM((SUB * SUB, LANES), jnp.int32),
            pltpu.VMEM((experts * 4, SUB, LANES), jnp.int32),
            pltpu.VMEM((n_e * block + region_rows() - block, LANES), F32),
            pltpu.VMEM((4 * SUB * SUB, LANES), F32),
        ],
        compiler_params=params(8),
        name="combine_rows",
    )(routes, pattern, *arrays)


def swap(value, axis, k):
    size = lax.axis_size(axis)
    return lax.ppermute(value, axis, [(i, i ^ k) for i in range(size)])


def body(x_tokens, grad_values, grad_scale, combine, routes, pattern, w_gate, w_up, w_down):
    n_e = lax.axis_size("expert")
    n_t = lax.axis_size("tensor")
    experts = pattern.shape[0]
    holders = n_e // experts
    toks, width = x_tokens.shape
    chunks = w_gate.shape[0] // LANES
    block = block_rows(chunks)

    routes, combine = routes.T, combine.T
    *sent, wg = dispatch(
        routes, combine, grad_scale, pattern, x_tokens, grad_values, w_gate, n_e, holders, chunks
    )
    parts = [sent[0]] + [swap(sent[k], "expert", k) for k in range(1, n_e)]
    wu = load_weights(w_up, sent[0])
    zx, zg = join(parts, block)
    all_x = [zx] + [swap(zx, "tensor", k) for k in range(1, n_t)]
    all_g = [zg] + [swap(zg, "tensor", k) for k in range(1, n_t)]
    rows_in, hidden, slope, silu, wd = forward(all_x, wg, wu, w_down, n_e, block, chunks)
    rows_grad, d_gate, d_up, *back = backward(all_g, slope, silu, wg, wu, wd, n_e, block, chunks)
    back = [back[0]] + [swap(back[k], "tensor", k) for k in range(1, n_t)]
    part_gate, part_up = outer(rows_in, [d_gate, d_up], 512, "grads_in")
    summed = sum_parts(back, n_e, block)
    summed = [summed[0]] + [swap(summed[k], "expert", k) for k in range(1, n_e)]
    (part_down,) = outer(hidden, [rows_grad], 1024, "grads_out")
    grad_tokens = combine_rows(routes, pattern, summed, toks, width, holders, chunks)
    return grad_tokens, part_gate, part_up, part_down


def solution(mesh):
    in_specs = (
        P(("group", "expert", "tensor"), None),
        P(("group", "expert", "tensor"), None),
        P(("group", "expert", "tensor")),
        P(("group", "expert", "tensor"), None),
        P(("group", "expert", "tensor"), None),
        P(),
        P(None, ("expert", "tensor")),
        P(None, ("expert", "tensor")),
        P(("expert", "tensor"), None),
    )
    out_specs = (
        P(("group", "expert", "tensor"), None),
        P("group", ("expert", "tensor")),
        P("group", ("expert", "tensor")),
        P(("expert", "tensor"), "group"),
    )
    return jax.shard_map(body, mesh=mesh, in_specs=in_specs, out_specs=out_specs, check_vma=False)
```

time: 79.5 us -> 50.7 us (0.64)
  Pallas kernels: 44.1 us -> 23.3 us
  local copies, waits for them, and re-layouts: 12.6 us -> 2.8 us
  waiting for transfers between devices: 3.31 us -> 5.09 us
    unnamed x18 -> x8, local copies, waits for them, and re-layouts: 12.6 us -> 2.8 us
    pallas_call x1, Pallas kernels: 12.5 us -> 6.1 us  [backward(): pl.pallas_call(functools.partial(backward_kernel, n_t=n_t, n_e=n_e, block...]
    pallas_call x1, Pallas kernels: 6.52 us -> 0.46 us  [load_weights(): pl.pallas_call(load_kernel, out_shape=vmem(weights.shape, weights.dtype),...]
    pallas_call x1, Pallas kernels: 7.14 us -> 3 us  [forward(): pl.pallas_call(functools.partial(forward_kernel, n_t=n_t, n_e=n_e, block=...]
    pallas_call x1, Pallas kernels: 3.93 us -> 1.56 us  [combine_rows(): pl.pallas_call(functools.partial(combine_kernel, n_e=n_e, holders=holders...]
    pallas_call x2, Pallas kernels: 11.5 us -> 9.2 us  [outer(): pl.pallas_call(outer_kernel, grid=(m // tile,), out_shape=[jax.ShapeDtype...]
    ppermute x15, waiting for transfers between devices: 3.31 us -> 5.09 us  [swap(): return lax.ppermute(value, axis, [(i, i ^ k) for i in range(size)])]
  transfers between devices with their start and end apart: 15 -> 15, of which waited for: 2 -> 4; matrix products, arithmetic and copies ran while one was open for 0% -> 0% of each run, Pallas kernels for 32% -> 25%
where the time goes in v2:
time: 50.7 us; the launch traced here: 50.4 us
  Pallas kernels  23.3 us (46%)
  starting transfers between devices  18.5 us (36%)
  waiting for transfers between devices  5.09 us (10%)
  local copies, waits for them, and re-layouts  2.8 us (6%)
  between operations  0.75 us (1%)
    ppermute x15, starting transfers between devices, swap(): return lax.ppermute(value, axis, [(i, i ^ k) for i in range(size)])  18.5 us
    pallas_call x2, Pallas kernels, outer(): pl.pallas_call(outer_kernel, grid=(m // tile,), out_shape=[jax.ShapeDtype...  9.2 us
    pallas_call x1, Pallas kernels, backward(): pl.pallas_call(functools.partial(backward_kernel, n_t=n_t, n_e=n_e, block...  6.1 us
    ppermute x15, waiting for transfers between devices, swap(): return lax.ppermute(value, axis, [(i, i ^ k) for i in range(size)])  5.09 us
    pallas_call x1, Pallas kernels, forward(): pl.pallas_call(functools.partial(forward_kernel, n_t=n_t, n_e=n_e, block=...  3 us
    pallas_call x1, Pallas kernels, dispatch(): pl.pallas_call(functools.partial(dispatch_kernel, n_e=n_e, holders=holder...  2.97 us
    unnamed x8, local copies, waits for them, and re-layouts  2.8 us
    pallas_call x1, Pallas kernels, combine_rows(): pl.pallas_call(functools.partial(combine_kernel, n_e=n_e, holders=holders...  1.56 us
  transfers between devices with their start and end apart: 15, of which 4 were waited for; matrix products, arithmetic and copies ran while one was open for 0% of the time, Pallas kernels for 25%

profile of v2, /device:TPU:0, one launch (start us, length us, event | category | flops | bytes accessed | tf_op | source)
XLA Modules:
  0.0 50.4 jit_solution(2020023720605817320)
XLA Ops:
  0.6 3.0 %dispatch.1 = (bf16[128,128]{1,0:T(8,128)(2,1)S(1)}, bf16[128,128]{1,0:T(8,128)(2,1)S(1)}, bf16[128,128]{1,0:T(8,128)(2,1)S(1)}, bf16[128,128]{1,0:T(8,128)(2,1)S(1)}, bf16[1536,2048]{1,0:T(8,128)(2,1)S(1)}) custom-call(s32[2,8]{1,0:T(2,128)} %bitcast.2, f32[2,8]{1,0:T(2,128)} %bitcast.4, f32[8]{0:T(128)} %scale_any.1, s32[4,768]{1,0:T(4,128)} %pattern.1, ...), custom_call_target="tpu_custom_call" | custom-call | tf_op jit(solution)/shard_map/dispatch/pallas_call | solution.py:174
  3.6 0.5 %collective-permute-start = (bf16[128,128]{1,0:T(8,128)(2,1)S(1)}, bf16[128,128]{1,0:T(8,128)(2,1)S(1)}, u32[]{:S(2)}, u32[]{:S(2)}) collective-permute-start(bf16[128,128]{1,0:T(8,128)(2,1)S(1)} %get-tuple-element.30), channel_id=1, source_target_pairs={{0,4},{4,0},{8,12},{12,8},{1,5},{5,1},{9,13},{13,9},{2,6},{6,2},{1... | collective-permute-start | bytes 98312 | tf_op jit(solution)/shard_map/ppermute | solution.py:454
  4.1 2.6 %collective-permute-start.1 = (bf16[128,128]{1,0:T(8,128)(2,1)S(1)}, bf16[128,128]{1,0:T(8,128)(2,1)S(1)}, u32[]{:S(2)}, u32[]{:S(2)}) collective-permute-start(bf16[128,128]{1,0:T(8,128)(2,1)S(1)} %get-tuple-element.31), channel_id=1, source_target_pairs={{0,8},{4,12},{8,0},{12,4},{1,9},{5,13},{9,1},{13,5},{2,10},{6,14},... | collective-permute-start | bytes 98312 | tf_op jit(solution)/shard_map/ppermute | solution.py:454
  6.7 0.1 collective-permute-start.2
  6.8 0.0 collective-permute-done.refs_1_
  6.8 1.9 %collective-permute-done.1.refs_2_ = bf16[128,128]{1,0:T(8,128)(2,1)S(1)} collective-permute-done((bf16[128,128]{1,0:T(8,128)(2,1)S(1)}, bf16[128,128]{1,0:T(8,128)(2,1)S(1)}, u32[]{:S(2)}, u32[]{:S(2)}) %collective-permute-start.1) | collective-permute-done | bytes 32800 | tf_op jit(solution)/shard_map/ppermute | solution.py:454
  8.7 1.4 %collective-permute-done.2.refs_3_ = bf16[128,128]{1,0:T(8,128)(2,1)S(1)} collective-permute-done((bf16[128,128]{1,0:T(8,128)(2,1)S(1)}, bf16[128,128]{1,0:T(8,128)(2,1)S(1)}, u32[]{:S(2)}, u32[]{:S(2)}) %collective-permute-start.2) | collective-permute-done | bytes 32800 | tf_op jit(solution)/shard_map/ppermute | solution.py:454
  10.1 3.7 %collective-permute-start.8 = (bf16[256,128]{1,0:T(8,128)(2,1)S(1)}, bf16[256,128]{1,0:T(8,128)(2,1)S(1)}, u32[]{:S(2)}, u32[]{:S(2)}) collective-permute-start(bf16[256,128]{1,0:T(8,128)(2,1)S(1)} %get-tuple-element.34.refs_0_), channel_id=1, source_target_pairs={{0,3},{1,2},{2,1},{3,0},{4,7},{5,6},{6,5},{7,4},{8,11},{9,10},{10,... | collective-permute-start | bytes 196616 | tf_op jit(solution)/shard_map/ppermute | solution.py:454
  13.7 0.0 collective-permute-start.7
  13.8 0.8 %collective-permute-start.6 = (bf16[256,128]{1,0:T(8,128)(2,1)S(1)}, bf16[256,128]{1,0:T(8,128)(2,1)S(1)}, u32[]{:S(2)}, u32[]{:S(2)}) collective-permute-start(bf16[256,128]{1,0:T(8,128)(2,1)S(1)} %get-tuple-element.34.refs_0_), channel_id=1, source_target_pairs={{0,1},{1,0},{2,3},{3,2},{4,5},{5,4},{6,7},{7,6},{8,9},{9,8},{10,11... | collective-permute-start | bytes 196616 | tf_op jit(solution)/shard_map/ppermute | solution.py:454
  14.5 0.0 copy-start
  14.5 2.8 %copy-done = bf16[1536,2048]{1,0:T(8,128)(2,1)S(1)} copy-done((bf16[1536,2048]{1,0:T(8,128)(2,1)S(1)}, bf16[1536,2048]{1,0:T(8,128)(2,1)}, u32[]{:S(2)}) %copy-start) | copy-done | bytes 6291480
  17.3 0.0 copy-start.1
  17.3 0.5 load_weights.1.refs_5_.refs_7_
  17.8 3.7 %collective-permute-start.5 = (bf16[256,128]{1,0:T(8,128)(2,1)S(1)}, bf16[256,128]{1,0:T(8,128)(2,1)S(1)}, u32[]{:S(2)}, u32[]{:S(2)}) collective-permute-start(bf16[256,128]{1,0:T(8,128)(2,1)S(1)} %get-tuple-element.33.refs_0_), channel_id=1, source_target_pairs={{0,3},{1,2},{2,1},{3,0},{4,7},{5,6},{6,5},{7,4},{8,11},{9,10},{10,... | collective-permute-start | bytes 196616 | tf_op jit(solution)/shard_map/ppermute | solution.py:454
  21.5 0.0 collective-permute-start.4
  21.5 0.0 collective-permute-done.8.refs_3_
  21.5 0.8 %collective-permute-start.3 = (bf16[256,128]{1,0:T(8,128)(2,1)S(1)}, bf16[256,128]{1,0:T(8,128)(2,1)S(1)}, u32[]{:S(2)}, u32[]{:S(2)}) collective-permute-start(bf16[256,128]{1,0:T(8,128)(2,1)S(1)} %get-tuple-element.33.refs_0_), channel_id=1, source_target_pairs={{0,1},{1,0},{2,3},{3,2},{4,5},{5,4},{6,7},{7,6},{8,9},{9,8},{10,11... | collective-permute-start | bytes 196616 | tf_op jit(solution)/shard_map/ppermute | solution.py:454
  22.2 0.0 collective-permute-done.7.refs_2_
  22.3 0.0 collective-permute-done.6.refs_1_
  22.3 0.0 copy-done.1
  22.3 3.0 %forward.1 = (bf16[80,1536]{1,0:T(8,128)(2,1)S(1)}, bf16[80,2048]{1,0:T(8,128)(2,1)S(1)}, f32[80,2048]{1,0:T(8,128)S(1)}, f32[80,2048]{1,0:T(8,128)S(1)}, bf16[2048,1536]{1,0:T(8,128)(2,1)S(1)}) custom-call(bf16[256,128]{1,0:T(8,128)(2,1)S(1)} %get-tuple-element.34.refs_0_, bf16[256,128]{1,0:T(8,128)(2,1)S(1)} %collective-permute-done.6.refs_1_, ...), custom_call_target="tpu_custom_call" | custom-call | flops 4026531840 | bytes 12582912 | tf_op jit(solution)/shard_map/forward/pallas_call | solution.py:261
  25.3 0.0 collective-permute-done.5.refs_3_
  25.3 1.5 %collective-permute-done.4.refs_2_ = bf16[256,128]{1,0:T(8,128)(2,1)S(1)} collective-permute-done((bf16[256,128]{1,0:T(8,128)(2,1)S(1)}, bf16[256,128]{1,0:T(8,128)(2,1)S(1)}, u32[]{:S(2)}, u32[]{:S(2)}) %collective-permute-start.4) | collective-permute-done | bytes 65568 | tf_op jit(solution)/shard_map/ppermute | solution.py:454
  26.7 0.3 collective-permute-done.3.refs_1_
  27.1 6.1 %backward.1 = (bf16[80,1536]{1,0:T(8,128)(2,1)S(1)}, bf16[80,2048]{1,0:T(8,128)(2,1)S(1)}, bf16[80,2048]{1,0:T(8,128)(2,1)S(1)}, bf16[256,128]{1,0:T(8,128)(2,1)...) custom-call(bf16[256,128]{1,0:T(8,128)(2,1)S(1)} %get-tuple-element.33.refs_0_, ...), custom_call_target="tpu_custom_call" | custom-call | flops 6039797760 | bytes 18874368 | tf_op jit(solution)/shard_map/backward/pallas_call | solution.py:318
  33.2 0.6 %collective-permute-start.9 = (bf16[256,128]{1,0:T(8,128)(2,1)S(1)}, bf16[256,128]{1,0:T(8,128)(2,1)S(1)}, u32[]{:S(2)}, u32[]{:S(2)}) collective-permute-start(bf16[256,128]{1,0:T(8,128)(2,1)S(1)} %get-tuple-element.40), channel_id=1, source_target_pairs={{0,1},{1,0},{2,3},{3,2},{4,5},{5,4},{6,7},{7,6},{8,9},{9,8},{10,11... | collective-permute-start | bytes 196616 | tf_op jit(solution)/shard_map/ppermute | solution.py:454
  33.8 2.2 %collective-permute-start.10 = (bf16[256,128]{1,0:T(8,128)(2,1)S(1)}, bf16[256,128]{1,0:T(8,128)(2,1)S(1)}, u32[]{:S(2)}, u32[]{:S(2)}) collective-permute-start(bf16[256,128]{1,0:T(8,128)(2,1)S(1)} %get-tuple-element.41), channel_id=1, source_target_pairs={{0,2},{1,3},{2,0},{3,1},{4,6},{5,7},{6,4},{7,5},{8,10},{9,11},{10,... | collective-permute-start | bytes 196616 | tf_op jit(solution)/shard_map/ppermute | solution.py:454
  36.0 1.6 %collective-permute-start.11 = (bf16[256,128]{1,0:T(8,128)(2,1)S(1)}, bf16[256,128]{1,0:T(8,128)(2,1)S(1)}, u32[]{:S(2)}, u32[]{:S(2)}) collective-permute-start(bf16[256,128]{1,0:T(8,128)(2,1)S(1)} %get-tuple-element.42), channel_id=1, source_target_pairs={{0,3},{1,2},{2,1},{3,0},{4,7},{5,6},{6,5},{7,4},{8,11},{9,10},{10,... | collective-permute-start | bytes 196616 | tf_op jit(solution)/shard_map/ppermute | solution.py:454
  37.6 5.4 %grads_in.1 = (bf16[1536,2048]{1,0:T(8,128)(2,1)}, bf16[1536,2048]{1,0:T(8,128)(2,1)}) custom-call(bf16[80,1536]{1,0:T(8,128)(2,1)S(1)} %get-tuple-element.47.left, bf16[80,2048]{1,0:T(8,128)(2,1)S(1)} %get-tuple-element.48.refs_0_, bf16[80,2048]{1,0:T(8,128)(2,1)S(1)} %get-tuple-element.49.refs_1_), custom_call_target="tpu_custom_call" | custom-call | flops 3221225472 | bytes 12582912 | tf_op jit(solution)/shard_map/grads_in/pallas_call | solution.py:351
  43.1 0.0 copy-start.2
  43.1 0.0 copy-start.3
  43.1 0.0 collective-permute-done.9.refs_1_
  43.1 0.0 collective-permute-done.10.refs_2_
  43.1 0.0 collective-permute-done.11.refs_3_
  43.2 0.1 collective-permute-start.12
  43.2 0.9 %collective-permute-start.13 = (bf16[64,128]{1,0:T(8,128)(2,1)S(1)}, bf16[64,128]{1,0:T(8,128)(2,1)S(1)}, u32[]{:S(2)}, u32[]{:S(2)}) collective-permute-start(bf16[64,128]{1,0:T(8,128)(2,1)S(1)} %get-tuple-element.45), channel_id=1, source_target_pairs={{0,8},{4,12},{8,0},{12,4},{1,9},{5,13},{9,1},{13,5},{2,10},{6,14},... | collective-permute-start | bytes 49160 | tf_op jit(solution)/shard_map/ppermute | solution.py:454
  44.2 0.9 %collective-permute-start.14 = (bf16[64,128]{1,0:T(8,128)(2,1)S(1)}, bf16[64,128]{1,0:T(8,128)(2,1)S(1)}, u32[]{:S(2)}, u32[]{:S(2)}) collective-permute-start(bf16[64,128]{1,0:T(8,128)(2,1)S(1)} %get-tuple-element.46), channel_id=1, source_target_pairs={{0,12},{4,8},{8,4},{12,0},{1,13},{5,9},{9,5},{13,1},{2,14},{6,10},... | collective-permute-start | bytes 49160 | tf_op jit(solution)/shard_map/ppermute | solution.py:454
  45.1 3.8 %grads_out.1 = bf16[2048,1536]{1,0:T(8,128)(2,1)} custom-call(bf16[80,2048]{1,0:T(8,128)(2,1)S(1)} %get-tuple-element.52.left, bf16[80,1536]{1,0:T(8,128)(2,1)S(1)} %get-tuple-element.53.refs_0_), custom_call_target="tpu_custom_call" | custom-call | flops 1610612736 | bytes 6291456 | tf_op jit(solution)/shard_map/grads_out/pallas_call | solution.py:351
  48.9 0.0 collective-permute-done.12.rest_1_
  48.9 0.0 collective-permute-done.13.rest_2_
  48.9 0.0 collective-permute-done.14.rest_3_
  48.9 0.0 copy-done.2
  48.9 0.0 copy-done.3
  48.9 1.6 %combine_rows.1 = bf16[8,3072]{1,0:T(8,128)(2,1)} custom-call(s32[2,8]{1,0:T(2,128)S(1)} %bitcast.3, s32[4,768]{1,0:T(4,128)S(1)} %copy-done.2, bf16[64,128]{1,0:T(8,128)(2,1)S(1)} %get-tuple-element.43.rest_0_, bf16[64,128]{1,0:T(8,128)(2,1)S(1)} %collective-permute-done.12.rest_1_, bf16[64,128]{1,0:T(8,128)(2,1)S(1)} %collective-permute-done.13.rest_2_, ...), custom_call_target="tpu_custom_call" | custom-call | tf_op jit(solution)/shard_map/combine_rows/pallas_call | solution.py:435
  (2 shorter events, 0.0 us)
Async XLA Ops:
  3.6 3.2 %collective-permute-start = (bf16[128,128]{1,0:T(8,128)(2,1)S(1)}, bf16[128,128]{1,0:T(8,128)(2,1)S(1)}, u32[]{:S(2)}, u32[]{:S(2)}) collective-permute-start(bf16[128,128]{1,0:T(8,128)(2,1)S(1)} %get-tuple-element.30), channel_id=1, source_target_pairs={{0,4},{4,0},{8,12},{12,8},{1,5},{5,1},{9,13},{13,9},{2,6},{6,2},{1... | collective-permute-start | bytes 98312 | tf_op jit(solution)/shard_map/ppermute | solution.py:454
  4.1 4.6 %collective-permute-start.1 = (bf16[128,128]{1,0:T(8,128)(2,1)S(1)}, bf16[128,128]{1,0:T(8,128)(2,1)S(1)}, u32[]{:S(2)}, u32[]{:S(2)}) collective-permute-start(bf16[128,128]{1,0:T(8,128)(2,1)S(1)} %get-tuple-element.31), channel_id=1, source_target_pairs={{0,8},{4,12},{8,0},{12,4},{1,9},{5,13},{9,1},{13,5},{2,10},{6,14},... | collective-permute-start | bytes 98312 | tf_op jit(solution)/shard_map/ppermute | solution.py:454
  6.7 3.3 %collective-permute-start.2 = (bf16[128,128]{1,0:T(8,128)(2,1)S(1)}, bf16[128,128]{1,0:T(8,128)(2,1)S(1)}, u32[]{:S(2)}, u32[]{:S(2)}) collective-permute-start(bf16[128,128]{1,0:T(8,128)(2,1)S(1)} %get-tuple-element.32), channel_id=1, source_target_pairs={{0,12},{4,8},{8,4},{12,0},{1,13},{5,9},{9,5},{13,1},{2,14},{6,10},... | collective-permute-start | bytes 98312 | tf_op jit(solution)/shard_map/ppermute | solution.py:454
  10.1 11.4 %collective-permute-start.8 = (bf16[256,128]{1,0:T(8,128)(2,1)S(1)}, bf16[256,128]{1,0:T(8,128)(2,1)S(1)}, u32[]{:S(2)}, u32[]{:S(2)}) collective-permute-start(bf16[256,128]{1,0:T(8,128)(2,1)S(1)} %get-tuple-element.34.refs_0_), channel_id=1, source_target_pairs={{0,3},{1,2},{2,1},{3,0},{4,7},{5,6},{6,5},{7,4},{8,11},{9,10},{10,... | collective-permute-start | bytes 196616 | tf_op jit(solution)/shard_map/ppermute | solution.py:454
  13.7 8.5 %collective-permute-start.7 = (bf16[256,128]{1,0:T(8,128)(2,1)S(1)}, bf16[256,128]{1,0:T(8,128)(2,1)S(1)}, u32[]{:S(2)}, u32[]{:S(2)}) collective-permute-start(bf16[256,128]{1,0:T(8,128)(2,1)S(1)} %get-tuple-element.34.refs_0_), channel_id=1, source_target_pairs={{0,2},{1,3},{2,0},{3,1},{4,6},{5,7},{6,4},{7,5},{8,10},{9,11},{10,... | collective-permute-start | bytes 196616 | tf_op jit(solution)/shard_map/ppermute | solution.py:454
  13.8 8.5 %collective-permute-start.6 = (bf16[256,128]{1,0:T(8,128)(2,1)S(1)}, bf16[256,128]{1,0:T(8,128)(2,1)S(1)}, u32[]{:S(2)}, u32[]{:S(2)}) collective-permute-start(bf16[256,128]{1,0:T(8,128)(2,1)S(1)} %get-tuple-element.34.refs_0_), channel_id=1, source_target_pairs={{0,1},{1,0},{2,3},{3,2},{4,5},{5,4},{6,7},{7,6},{8,9},{9,8},{10,11... | collective-permute-start | bytes 196616 | tf_op jit(solution)/shard_map/ppermute | solution.py:454
  14.5 2.8 %copy-start = (bf16[1536,2048]{1,0:T(8,128)(2,1)S(1)}, bf16[1536,2048]{1,0:T(8,128)(2,1)}, u32[]{:S(2)}) copy-start(bf16[1536,2048]{1,0:T(8,128)(2,1)} %w_ref.1) | copy-start | bytes 18874372
  17.3 4.9 %copy-start.1 = (bf16[2048,1536]{1,0:T(8,128)(2,1)S(1)}, bf16[2048,1536]{1,0:T(8,128)(2,1)}, u32[]{:S(2)}) copy-start(bf16[2048,1536]{1,0:T(8,128)(2,1)} %refs_6_.1) | copy-start | bytes 18874372
  17.8 7.5 %collective-permute-start.5 = (bf16[256,128]{1,0:T(8,128)(2,1)S(1)}, bf16[256,128]{1,0:T(8,128)(2,1)S(1)}, u32[]{:S(2)}, u32[]{:S(2)}) collective-permute-start(bf16[256,128]{1,0:T(8,128)(2,1)S(1)} %get-tuple-element.33.refs_0_), channel_id=1, source_target_pairs={{0,3},{1,2},{2,1},{3,0},{4,7},{5,6},{6,5},{7,4},{8,11},{9,10},{10,... | collective-permute-start | bytes 196616 | tf_op jit(solution)/shard_map/ppermute | solution.py:454
  21.5 5.3 %collective-permute-start.4 = (bf16[256,128]{1,0:T(8,128)(2,1)S(1)}, bf16[256,128]{1,0:T(8,128)(2,1)S(1)}, u32[]{:S(2)}, u32[]{:S(2)}) collective-permute-start(bf16[256,128]{1,0:T(8,128)(2,1)S(1)} %get-tuple-element.33.refs_0_), channel_id=1, source_target_pairs={{0,2},{1,3},{2,0},{3,1},{4,6},{5,7},{6,4},{7,5},{8,10},{9,11},{10,... | collective-permute-start | bytes 196616 | tf_op jit(solution)/shard_map/ppermute | solution.py:454
  21.5 5.6 %collective-permute-start.3 = (bf16[256,128]{1,0:T(8,128)(2,1)S(1)}, bf16[256,128]{1,0:T(8,128)(2,1)S(1)}, u32[]{:S(2)}, u32[]{:S(2)}) collective-permute-start(bf16[256,128]{1,0:T(8,128)(2,1)S(1)} %get-tuple-element.33.refs_0_), channel_id=1, source_target_pairs={{0,1},{1,0},{2,3},{3,2},{4,5},{5,4},{6,7},{7,6},{8,9},{9,8},{10,11... | collective-permute-start | bytes 196616 | tf_op jit(solution)/shard_map/ppermute | solution.py:454
  33.2 9.9 %collective-permute-start.9 = (bf16[256,128]{1,0:T(8,128)(2,1)S(1)}, bf16[256,128]{1,0:T(8,128)(2,1)S(1)}, u32[]{:S(2)}, u32[]{:S(2)}) collective-permute-start(bf16[256,128]{1,0:T(8,128)(2,1)S(1)} %get-tuple-element.40), channel_id=1, source_target_pairs={{0,1},{1,0},{2,3},{3,2},{4,5},{5,4},{6,7},{7,6},{8,9},{9,8},{10,11... | collective-permute-start | bytes 196616 | tf_op jit(solution)/shard_map/ppermute | solution.py:454
  33.8 9.3 %collective-permute-start.10 = (bf16[256,128]{1,0:T(8,128)(2,1)S(1)}, bf16[256,128]{1,0:T(8,128)(2,1)S(1)}, u32[]{:S(2)}, u32[]{:S(2)}) collective-permute-start(bf16[256,128]{1,0:T(8,128)(2,1)S(1)} %get-tuple-element.41), channel_id=1, source_target_pairs={{0,2},{1,3},{2,0},{3,1},{4,6},{5,7},{6,4},{7,5},{8,10},{9,11},{10,... | collective-permute-start | bytes 196616 | tf_op jit(solution)/shard_map/ppermute | solution.py:454
  36.0 7.1 %collective-permute-start.11 = (bf16[256,128]{1,0:T(8,128)(2,1)S(1)}, bf16[256,128]{1,0:T(8,128)(2,1)S(1)}, u32[]{:S(2)}, u32[]{:S(2)}) collective-permute-start(bf16[256,128]{1,0:T(8,128)(2,1)S(1)} %get-tuple-element.42), channel_id=1, source_target_pairs={{0,3},{1,2},{2,1},{3,0},{4,7},{5,6},{6,5},{7,4},{8,11},{9,10},{10,... | collective-permute-start | bytes 196616 | tf_op jit(solution)/shard_map/ppermute | solution.py:454
  43.1 5.8 %copy-start.2 = (s32[4,768]{1,0:T(4,128)S(1)}, s32[4,768]{1,0:T(4,128)}, u32[]{:S(2)}) copy-start(s32[4,768]{1,0:T(4,128)} %pattern.1) | copy-start | bytes 36868
  43.1 5.8 %copy-start.3 = (s32[8,2]{0,1:T(2,128)S(1)}, s32[8,2]{0,1:T(2,128)}, u32[]{:S(2)}) copy-start(s32[8,2]{0,1:T(2,128)} %param.13) | copy-start | bytes 196
  43.2 5.7 %collective-permute-start.12 = (bf16[64,128]{1,0:T(8,128)(2,1)S(1)}, bf16[64,128]{1,0:T(8,128)(2,1)S(1)}, u32[]{:S(2)}, u32[]{:S(2)}) collective-permute-start(bf16[64,128]{1,0:T(8,128)(2,1)S(1)} %get-tuple-element.44), channel_id=1, source_target_pairs={{0,4},{4,0},{8,12},{12,8},{1,5},{5,1},{9,13},{13,9},{2,6},{6,2},{1... | collective-permute-start | bytes 49160 | tf_op jit(solution)/shard_map/ppermute | solution.py:454
  43.2 5.6 %collective-permute-start.13 = (bf16[64,128]{1,0:T(8,128)(2,1)S(1)}, bf16[64,128]{1,0:T(8,128)(2,1)S(1)}, u32[]{:S(2)}, u32[]{:S(2)}) collective-permute-start(bf16[64,128]{1,0:T(8,128)(2,1)S(1)} %get-tuple-element.45), channel_id=1, source_target_pairs={{0,8},{4,12},{8,0},{12,4},{1,9},{5,13},{9,1},{13,5},{2,10},{6,14},... | collective-permute-start | bytes 49160 | tf_op jit(solution)/shard_map/ppermute | solution.py:454
  44.2 4.7 %collective-permute-start.14 = (bf16[64,128]{1,0:T(8,128)(2,1)S(1)}, bf16[64,128]{1,0:T(8,128)(2,1)S(1)}, u32[]{:S(2)}, u32[]{:S(2)}) collective-permute-start(bf16[64,128]{1,0:T(8,128)(2,1)S(1)} %get-tuple-element.46), channel_id=1, source_target_pairs={{0,12},{4,8},{8,4},{12,0},{1,13},{5,9},{9,5},{13,1},{2,14},{6,10},... | collective-permute-start | bytes 49160 | tf_op jit(solution)/shard_map/ppermute | solution.py:454

commit v3 on v2

--- a/solution.py
+++ b/solution.py
@@ -11,7 +11,7 @@
 LANES = 128
 SUB = 8
 PIECES = 4
-DISPATCH_MIB = 56
+TOKEN = (SUB, LANES)
 F32 = jnp.float32
 BF16 = jnp.bfloat16
 VMEM = pl.BlockSpec(memory_space=pltpu.VMEM)
@@ -21,6 +21,10 @@
 
 def vmem(shape, dtype):
     return pltpu.VMEM(shape, dtype)
+
+
+def in_hbm(value):
+    return pltpu.with_memory_space_constraint(value, pltpu.HBM)
 
 
 def params(mib=48):
@@ -70,33 +74,12 @@
     ]
 
 
-def load_kernel(w_ref, after, w_out, sems):
-    loads = row_copies(w_ref, w_out, sems)
-    for load in loads:
-        load.start()
-    for load in loads:
-        load.wait()
-
-
-def load_weights(weights, after):
-    return pl.pallas_call(
-        load_kernel,
-        out_shape=vmem(weights.shape, weights.dtype),
-        in_specs=[ANY] * 2,
-        out_specs=VMEM,
-        scratch_shapes=[pltpu.SemaphoreType.DMA((PIECES,))],
-        compiler_params=params(4),
-        cost_estimate=cost(0, 2 * weights.size),
-        name="load_weights",
-    )(weights, after)
-
-
 def dispatch_kernel(
-    routes_any, combine_any, scale_any, pattern_any, x_any, g_any, w_any, *rest, n_e, holders, chunks
+    routes_any, combine_any, scale_any, pattern_any, x_any, g_any, _a, _b, _c, *rest, n_e, holders, chunks
 ):
-    outs, rest = rest[:n_e], rest[n_e:]
-    w_out, routes, weights, scale, count, pattern, x_in, g_in, codes = rest[:9]
-    x_rows, g_rows, index, stage, in_sems, sems = rest[9:]
+    outs, rest = rest[:2], rest[2:]
+    routes, weights, scale, count, pattern, x_in, g_in, codes = rest[:8]
+    x_rows, g_rows, index, stage, in_sems = rest[8:]
     moves = [
         pltpu.make_async_copy(source, target, in_sems.at[i])
         for i, (source, target) in enumerate(
@@ -112,9 +95,6 @@
     ]
     for move in moves:
         move.start()
-    loads = row_copies(w_any, w_out, sems)
-    for load in loads:
-        load.start()
     experts, toks = pattern.shape[0], x_in.shape[0]
     parts = chunks // 2
     block, region = block_rows(chunks), region_rows()
@@ -157,25 +137,22 @@
         expert = jnp.bitwise_xor(me, k) // holders
         for array in range(2):
             at = pl.multiple_of((expert * 2 + array) * region, 16)
-            outs[k][array * block : (array + 1) * block, :] = stage[pl.ds(at, block), :].astype(
-                BF16
-            )
-    for load in loads:
-        load.wait()
+            to = (k // 2 * 2 + array) * block
+            outs[k % 2][to : to + block, :] = stage[pl.ds(at, block), :].astype(BF16)
 
 
 def region_rows():
     return -(-((SUB - 1) * 2 * MOST + 2 * MOST) // 16) * 16
 
 
-def dispatch(routes, combine, scale, pattern, x, g, weights, n_e, holders, chunks):
+def dispatch(routes, combine, scale, pattern, x, g, ws, n_e, holders, chunks):
     block, region = block_rows(chunks), region_rows()
     experts, toks = pattern.shape[0], x.shape[0]
     return pl.pallas_call(
         functools.partial(dispatch_kernel, n_e=n_e, holders=holders, chunks=chunks),
-        out_shape=[vmem((2 * block, LANES), BF16)] * n_e + [vmem(weights.shape, weights.dtype)],
-        in_specs=[ANY] * 7,
-        out_specs=[VMEM] * (n_e + 1),
+        out_shape=[vmem((n_e * block, LANES), BF16)] * 2,
+        in_specs=[ANY] * 9,
+        out_specs=[VMEM] * 2,
         scratch_shapes=[
             pltpu.SMEM(routes.shape, jnp.int32),
             pltpu.SMEM(combine.shape, F32),
@@ -190,30 +167,62 @@
             pltpu.VMEM((experts * 2, SUB, LANES), jnp.int32),
             pltpu.VMEM((experts * 2 * region, LANES), F32),
             pltpu.SemaphoreType.DMA((6,)),
-            pltpu.SemaphoreType.DMA((PIECES,)),
         ],
-        compiler_params=params(DISPATCH_MIB),
+        compiler_params=params(8),
         name="dispatch",
-    )(routes, combine, scale, pattern, x, g, weights)
-
-
-def join_kernel(*refs, n_e, block):
-    ins, (zx, zg) = refs[:n_e], refs[n_e:]
-    for k in range(n_e):
-        zx[k * block : (k + 1) * block, :] = ins[k][:block, :]
-        zg[k * block : (k + 1) * block, :] = ins[k][block:, :]
-
-
-def join(parts, block):
-    n_e = len(parts)
-    return pl.pallas_call(
-        functools.partial(join_kernel, n_e=n_e, block=block),
-        out_shape=[vmem((n_e * block, LANES), BF16)] * 2,
-        in_specs=[VMEM] * n_e,
+    )(*(in_hbm(v) for v in (routes, combine, scale, pattern, x, g, *ws)))
+
+
+def merge_kernel(keep, received, keep_out, send_out, *, run):
+    for h in range(keep.shape[0] // run):
+        at, to = slice(h * run, (h + 1) * run), h // 2 * 2 * run
+        out = send_out if h % 2 else keep_out
+        out[to : to + run, :] = keep[at, :]
+        out[to + run : to + 2 * run, :] = received[at, :]
+
+
+def merge(keep, received, run):
+    return pl.pallas_call(
+        functools.partial(merge_kernel, run=run),
+        out_shape=[vmem(keep.shape, BF16)] * 2,
+        in_specs=[VMEM] * 2,
         out_specs=[VMEM] * 2,
         compiler_params=params(8),
+        name="merge",
+    )(keep, received)
+
+
+def exchange(keep, send, rows):
+    n_e = lax.axis_size("expert")
+    bit = 1
+    while True:
+        received = swap(send, "expert", bit)
+        if 2 * bit >= n_e:
+            return keep, received
+        keep, send = merge(keep, received, bit * rows)
+        bit *= 2
+
+
+def join_kernel(keep, received, zx, zg, stage, *, n_e, block, dense):
+    for array, out in enumerate((zx, zg)):
+        for k in range(n_e):
+            half, at = divmod(k, n_e // 2)
+            at = (2 * at + array) * block
+            source = (keep, received)[half]
+            stage[k * dense : k * dense + block, :] = source[at : at + block, :].astype(F32)
+        out[...] = stage[: n_e * dense, :].astype(BF16)
+
+
+def join(keep, received, n_e, block, dense):
+    return pl.pallas_call(
+        functools.partial(join_kernel, n_e=n_e, block=block, dense=dense),
+        out_shape=[vmem((n_e * dense, LANES), BF16)] * 2,
+        in_specs=[VMEM] * 2,
+        out_specs=[VMEM] * 2,
+        scratch_shapes=[pltpu.VMEM((n_e * dense + block, LANES), F32)],
+        compiler_params=params(8),
         name="join",
-    )(*parts)
+    )(keep, received)
 
 
 def unpack_rows(arrays, stage, rows_ref, n_e, block, chunks):
@@ -233,8 +242,12 @@
 
 
 def forward_kernel(*refs, n_t, n_e, block, chunks):
-    arrays, (wg, wu, wd, rows, hidden, slope, silu_out, wd_out, stage, sems) = refs[:n_t], refs[n_t:]
-    loads = row_copies(wd, wd_out, sems)
+    arrays, refs = refs[:n_t], refs[n_t:]
+    (wg, wu), (rows, hidden, slope, silu_out), held = refs[:2], refs[2:6], refs[6:8]
+    stage, sems = refs[8:]
+    loads = []
+    for i, (source, target) in enumerate(zip((wg, wu), held)):
+        loads += row_copies(source, target, sems.at[i])
     for load in loads:
         load.start()
     unpack_rows(arrays, stage, rows, n_e, block, chunks)
@@ -254,7 +267,7 @@
         load.wait()
 
 
-def forward(arrays, wg, wu, wd, n_e, block, chunks):
+def forward(arrays, wg, wu, n_e, block, chunks):
     n_t = len(arrays)
     count = MOST * n_e * n_t
     kept, hid = wg.shape
@@ -265,23 +278,23 @@
             vmem((count, hid), BF16),
             vmem((count, hid), F32),
             vmem((count, hid), F32),
-            vmem(wd.shape, wd.dtype),
+            *(vmem(w.shape, w.dtype) for w in (wg, wu)),
         ],
-        in_specs=[VMEM] * (n_t + 2) + [ANY],
-        out_specs=[VMEM] * 5,
+        in_specs=[VMEM] * (n_t + 2),
+        out_specs=[VMEM] * 6,
         scratch_shapes=[
             pltpu.VMEM((n_t * n_e * block, LANES), F32),
-            pltpu.SemaphoreType.DMA((PIECES,)),
+            pltpu.SemaphoreType.DMA((2, PIECES)),
         ],
         compiler_params=params(12),
         cost_estimate=cost(4 * 4 * count * kept * hid, 4 * kept * hid),
         name="forward",
-    )(*arrays, wg, wu, wd)
+    )(*arrays, wg, wu)
 
 
 def backward_kernel(*refs, n_t, n_e, block, chunks):
     arrays, (slope, silu, wg, wu, wd), rest = refs[:n_t], refs[n_t : n_t + 5], refs[n_t + 5 :]
-    (rows, d_gate, d_up), outs, (stage, total) = rest[:3], rest[3 : 3 + n_t], rest[3 + n_t :]
+    (rows, d_gate, d_up), outs, stage = rest[:3], rest[3 : 3 + n_t], rest[3 + n_t]
     unpack_rows(arrays, stage, rows, n_e, block, chunks)
     last = (((1,), (1,)), ((), ()))
     hid, kept = wd.shape
@@ -293,8 +306,6 @@
         d_gate[:, at] = (grad * slope[:, at]).astype(BF16)
         d_up[:, at] = (grad * silu[:, at]).astype(BF16)
     sources = n_e * n_t
-    for row in range(chunks * MOST, block):
-        stage[pl.ds(row, sources, stride=block), :] = jnp.zeros((sources, LANES), F32)
     dg, du = d_gate[...], d_up[...]
     width = 2 * LANES if kept % (2 * LANES) == 0 else LANES
     for i in range(kept // width):
@@ -325,72 +336,96 @@
         + [vmem((n_e * block, LANES), BF16)] * n_t,
         in_specs=[VMEM] * (n_t + 5),
         out_specs=[VMEM] * (3 + n_t),
-        scratch_shapes=[
-            pltpu.VMEM((n_t * n_e * block, LANES), F32),
-            pltpu.VMEM((SUB, LANES), F32),
-        ],
+        scratch_shapes=[pltpu.VMEM((n_t * n_e * block, LANES), F32)],
         compiler_params=params(12),
         cost_estimate=cost(6 * 4 * count * kept * hid, 6 * kept * hid),
         name="backward",
     )(*arrays, slope, silu, wg, wu, wd)
 
 
-def outer_kernel(left, *refs):
-    rights, outs = refs[: len(refs) // 2], refs[len(refs) // 2 :]
+def outer_kernel(left, *refs, count, tile, width):
+    rights, outs, token = refs[:count], refs[count : 2 * count], refs[2 * count]
+    held, sems = refs[2 * count + 1 :]
     first = (((0,), (0,)), ((), ()))
-    for right, out in zip(rights, outs):
-        out[...] = lax.dot_general(left[...], right[...], first, preferred_element_type=F32).astype(
-            BF16
-        )
-
-
-def outer(left, rights, tile, name):
-    count, m = left.shape
+    token[...] = jnp.zeros(TOKEN, F32)
+    m, n = outs[0].shape
+    moves = []
+    for i in range(m // tile):
+        rows = pl.ds(i * tile, tile)
+        for array in range(count):
+            for j in range(n // width):
+                at = slice(j * width, (j + 1) * width)
+                value = lax.dot_general(
+                    left[:, i * tile : (i + 1) * tile],
+                    rights[array][:, at],
+                    first,
+                    preferred_element_type=F32,
+                )
+                held[array, rows, at] = value.astype(BF16)
+            move = pltpu.make_async_copy(
+                held.at[array, rows], outs[array].at[rows], sems.at[array, i]
+            )
+            move.start()
+            moves.append(move)
+    for move in moves:
+        move.wait()
+
+
+def outer(left, rights, name):
+    rows, m = left.shape
     n = rights[0].shape[1]
-    tile = tile_of(m, tile)
-    return pl.pallas_call(
-        outer_kernel,
-        grid=(m // tile,),
-        out_shape=[jax.ShapeDtypeStruct((m, n), BF16)] * len(rights),
-        in_specs=[pl.BlockSpec((count, tile), lambda i: (0, i))]
-        + [pl.BlockSpec((count, n), lambda i: (0, 0))] * len(rights),
-        out_specs=[pl.BlockSpec((tile, n), lambda i: (i, 0))] * len(rights),
-        compiler_params=params(20),
-        cost_estimate=cost(2 * 256 * m * n * len(rights), 2 * m * n * len(rights)),
+    count = len(rights)
+    tile, width = tile_of(m, 256), tile_of(n, 512)
+    return pl.pallas_call(
+        functools.partial(outer_kernel, count=count, tile=tile, width=width),
+        out_shape=[jax.ShapeDtypeStruct((m, n), BF16)] * count + [vmem(TOKEN, F32)],
+        in_specs=[VMEM] * (1 + count),
+        out_specs=[ANY] * count + [VMEM],
+        scratch_shapes=[
+            pltpu.VMEM((count, m, n), BF16),
+            pltpu.SemaphoreType.DMA((count, m // tile)),
+        ],
+        compiler_params=params(28),
+        cost_estimate=cost(2 * 256 * m * n * count, 2 * m * n * count),
         name=name,
     )(left, *rights)
 
 
-def sum_kernel(*refs, n_t, n_e, block):
-    ins, outs = refs[:n_t], refs[n_t:]
+def sum_kernel(*refs, n_t, n_e, block, dense):
+    ins, (token, keep, send, stage) = refs[:n_t], refs[n_t:]
+    total = ins[0][...].astype(F32)
+    for ref in ins[1:]:
+        total = total + ref[...].astype(F32)
+    stage[: n_e * dense, :] = total
+    stage[n_e * dense :, :] = jnp.zeros((stage.shape[0] - n_e * dense, LANES), F32)
     for k in range(n_e):
-        at = slice(k * block, (k + 1) * block)
-        total = ins[0][at, :].astype(F32)
-        for ref in ins[1:]:
-            total = total + ref[at, :].astype(F32)
-        outs[k][...] = total.astype(BF16)
-
-
-def sum_parts(arrays, n_e, block):
+        out = send if k % 2 else keep
+        value = stage[k * dense : k * dense + block, :].astype(BF16)
+        out[k // 2 * block : (k // 2 + 1) * block, :] = value
+
+
+def sum_parts(arrays, token, n_e, block, dense):
     n_t = len(arrays)
     return pl.pallas_call(
-        functools.partial(sum_kernel, n_t=n_t, n_e=n_e, block=block),
-        out_shape=[vmem((block, LANES), BF16)] * n_e,
-        in_specs=[VMEM] * n_t,
-        out_specs=[VMEM] * n_e,
+        functools.partial(sum_kernel, n_t=n_t, n_e=n_e, block=block, dense=dense),
+        out_shape=[vmem((n_e // 2 * block, LANES), BF16)] * 2,
+        in_specs=[VMEM] * (n_t + 1),
+        out_specs=[VMEM] * 2,
+        scratch_shapes=[pltpu.VMEM((n_e * dense + block, LANES), F32)],
         compiler_params=params(8),
         name="sum_parts",
-    )(*arrays)
+    )(*arrays, token)
 
 
 def combine_kernel(routes, pattern, *rest, n_e, holders, chunks):
-    ins, (out, count, codes, index, stage, spread) = rest[:n_e], rest[n_e:]
+    ins, (out, count, codes, index, stage, spread) = rest[:2], rest[2:]
     experts, toks = pattern.shape[0], out.shape[0]
-    block = ins[0].shape[0]
+    block = 2 * ins[0].shape[0] // n_e
     me = lax.axis_index("expert")
     lane, _ = iotas()
-    for k in range(n_e):
-        stage[k * block : (k + 1) * block, :] = ins[k][...].astype(F32)
+    for half, ref in enumerate(ins):
+        rows = ref.shape[0]
+        stage[half * rows : (half + 1) * rows, :] = ref[...].astype(F32)
     tail = stage.shape[0] - n_e * block
     stage[n_e * block :, :] = jnp.zeros((tail, LANES), F32)
     pattern_rows(pattern, codes, chunks // 2)
@@ -428,14 +463,13 @@
         out[:, m * LANES : (m + 1) * LANES] = spread[m * SUB : (m + 1) * SUB, :].astype(BF16)
 
 
-def combine_rows(routes, pattern, arrays, toks, width, holders, chunks):
-    n_e = len(arrays)
-    block = arrays[0].shape[0]
+def combine_rows(routes, pattern, arrays, toks, width, n_e, holders, chunks):
+    block = 2 * arrays[0].shape[0] // n_e
     experts = pattern.shape[0]
     return pl.pallas_call(
         functools.partial(combine_kernel, n_e=n_e, holders=holders, chunks=chunks),
         out_shape=jax.ShapeDtypeStruct((toks, width), BF16),
-        in_specs=[SMEM, VMEM] + [VMEM] * n_e,
+        in_specs=[SMEM, VMEM] + [VMEM] * 2,
         out_specs=VMEM,
         scratch_shapes=[
             pltpu.SMEM((experts,), jnp.int32),
@@ -454,6 +488,16 @@
     return lax.ppermute(value, axis, [(i, i ^ k) for i in range(size)])
 
 
+def gather_line(value):
+    held = {0: value}
+    bit = lax.axis_size("tensor") // 2
+    while bit:
+        for k in list(held):
+            held[k ^ bit] = swap(held[k], "tensor", bit)
+        bit //= 2
+    return [held[k] for k in range(len(held))]
+
+
 def body(x_tokens, grad_values, grad_scale, combine, routes, pattern, w_gate, w_up, w_down):
     n_e = lax.axis_size("expert")
     n_t = lax.axis_size("tensor")
@@ -462,24 +506,24 @@
     toks, width = x_tokens.shape
     chunks = w_gate.shape[0] // LANES
     block = block_rows(chunks)
+    dense = chunks * MOST
 
     routes, combine = routes.T, combine.T
-    *sent, wg = dispatch(
-        routes, combine, grad_scale, pattern, x_tokens, grad_values, w_gate, n_e, holders, chunks
+    keep, send = dispatch(
+        routes, combine, grad_scale, pattern, x_tokens, grad_values, (w_gate, w_up, w_down), n_e, holders, chunks
     )
-    parts = [sent[0]] + [swap(sent[k], "expert", k) for k in range(1, n_e)]
-    wu = load_weights(w_up, sent[0])
-    zx, zg = join(parts, block)
-    all_x = [zx] + [swap(zx, "tensor", k) for k in range(1, n_t)]
-    all_g = [zg] + [swap(zg, "tensor", k) for k in range(1, n_t)]
-    rows_in, hidden, slope, silu, wd = forward(all_x, wg, wu, w_down, n_e, block, chunks)
-    rows_grad, d_gate, d_up, *back = backward(all_g, slope, silu, wg, wu, wd, n_e, block, chunks)
+    zx, zg = join(*exchange(keep, send, 2 * block), n_e, block, dense)
+    all_x, all_g = gather_line(zx), gather_line(zg)
+    rows_in, hidden, slope, silu, wg, wu = forward(all_x, w_gate, w_up, n_e, dense, chunks)
+    rows_grad, d_gate, d_up, *back = backward(
+        all_g, slope, silu, wg, wu, w_down, n_e, dense, chunks
+    )
     back = [back[0]] + [swap(back[k], "tensor", k) for k in range(1, n_t)]
-    part_gate, part_up = outer(rows_in, [d_gate, d_up], 512, "grads_in")
-    summed = sum_parts(back, n_e, block)
-    summed = [summed[0]] + [swap(summed[k], "expert", k) for k in range(1, n_e)]
-    (part_down,) = outer(hidden, [rows_grad], 1024, "grads_out")
-    grad_tokens = combine_rows(routes, pattern, summed, toks, width, holders, chunks)
+    part_gate, part_up, token = outer(rows_in, [d_gate, d_up], "grads_in")
+    keep, send = sum_parts(back, token, n_e, block, dense)
+    summed = exchange(keep, send, block)
+    part_down, _ = outer(hidden, [rows_grad], "grad_down")
+    grad_tokens = combine_rows(routes, pattern, summed, toks, width, n_e, holders, chunks)
     return grad_tokens, part_gate, part_up, part_down
 
 

time: 50.7 us -> 48.4 us (0.955)
  local copies, waits for them, and re-layouts: 2.8 us -> 0.02 us
  Pallas kernels: 23.3 us -> 21.1 us
  starting transfers between devices: 18.5 us -> 20.2 us
  waiting for transfers between devices: 5.09 us -> 6.14 us
    unnamed x8 -> x12, local copies, waits for them, and re-layouts: 2.8 us -> 0.02 us
    ppermute x15 -> x13, starting transfers between devices: 18.5 us -> 20.2 us  [swap(): return lax.ppermute(value, axis, [(i, i ^ k) for i in range(size)])]
    pallas_call x1, Pallas kernels: 2.97 us -> 1.41 us  [dispatch(): pl.pallas_call(functools.partial(dispatch_kernel, n_e=n_e, holders=holder...]
    ppermute x15 -> x13, waiting for transfers between devices: 5.09 us -> 6.14 us  [swap(): return lax.ppermute(value, axis, [(i, i ^ k) for i in range(size)])]
    pallas_call x4 -> x5, Pallas kernels: 9.67 us -> 8.88 us  [the longest x2 8.84 us: outer(): pl.pallas_call(functools.partial(outer_kernel, count=count, tile=tile, wi...]
  transfers between devices with their start and end apart: 15 -> 13, of which waited for: 4 -> 6; matrix products, arithmetic and copies ran while one was open for 0% -> 0% of each run, Pallas kernels for 25% -> 25%
where the time goes in v3:
time: 48.4 us; the launch traced here: 48.2 us
  Pallas kernels  21.1 us (44%)
  starting transfers between devices  20.2 us (42%)
  waiting for transfers between devices  6.14 us (13%)
  between operations  0.79 us (2%)
    ppermute x13, starting transfers between devices, swap(): return lax.ppermute(value, axis, [(i, i ^ k) for i in range(size)])  20.2 us
    pallas_call x2, Pallas kernels, outer(): pl.pallas_call(functools.partial(outer_kernel, count=count, tile=tile, wi...  8.84 us
    ppermute x13, waiting for transfers between devices, swap(): return lax.ppermute(value, axis, [(i, i ^ k) for i in range(size)])  6.14 us
    pallas_call x1, Pallas kernels, backward(): pl.pallas_call(functools.partial(backward_kernel, n_t=n_t, n_e=n_e, block...  5.91 us
    pallas_call x1, Pallas kernels, forward(): pl.pallas_call(functools.partial(forward_kernel, n_t=n_t, n_e=n_e, block=...  3.32 us
    pallas_call x1, Pallas kernels, combine_rows(): pl.pallas_call(functools.partial(combine_kernel, n_e=n_e, holders=holders...  1.56 us
    pallas_call x1, Pallas kernels, dispatch(): pl.pallas_call(functools.partial(dispatch_kernel, n_e=n_e, holders=holder...  1.41 us
  transfers between devices with their start and end apart: 13, of which 6 were waited for; matrix products, arithmetic and copies ran while one was open for 0% of the time, Pallas kernels for 25%

profile of v3, /device:TPU:0, one launch (start us, length us, event | category | flops | bytes accessed | tf_op | source)
XLA Modules:
  0.0 48.2 jit_solution(17311409380277929758)
XLA Ops:
  0.6 0.0 copy-start
  0.6 0.0 copy-start.1
  0.7 1.4 %dispatch.1 = (bf16[256,128]{1,0:T(8,128)(2,1)S(1)}, bf16[256,128]{1,0:T(8,128)(2,1)S(1)}) custom-call(s32[2,8]{1,0:T(2,128)} %bitcast.4, f32[2,8]{1,0:T(2,128)} %bitcast.6, f32[8]{0:T(128)} %scale_any.1, s32[4,768]{1,0:T(4,128)} %pattern.1, bf16[8,3072]{1,0:T(8,128)(2,1)} %x_any.1, bf16[8,3072]{1,0:T(8,128)(2,1)} %g_any.1, bf16[1536,2048]{1,0:T(8,128)(2,1)} %refs_4_.1, ...), custom_call_target="tpu_custom_call" | custom-call | tf_op jit(solution)/shard_map/dispatch/pallas_call | solution.py:151
  2.1 0.5 %collective-permute-start = (bf16[256,128]{1,0:T(8,128)(2,1)S(1)}, bf16[256,128]{1,0:T(8,128)(2,1)S(1)}, u32[]{:S(2)}, u32[]{:S(2)}) collective-permute-start(bf16[256,128]{1,0:T(8,128)(2,1)S(1)} %get-tuple-element.32), channel_id=1, source_target_pairs={{0,4},{4,0},{8,12},{12,8},{1,5},{5,1},{9,13},{13,9},{2,6},{6,2},{1... | collective-permute-start | bytes 196616 | tf_op jit(solution)/shard_map/ppermute | solution.py:488
  2.6 0.9 %collective-permute-done.received = bf16[256,128]{1,0:T(8,128)(2,1)S(1)} collective-permute-done((bf16[256,128]{1,0:T(8,128)(2,1)S(1)}, bf16[256,128]{1,0:T(8,128)(2,1)S(1)}, u32[]{:S(2)}, u32[]{:S(2)}) %collective-permute-start) | collective-permute-done | bytes 65568 | tf_op jit(solution)/shard_map/ppermute | solution.py:488
  3.5 2.9 %collective-permute-start.1 = (bf16[256,128]{1,0:T(8,128)(2,1)S(1)}, bf16[256,128]{1,0:T(8,128)(2,1)S(1)}, u32[]{:S(2)}, u32[]{:S(2)}) collective-permute-start(bf16[256,128]{1,0:T(8,128)(2,1)S(1)} %get-tuple-element.34), channel_id=1, source_target_pairs={{0,8},{4,12},{8,0},{12,4},{1,9},{5,13},{9,1},{13,5},{2,10},{6,14},... | collective-permute-start | bytes 196616 | tf_op jit(solution)/shard_map/ppermute | solution.py:488
  6.4 2.4 %collective-permute-done.1.received = bf16[256,128]{1,0:T(8,128)(2,1)S(1)} collective-permute-done((bf16[256,128]{1,0:T(8,128)(2,1)S(1)}, bf16[256,128]{1,0:T(8,128)(2,1)S(1)}, u32[]{:S(2)}, u32[]{:S(2)}) %collective-permute-start.1) | collective-permute-done | bytes 65568 | tf_op jit(solution)/shard_map/ppermute | solution.py:488
  8.9 3.0 %collective-permute-start.6 = (bf16[240,128]{1,0:T(8,128)(2,1)S(1)}, bf16[240,128]{1,0:T(8,128)(2,1)S(1)}, u32[]{:S(2)}, u32[]{:S(2)}) collective-permute-start(bf16[240,128]{1,0:T(8,128)(2,1)S(1)} %get-tuple-element.36.refs_0_), channel_id=1, source_target_pairs={{0,2},{1,3},{2,0},{3,1},{4,6},{5,7},{6,4},{7,5},{8,10},{9,11},{10,... | collective-permute-start | bytes 184328 | tf_op jit(solution)/shard_map/ppermute | solution.py:488
  11.9 0.0 slice-start
  11.9 0.0 slice-start.1
  11.9 0.1 collective-permute-start.3
  12.0 1.8 %collective-permute-start.5 = (bf16[240,128]{1,0:T(8,128)(2,1)S(1)}, bf16[240,128]{1,0:T(8,128)(2,1)S(1)}, u32[]{:S(2)}, u32[]{:S(2)}) collective-permute-start(bf16[240,128]{1,0:T(8,128)(2,1)S(1)} %get-tuple-element.36.refs_0_), channel_id=1, source_target_pairs={{0,1},{1,0},{2,3},{3,2},{4,5},{5,4},{6,7},{7,6},{8,9},{9,8},{10,11... | collective-permute-start | bytes 184328 | tf_op jit(solution)/shard_map/ppermute | solution.py:488
  13.8 0.5 collective-permute-done.6.refs_2_
  14.2 2.8 %collective-permute-start.7 = (bf16[240,128]{1,0:T(8,128)(2,1)S(1)}, bf16[240,128]{1,0:T(8,128)(2,1)S(1)}, u32[]{:S(2)}, u32[]{:S(2)}) collective-permute-start(bf16[240,128]{1,0:T(8,128)(2,1)S(1)} %collective-permute-done.6.refs_2_), channel_id=1, source_target_pairs={{0,1},{1,0},{2,3},{3,2},{4,5},{5,4},{6,7},{7,6},{8,9},{9,8},{10,11... | collective-permute-start | bytes 184328 | tf_op jit(solution)/shard_map/ppermute | solution.py:488
  17.1 0.0 collective-permute-start.2
  17.1 0.0 collective-permute-done.3.refs_2_
  17.1 2.0 %collective-permute-start.4 = (bf16[240,128]{1,0:T(8,128)(2,1)S(1)}, bf16[240,128]{1,0:T(8,128)(2,1)S(1)}, u32[]{:S(2)}, u32[]{:S(2)}) collective-permute-start(bf16[240,128]{1,0:T(8,128)(2,1)S(1)} %collective-permute-done.3.refs_2_), channel_id=1, source_target_pairs={{0,1},{1,0},{2,3},{3,2},{4,5},{5,4},{6,7},{7,6},{8,9},{9,8},{10,11... | collective-permute-start | bytes 184328 | tf_op jit(solution)/shard_map/ppermute | solution.py:488
  19.1 0.0 collective-permute-done.5.refs_1_
  19.1 0.3 collective-permute-done.7.refs_3_
  19.4 0.0 copy-done
  19.4 0.0 copy-done.1
  19.4 3.3 %forward.1 = (bf16[80,1536]{1,0:T(8,128)(2,1)S(1)}, bf16[80,2048]{1,0:T(8,128)(2,1)S(1)}, f32[80,2048]{1,0:T(8,128)S(1)}, f32[80,2048]{1,0:T(8,128)S(1)}, bf16[1...) custom-call(bf16[240,128]{1,0:T(8,128)(2,1)S(1)} %get-tuple-element.36.refs_0_, ...), custom_call_target="tpu_custom_call" | custom-call | flops 4026531840 | bytes 12582912 | tf_op jit(solution)/shard_map/forward/pallas_call | solution.py:274
  22.7 0.0 collective-permute-done.2.refs_1_
  22.7 0.0 collective-permute-done.4.refs_3_
  22.7 0.0 slice-done
  22.7 0.0 slice-done.1
  22.8 5.9 %backward.1 = (bf16[80,1536]{1,0:T(8,128)(2,1)S(1)}, bf16[80,2048]{1,0:T(8,128)(2,1)S(1)}, bf16[80,2048]{1,0:T(8,128)(2,1)S(1)}, bf16[240,128]{1,0:T(8,128)(2,1)...) custom-call(bf16[240,128]{1,0:T(8,128)(2,1)S(1)} %get-tuple-element.35.refs_0_, ...), custom_call_target="tpu_custom_call" | custom-call | flops 6039797760 | bytes 18874368 | tf_op jit(solution)/shard_map/backward/pallas_call | solution.py:329
  28.7 2.0 %collective-permute-start.8 = (bf16[240,128]{1,0:T(8,128)(2,1)S(1)}, bf16[240,128]{1,0:T(8,128)(2,1)S(1)}, u32[]{:S(2)}, u32[]{:S(2)}) collective-permute-start(bf16[240,128]{1,0:T(8,128)(2,1)S(1)} %get-tuple-element.42), channel_id=1, source_target_pairs={{0,1},{1,0},{2,3},{3,2},{4,5},{5,4},{6,7},{7,6},{8,9},{9,8},{10,11... | collective-permute-start | bytes 184328 | tf_op jit(solution)/shard_map/ppermute | solution.py:488
  30.6 3.4 %collective-permute-start.9 = (bf16[240,128]{1,0:T(8,128)(2,1)S(1)}, bf16[240,128]{1,0:T(8,128)(2,1)S(1)}, u32[]{:S(2)}, u32[]{:S(2)}) collective-permute-start(bf16[240,128]{1,0:T(8,128)(2,1)S(1)} %get-tuple-element.43), channel_id=1, source_target_pairs={{0,2},{1,3},{2,0},{3,1},{4,6},{5,7},{6,4},{7,5},{8,10},{9,11},{10,... | collective-permute-start | bytes 184328 | tf_op jit(solution)/shard_map/ppermute | solution.py:488
  34.1 0.0 collective-permute-start.10
  34.1 0.0 copy-start.2
  34.1 0.0 copy-start.3
  34.1 5.1 %grads_in.1 = (bf16[1536,2048]{1,0:T(8,128)(2,1)}, bf16[1536,2048]{1,0:T(8,128)(2,1)}, f32[8,128]{1,0:T(8,128)S(1)}) custom-call(bf16[80,1536]{1,0:T(8,128)(2,1)S(1)} %get-tuple-element.45.left, bf16[80,2048]{1,0:T(8,128)(2,1)S(1)} %get-tuple-element.46.refs_0_, bf16[80,2048]{1,0:T(8,128)(2,1)S(1)} %get-tuple-element.47.refs_1_), custom_call_target="tpu_custom_call" | custom-call | flops 3221225472 | bytes 12582912 | tf_op jit(solution)/shard_map/grads_in/pallas_call | solution.py:379
  39.2 0.0 collective-permute-done.8.refs_1_
  39.2 0.0 collective-permute-done.9.refs_2_
  39.2 0.9 %collective-permute-done.10.refs_3_ = bf16[240,128]{1,0:T(8,128)(2,1)S(1)} collective-permute-done((bf16[240,128]{1,0:T(8,128)(2,1)S(1)}, bf16[240,128]{1,0:T(8,128)(2,1)S(1)}, u32[]{:S(2)}, u32[]{:S(2)}) %collective-permute-start.10) | collective-permute-done | bytes 61472 | tf_op jit(solution)/shard_map/ppermute | solution.py:488
  40.1 0.1 collective-permute-start.11
  40.2 1.2 %collective-permute-done.11.received = bf16[128,128]{1,0:T(8,128)(2,1)S(1)} collective-permute-done((bf16[128,128]{1,0:T(8,128)(2,1)S(1)}, bf16[128,128]{1,0:T(8,128)(2,1)S(1)}, u32[]{:S(2)}, u32[]{:S(2)}) %collective-permute-start.11) | collective-permute-done | bytes 32800 | tf_op jit(solution)/shard_map/ppermute | solution.py:488
  41.4 1.5 %collective-permute-start.12 = (bf16[128,128]{1,0:T(8,128)(2,1)S(1)}, bf16[128,128]{1,0:T(8,128)(2,1)S(1)}, u32[]{:S(2)}, u32[]{:S(2)}) collective-permute-start(bf16[128,128]{1,0:T(8,128)(2,1)S(1)} %get-tuple-element.52), channel_id=1, source_target_pairs={{0,8},{4,12},{8,0},{12,4},{1,9},{5,13},{9,1},{13,5},{2,10},{6,14},... | collective-permute-start | bytes 98312 | tf_op jit(solution)/shard_map/ppermute | solution.py:488
  42.9 3.7 %grad_down.1 = (bf16[2048,1536]{1,0:T(8,128)(2,1)}, f32[8,128]{1,0:T(8,128)}) custom-call(bf16[80,2048]{1,0:T(8,128)(2,1)S(1)} %get-tuple-element.55.left, bf16[80,1536]{1,0:T(8,128)(2,1)S(1)} %get-tuple-element.56.refs_0_), custom_call_target="tpu_custom_call" | custom-call | flops 1610612736 | bytes 6291456 | tf_op jit(solution)/shard_map/grad_down/pallas_call | solution.py:379
  46.7 0.0 collective-permute-done.12.rest_1_
  46.7 0.0 copy-done.2
  46.7 0.0 copy-done.3
  46.7 1.6 %combine_rows.1 = bf16[8,3072]{1,0:T(8,128)(2,1)} custom-call(s32[2,8]{1,0:T(2,128)S(1)} %bitcast.5, s32[4,768]{1,0:T(4,128)S(1)} %copy-done.2, bf16[128,128]{1,0:T(8,128)(2,1)S(1)} %get-tuple-element.51.rest_0_, bf16[128,128]{1,0:T(8,128)(2,1)S(1)} %collective-permute-done.12.rest_1_), custom_call_target="tpu_custom_call" | custom-call | tf_op jit(solution)/shard_map/combine_rows/pallas_call | solution.py:469
  (5 shorter events, 0.1 us)
Async XLA Ops:
  0.6 18.7 %copy-start = (bf16[1536,2048]{1,0:T(8,128)(2,1)S(1)}, bf16[1536,2048]{1,0:T(8,128)(2,1)}, u32[]{:S(2)}) copy-start(bf16[1536,2048]{1,0:T(8,128)(2,1)} %refs_4_.1) | copy-start | bytes 18874372
  0.6 18.7 %copy-start.1 = (bf16[1536,2048]{1,0:T(8,128)(2,1)S(1)}, bf16[1536,2048]{1,0:T(8,128)(2,1)}, u32[]{:S(2)}) copy-start(bf16[1536,2048]{1,0:T(8,128)(2,1)} %refs_5_.1) | copy-start | bytes 18874372
  2.1 1.4 %collective-permute-start = (bf16[256,128]{1,0:T(8,128)(2,1)S(1)}, bf16[256,128]{1,0:T(8,128)(2,1)S(1)}, u32[]{:S(2)}, u32[]{:S(2)}) collective-permute-start(bf16[256,128]{1,0:T(8,128)(2,1)S(1)} %get-tuple-element.32), channel_id=1, source_target_pairs={{0,4},{4,0},{8,12},{12,8},{1,5},{5,1},{9,13},{13,9},{2,6},{6,2},{1... | collective-permute-start | bytes 196616 | tf_op jit(solution)/shard_map/ppermute | solution.py:488
  3.5 5.3 %collective-permute-start.1 = (bf16[256,128]{1,0:T(8,128)(2,1)S(1)}, bf16[256,128]{1,0:T(8,128)(2,1)S(1)}, u32[]{:S(2)}, u32[]{:S(2)}) collective-permute-start(bf16[256,128]{1,0:T(8,128)(2,1)S(1)} %get-tuple-element.34), channel_id=1, source_target_pairs={{0,8},{4,12},{8,0},{12,4},{1,9},{5,13},{9,1},{13,5},{2,10},{6,14},... | collective-permute-start | bytes 196616 | tf_op jit(solution)/shard_map/ppermute | solution.py:488
  8.9 5.4 %collective-permute-start.6 = (bf16[240,128]{1,0:T(8,128)(2,1)S(1)}, bf16[240,128]{1,0:T(8,128)(2,1)S(1)}, u32[]{:S(2)}, u32[]{:S(2)}) collective-permute-start(bf16[240,128]{1,0:T(8,128)(2,1)S(1)} %get-tuple-element.36.refs_0_), channel_id=1, source_target_pairs={{0,2},{1,3},{2,0},{3,1},{4,6},{5,7},{6,4},{7,5},{8,10},{9,11},{10,... | collective-permute-start | bytes 184328 | tf_op jit(solution)/shard_map/ppermute | solution.py:488
  11.9 10.9 %slice-start = ((s8[6291456]{0:T(1024)(128)(4,1)}), s8[4194304]{0:T(1024)(128)(4,1)S(1)}, s32[]{:S(2)}) async-start(s8[6291456]{0:T(1024)(128)(4,1)} %bitcast.2), calls=%async_computation | async-start | bytes 8388608
  11.9 10.9 %slice-start.1 = ((s8[6291456]{0:T(1024)(128)(4,1)}), s8[2097152]{0:T(1024)(128)(4,1)S(1)}, s32[]{:S(2)}) async-start(s8[6291456]{0:T(1024)(128)(4,1)} %bitcast.2), calls=%async_computation.1 | async-start | bytes 4194304
  11.9 5.2 %collective-permute-start.3 = (bf16[240,128]{1,0:T(8,128)(2,1)S(1)}, bf16[240,128]{1,0:T(8,128)(2,1)S(1)}, u32[]{:S(2)}, u32[]{:S(2)}) collective-permute-start(bf16[240,128]{1,0:T(8,128)(2,1)S(1)} %get-tuple-element.35.refs_0_), channel_id=1, source_target_pairs={{0,2},{1,3},{2,0},{3,1},{4,6},{5,7},{6,4},{7,5},{8,10},{9,11},{10,... | collective-permute-start | bytes 184328 | tf_op jit(solution)/shard_map/ppermute | solution.py:488
  12.0 7.1 %collective-permute-start.5 = (bf16[240,128]{1,0:T(8,128)(2,1)S(1)}, bf16[240,128]{1,0:T(8,128)(2,1)S(1)}, u32[]{:S(2)}, u32[]{:S(2)}) collective-permute-start(bf16[240,128]{1,0:T(8,128)(2,1)S(1)} %get-tuple-element.36.refs_0_), channel_id=1, source_target_pairs={{0,1},{1,0},{2,3},{3,2},{4,5},{5,4},{6,7},{7,6},{8,9},{9,8},{10,11... | collective-permute-start | bytes 184328 | tf_op jit(solution)/shard_map/ppermute | solution.py:488
  14.2 5.1 %collective-permute-start.7 = (bf16[240,128]{1,0:T(8,128)(2,1)S(1)}, bf16[240,128]{1,0:T(8,128)(2,1)S(1)}, u32[]{:S(2)}, u32[]{:S(2)}) collective-permute-start(bf16[240,128]{1,0:T(8,128)(2,1)S(1)} %collective-permute-done.6.refs_2_), channel_id=1, source_target_pairs={{0,1},{1,0},{2,3},{3,2},{4,5},{5,4},{6,7},{7,6},{8,9},{9,8},{10,11... | collective-permute-start | bytes 184328 | tf_op jit(solution)/shard_map/ppermute | solution.py:488
  17.1 5.7 %collective-permute-start.2 = (bf16[240,128]{1,0:T(8,128)(2,1)S(1)}, bf16[240,128]{1,0:T(8,128)(2,1)S(1)}, u32[]{:S(2)}, u32[]{:S(2)}) collective-permute-start(bf16[240,128]{1,0:T(8,128)(2,1)S(1)} %get-tuple-element.35.refs_0_), channel_id=1, source_target_pairs={{0,1},{1,0},{2,3},{3,2},{4,5},{5,4},{6,7},{7,6},{8,9},{9,8},{10,11... | collective-permute-start | bytes 184328 | tf_op jit(solution)/shard_map/ppermute | solution.py:488
  17.1 5.6 %collective-permute-start.4 = (bf16[240,128]{1,0:T(8,128)(2,1)S(1)}, bf16[240,128]{1,0:T(8,128)(2,1)S(1)}, u32[]{:S(2)}, u32[]{:S(2)}) collective-permute-start(bf16[240,128]{1,0:T(8,128)(2,1)S(1)} %collective-permute-done.3.refs_2_), channel_id=1, source_target_pairs={{0,1},{1,0},{2,3},{3,2},{4,5},{5,4},{6,7},{7,6},{8,9},{9,8},{10,11... | collective-permute-start | bytes 184328 | tf_op jit(solution)/shard_map/ppermute | solution.py:488
  28.7 10.5 %collective-permute-start.8 = (bf16[240,128]{1,0:T(8,128)(2,1)S(1)}, bf16[240,128]{1,0:T(8,128)(2,1)S(1)}, u32[]{:S(2)}, u32[]{:S(2)}) collective-permute-start(bf16[240,128]{1,0:T(8,128)(2,1)S(1)} %get-tuple-element.42), channel_id=1, source_target_pairs={{0,1},{1,0},{2,3},{3,2},{4,5},{5,4},{6,7},{7,6},{8,9},{9,8},{10,11... | collective-permute-start | bytes 184328 | tf_op jit(solution)/shard_map/ppermute | solution.py:488
  30.6 8.6 %collective-permute-start.9 = (bf16[240,128]{1,0:T(8,128)(2,1)S(1)}, bf16[240,128]{1,0:T(8,128)(2,1)S(1)}, u32[]{:S(2)}, u32[]{:S(2)}) collective-permute-start(bf16[240,128]{1,0:T(8,128)(2,1)S(1)} %get-tuple-element.43), channel_id=1, source_target_pairs={{0,2},{1,3},{2,0},{3,1},{4,6},{5,7},{6,4},{7,5},{8,10},{9,11},{10,... | collective-permute-start | bytes 184328 | tf_op jit(solution)/shard_map/ppermute | solution.py:488
  34.1 6.0 %collective-permute-start.10 = (bf16[240,128]{1,0:T(8,128)(2,1)S(1)}, bf16[240,128]{1,0:T(8,128)(2,1)S(1)}, u32[]{:S(2)}, u32[]{:S(2)}) collective-permute-start(bf16[240,128]{1,0:T(8,128)(2,1)S(1)} %get-tuple-element.44), channel_id=1, source_target_pairs={{0,3},{1,2},{2,1},{3,0},{4,7},{5,6},{6,5},{7,4},{8,11},{9,10},{10,... | collective-permute-start | bytes 184328 | tf_op jit(solution)/shard_map/ppermute | solution.py:488
  34.1 12.6 %copy-start.2 = (s32[4,768]{1,0:T(4,128)S(1)}, s32[4,768]{1,0:T(4,128)}, u32[]{:S(2)}) copy-start(s32[4,768]{1,0:T(4,128)} %pattern.1) | copy-start | bytes 36868
  34.1 12.6 %copy-start.3 = (s32[8,2]{0,1:T(2,128)S(1)}, s32[8,2]{0,1:T(2,128)}, u32[]{:S(2)}) copy-start(s32[8,2]{0,1:T(2,128)} %param.13) | copy-start | bytes 196
  40.1 1.3 %collective-permute-start.11 = (bf16[128,128]{1,0:T(8,128)(2,1)S(1)}, bf16[128,128]{1,0:T(8,128)(2,1)S(1)}, u32[]{:S(2)}, u32[]{:S(2)}) collective-permute-start(bf16[128,128]{1,0:T(8,128)(2,1)S(1)} %get-tuple-element.50), channel_id=1, source_target_pairs={{0,4},{4,0},{8,12},{12,8},{1,5},{5,1},{9,13},{13,9},{2,6},{6,2},{1... | collective-permute-start | bytes 98312 | tf_op jit(solution)/shard_map/ppermute | solution.py:488
  41.4 5.2 %collective-permute-start.12 = (bf16[128,128]{1,0:T(8,128)(2,1)S(1)}, bf16[128,128]{1,0:T(8,128)(2,1)S(1)}, u32[]{:S(2)}, u32[]{:S(2)}) collective-permute-start(bf16[128,128]{1,0:T(8,128)(2,1)S(1)} %get-tuple-element.52), channel_id=1, source_target_pairs={{0,8},{4,12},{8,0},{12,4},{1,9},{5,13},{9,1},{13,5},{2,10},{6,14},... | collective-permute-start | bytes 98312 | tf_op jit(solution)/shard_map/ppermute | solution.py:488

commit v4 on v3

--- a/solution.py
+++ b/solution.py
@@ -203,35 +203,32 @@
         bit *= 2
 
 
-def join_kernel(keep, received, zx, zg, stage, *, n_e, block, dense):
-    for array, out in enumerate((zx, zg)):
-        for k in range(n_e):
-            half, at = divmod(k, n_e // 2)
-            at = (2 * at + array) * block
-            source = (keep, received)[half]
-            stage[k * dense : k * dense + block, :] = source[at : at + block, :].astype(F32)
-        out[...] = stage[: n_e * dense, :].astype(BF16)
-
-
-def join(keep, received, n_e, block, dense):
-    return pl.pallas_call(
-        functools.partial(join_kernel, n_e=n_e, block=block, dense=dense),
-        out_shape=[vmem((n_e * dense, LANES), BF16)] * 2,
-        in_specs=[VMEM] * 2,
-        out_specs=[VMEM] * 2,
-        scratch_shapes=[pltpu.VMEM((n_e * dense + block, LANES), F32)],
+def join_kernel(blocks, out, stage, *, block, dense):
+    count = blocks.shape[0] // (2 * block)
+    for array in range(2):
+        for k in range(count):
+            at, to = (2 * k + array) * block, (array * count + k) * dense
+            stage[to : to + block, :] = blocks[at : at + block, :].astype(F32)
+    out[...] = stage[: 2 * count * dense, :].astype(BF16)
+
+
+def join(blocks, block, dense):
+    rows = blocks.shape[0] // block * dense
+    return pl.pallas_call(
+        functools.partial(join_kernel, block=block, dense=dense),
+        out_shape=vmem((rows, LANES), BF16),
+        in_specs=[VMEM],
+        out_specs=VMEM,
+        scratch_shapes=[pltpu.VMEM((rows + block, LANES), F32)],
         compiler_params=params(8),
         name="join",
-    )(keep, received)
-
-
-def unpack_rows(arrays, stage, rows_ref, n_e, block, chunks):
-    sources = n_e * len(arrays)
-    for i, ref in enumerate(arrays):
-        stage[i * n_e * block : (i + 1) * n_e * block, :] = ref[...].astype(F32)
+    )(blocks)
+
+
+def unpack_rows(stage, rows_ref, sources, dense, chunks):
     for c in range(chunks):
         for slot in range(MOST):
-            picked = stage[pl.ds(c * MOST + slot, sources, stride=block), :]
+            picked = stage[pl.ds(c * MOST + slot, sources, stride=dense), :]
             rows_ref[slot * sources : (slot + 1) * sources, c * LANES : (c + 1) * LANES] = (
                 picked.astype(BF16)
             )
@@ -241,71 +238,32 @@
     return min(size, most)
 
 
-def forward_kernel(*refs, n_t, n_e, block, chunks):
-    arrays, refs = refs[:n_t], refs[n_t:]
-    (wg, wu), (rows, hidden, slope, silu_out), held = refs[:2], refs[2:6], refs[6:8]
-    stage, sems = refs[8:]
-    loads = []
-    for i, (source, target) in enumerate(zip((wg, wu), held)):
-        loads += row_copies(source, target, sems.at[i])
-    for load in loads:
-        load.start()
-    unpack_rows(arrays, stage, rows, n_e, block, chunks)
-    x = rows[...]
-    hid = wg.shape[1]
+def expert_kernel(*refs, n_t, n_e, dense, chunks):
+    near, far, (wg, wu, wd), refs = refs[:n_t], refs[n_t : 2 * n_t], refs[2 * n_t :][:3], refs[2 * n_t + 3 :]
+    (rows_in, rows_grad, hidden, d_gate, d_up), outs, (x_stage, g_stage) = refs[:5], refs[5:-2], refs[-2:]
+    sources, size = n_e * n_t, n_e // 2 * dense
+    for part, arrays in enumerate((near, far)):
+        for k, ref in enumerate(arrays):
+            value = ref[...].astype(F32)
+            at = (2 * k + part) * size
+            x_stage[at : at + size, :] = value[:size]
+            g_stage[at : at + size, :] = value[size:]
+    unpack_rows(x_stage, rows_in, sources, dense, chunks)
+    unpack_rows(g_stage, rows_grad, sources, dense, chunks)
+    last = (((1,), (1,)), ((), ()))
+    hid, kept = wd.shape
     tile = tile_of(hid, 256)
+    x, g = rows_in[...], rows_grad[...]
     for i in range(hid // tile):
         at = slice(i * tile, (i + 1) * tile)
         gate = jnp.dot(x, wg[:, at], preferred_element_type=F32)
         up = jnp.dot(x, wu[:, at], preferred_element_type=F32)
+        grad = lax.dot_general(g, wd[at, :], last, preferred_element_type=F32)
         sig = jax.nn.sigmoid(gate)
         silu = gate * sig
         hidden[:, at] = (silu * up).astype(BF16)
-        slope[:, at] = up * sig * (1.0 + gate * (1.0 - sig))
-        silu_out[:, at] = silu
-    for load in loads:
-        load.wait()
-
-
-def forward(arrays, wg, wu, n_e, block, chunks):
-    n_t = len(arrays)
-    count = MOST * n_e * n_t
-    kept, hid = wg.shape
-    return pl.pallas_call(
-        functools.partial(forward_kernel, n_t=n_t, n_e=n_e, block=block, chunks=chunks),
-        out_shape=[
-            vmem((count, kept), BF16),
-            vmem((count, hid), BF16),
-            vmem((count, hid), F32),
-            vmem((count, hid), F32),
-            *(vmem(w.shape, w.dtype) for w in (wg, wu)),
-        ],
-        in_specs=[VMEM] * (n_t + 2),
-        out_specs=[VMEM] * 6,
-        scratch_shapes=[
-            pltpu.VMEM((n_t * n_e * block, LANES), F32),
-            pltpu.SemaphoreType.DMA((2, PIECES)),
-        ],
-        compiler_params=params(12),
-        cost_estimate=cost(4 * 4 * count * kept * hid, 4 * kept * hid),
-        name="forward",
-    )(*arrays, wg, wu)
-
-
-def backward_kernel(*refs, n_t, n_e, block, chunks):
-    arrays, (slope, silu, wg, wu, wd), rest = refs[:n_t], refs[n_t : n_t + 5], refs[n_t + 5 :]
-    (rows, d_gate, d_up), outs, stage = rest[:3], rest[3 : 3 + n_t], rest[3 + n_t]
-    unpack_rows(arrays, stage, rows, n_e, block, chunks)
-    last = (((1,), (1,)), ((), ()))
-    hid, kept = wd.shape
-    tile = tile_of(hid, 256)
-    g = rows[...]
-    for i in range(hid // tile):
-        at = slice(i * tile, (i + 1) * tile)
-        grad = lax.dot_general(g, wd[at, :], last, preferred_element_type=F32)
-        d_gate[:, at] = (grad * slope[:, at]).astype(BF16)
-        d_up[:, at] = (grad * silu[:, at]).astype(BF16)
-    sources = n_e * n_t
+        d_gate[:, at] = (grad * up * sig * (1.0 + gate * (1.0 - sig))).astype(BF16)
+        d_up[:, at] = (grad * silu).astype(BF16)
     dg, du = d_gate[...], d_up[...]
     width = 2 * LANES if kept % (2 * LANES) == 0 else LANES
     for i in range(kept // width):
@@ -315,32 +273,29 @@
         for half in range(width // LANES):
             c = i * (width // LANES) + half
             for slot in range(MOST):
-                stage[pl.ds(c * MOST + slot, sources, stride=block), :] = back[
+                x_stage[pl.ds(c * MOST + slot, sources, stride=dense), :] = back[
                     slot * sources : (slot + 1) * sources, half * LANES : (half + 1) * LANES
                 ]
-    for i in range(n_t):
-        outs[i][...] = stage[i * n_e * block : (i + 1) * n_e * block, :].astype(BF16)
-
-
-def backward(arrays, slope, silu, wg, wu, wd, n_e, block, chunks):
-    n_t = len(arrays)
+    for k in range(n_t):
+        outs[k][...] = x_stage[2 * k * size : 2 * (k + 1) * size, :].astype(BF16)
+
+
+def expert_rows(near, far, wg, wu, wd, n_e, dense, chunks):
+    n_t = len(near)
     count = MOST * n_e * n_t
     kept, hid = wg.shape
     return pl.pallas_call(
-        functools.partial(backward_kernel, n_t=n_t, n_e=n_e, block=block, chunks=chunks),
-        out_shape=[
-            vmem((count, kept), BF16),
-            vmem((count, hid), BF16),
-            vmem((count, hid), BF16),
-        ]
-        + [vmem((n_e * block, LANES), BF16)] * n_t,
-        in_specs=[VMEM] * (n_t + 5),
-        out_specs=[VMEM] * (3 + n_t),
-        scratch_shapes=[pltpu.VMEM((n_t * n_e * block, LANES), F32)],
-        compiler_params=params(12),
-        cost_estimate=cost(6 * 4 * count * kept * hid, 6 * kept * hid),
-        name="backward",
-    )(*arrays, slope, silu, wg, wu, wd)
+        functools.partial(expert_kernel, n_t=n_t, n_e=n_e, dense=dense, chunks=chunks),
+        out_shape=[vmem((count, kept), BF16)] * 2
+        + [vmem((count, hid), BF16)] * 3
+        + [vmem((n_e * dense, LANES), BF16)] * n_t,
+        in_specs=[VMEM] * (2 * n_t + 3),
+        out_specs=[VMEM] * (5 + n_t),
+        scratch_shapes=[pltpu.VMEM((n_t * n_e * dense, LANES), F32)] * 2,
+        compiler_params=params(20),
+        cost_estimate=cost(10 * 4 * count * kept * hid, 6 * kept * hid),
+        name="expert_rows",
+    )(*near, *far, wg, wu, wd)
 
 
 def outer_kernel(left, *refs, count, tile, width):
@@ -512,11 +467,9 @@
     keep, send = dispatch(
         routes, combine, grad_scale, pattern, x_tokens, grad_values, (w_gate, w_up, w_down), n_e, holders, chunks
     )
-    zx, zg = join(*exchange(keep, send, 2 * block), n_e, block, dense)
-    all_x, all_g = gather_line(zx), gather_line(zg)
-    rows_in, hidden, slope, silu, wg, wu = forward(all_x, w_gate, w_up, n_e, dense, chunks)
-    rows_grad, d_gate, d_up, *back = backward(
-        all_g, slope, silu, wg, wu, w_down, n_e, dense, chunks
+    near, far = (gather_line(join(b, block, dense)) for b in exchange(keep, send, 2 * block))
+    rows_in, rows_grad, hidden, d_gate, d_up, *back = expert_rows(
+        near, far, w_gate, w_up, w_down, n_e, dense, chunks
     )
     back = [back[0]] + [swap(back[k], "tensor", k) for k in range(1, n_t)]
     part_gate, part_up, token = outer(rows_in, [d_gate, d_up], "grads_in")

time: 48.4 us -> 45.5 us (0.940)
  Pallas kernels: 21.1 us -> 19.8 us
  starting transfers between devices: 20.2 us -> 19.2 us
  waiting for transfers between devices: 6.14 us -> 5.56 us
    pallas_call x3, Pallas kernels: 9.26 us -> 7.93 us  [the longest x1 7.9 us: expert_rows(): pl.pallas_call(functools.partial(expert_kernel, n_t=n_t, n_e=n_e, dense=d...]
    ppermute x13, starting transfers between devices: 20.2 us -> 19.2 us  [swap(): return lax.ppermute(value, axis, [(i, i ^ k) for i in range(size)])]
    ppermute x13, waiting for transfers between devices: 6.14 us -> 5.56 us  [swap(): return lax.ppermute(value, axis, [(i, i ^ k) for i in range(size)])]
  transfers between devices with their start and end apart: 13 -> 13, of which waited for: 6 -> 6; matrix products, arithmetic and copies ran while one was open for 0% -> 0% of each run, Pallas kernels for 25% -> 20%
where the time goes in v4:
time: 45.5 us; the launch traced here: 45.4 us
  Pallas kernels  19.8 us (44%)
  starting transfers between devices  19.2 us (42%)
  waiting for transfers between devices  5.56 us (12%)
  between operations  0.77 us (2%)
    ppermute x13, starting transfers between devices, swap(): return lax.ppermute(value, axis, [(i, i ^ k) for i in range(size)])  19.2 us
    pallas_call x2, Pallas kernels, outer(): pl.pallas_call(functools.partial(outer_kernel, count=count, tile=tile, wi...  8.84 us
    pallas_call x1, Pallas kernels, expert_rows(): pl.pallas_call(functools.partial(expert_kernel, n_t=n_t, n_e=n_e, dense=d...  7.9 us
    ppermute x13, waiting for transfers between devices, swap(): return lax.ppermute(value, axis, [(i, i ^ k) for i in range(size)])  5.56 us
    pallas_call x1, Pallas kernels, combine_rows(): pl.pallas_call(functools.partial(combine_kernel, n_e=n_e, holders=holders...  1.55 us
    pallas_call x1, Pallas kernels, dispatch(): pl.pallas_call(functools.partial(dispatch_kernel, n_e=n_e, holders=holder...  1.4 us
  transfers between devices with their start and end apart: 13, of which 6 were waited for; matrix products, arithmetic and copies ran while one was open for 0% of the time, Pallas kernels for 20%

profile of v4, /device:TPU:0, one launch (start us, length us, event | category | flops | bytes accessed | tf_op | source)
XLA Modules:
  0.0 45.4 jit_solution(8761897380798655797)
XLA Ops:
  0.6 0.0 copy-start
  0.6 0.0 copy-start.1
  0.7 0.0 copy-start.2
  0.7 1.4 %dispatch.1 = (bf16[256,128]{1,0:T(8,128)(2,1)S(1)}, bf16[256,128]{1,0:T(8,128)(2,1)S(1)}) custom-call(s32[2,8]{1,0:T(2,128)} %bitcast.2, f32[2,8]{1,0:T(2,128)} %bitcast.4, f32[8]{0:T(128)} %scale_any.1, s32[4,768]{1,0:T(4,128)} %pattern.1, bf16[8,3072]{1,0:T(8,128)(2,1)} %x_any.1, bf16[8,3072]{1,0:T(8,128)(2,1)} %g_any.1, bf16[1536,2048]{1,0:T(8,128)(2,1)} %refs_8_.1, ...), custom_call_target="tpu_custom_call" | custom-call | tf_op jit(solution)/shard_map/dispatch/pallas_call | solution.py:151
  2.1 0.5 %collective-permute-start = (bf16[256,128]{1,0:T(8,128)(2,1)S(1)}, bf16[256,128]{1,0:T(8,128)(2,1)S(1)}, u32[]{:S(2)}, u32[]{:S(2)}) collective-permute-start(bf16[256,128]{1,0:T(8,128)(2,1)S(1)} %get-tuple-element.26), channel_id=1, source_target_pairs={{0,4},{4,0},{8,12},{12,8},{1,5},{5,1},{9,13},{13,9},{2,6},{6,2},{1... | collective-permute-start | bytes 196616 | tf_op jit(solution)/shard_map/ppermute | solution.py:443
  2.6 0.9 %collective-permute-done.received = bf16[256,128]{1,0:T(8,128)(2,1)S(1)} collective-permute-done((bf16[256,128]{1,0:T(8,128)(2,1)S(1)}, bf16[256,128]{1,0:T(8,128)(2,1)S(1)}, u32[]{:S(2)}, u32[]{:S(2)}) %collective-permute-start) | collective-permute-done | bytes 65568 | tf_op jit(solution)/shard_map/ppermute | solution.py:443
  3.5 2.9 %collective-permute-start.4 = (bf16[256,128]{1,0:T(8,128)(2,1)S(1)}, bf16[256,128]{1,0:T(8,128)(2,1)S(1)}, u32[]{:S(2)}, u32[]{:S(2)}) collective-permute-start(bf16[256,128]{1,0:T(8,128)(2,1)S(1)} %get-tuple-element.28), channel_id=1, source_target_pairs={{0,8},{4,12},{8,0},{12,4},{1,9},{5,13},{9,1},{13,5},{2,10},{6,14},... | collective-permute-start | bytes 196616 | tf_op jit(solution)/shard_map/ppermute | solution.py:443
  6.5 2.7 %collective-permute-start.2 = (bf16[240,128]{1,0:T(8,128)(2,1)S(1)}, bf16[240,128]{1,0:T(8,128)(2,1)S(1)}, u32[]{:S(2)}, u32[]{:S(2)}) collective-permute-start(bf16[240,128]{1,0:T(8,128)(2,1)S(1)} %join.2.refs_0_), channel_id=1, source_target_pairs={{0,2},{1,3},{2,0},{3,1},{4,6},{5,7},{6,4},{7,5},{8,10},{9,11},{10,... | collective-permute-start | bytes 184328 | tf_op jit(solution)/shard_map/ppermute | solution.py:443
  9.1 0.0 collective-permute-done.4.blocks
  9.1 2.7 %collective-permute-start.6 = (bf16[240,128]{1,0:T(8,128)(2,1)S(1)}, bf16[240,128]{1,0:T(8,128)(2,1)S(1)}, u32[]{:S(2)}, u32[]{:S(2)}) collective-permute-start(bf16[240,128]{1,0:T(8,128)(2,1)S(1)} %join.3.refs_4_), channel_id=1, source_target_pairs={{0,2},{1,3},{2,0},{3,1},{4,6},{5,7},{6,4},{7,5},{8,10},{9,11},{10,... | collective-permute-start | bytes 184328 | tf_op jit(solution)/shard_map/ppermute | solution.py:443
  11.9 1.6 %collective-permute-start.1 = (bf16[240,128]{1,0:T(8,128)(2,1)S(1)}, bf16[240,128]{1,0:T(8,128)(2,1)S(1)}, u32[]{:S(2)}, u32[]{:S(2)}) collective-permute-start(bf16[240,128]{1,0:T(8,128)(2,1)S(1)} %join.2.refs_0_), channel_id=1, source_target_pairs={{0,1},{1,0},{2,3},{3,2},{4,5},{5,4},{6,7},{7,6},{8,9},{9,8},{10,11... | collective-permute-start | bytes 184328 | tf_op jit(solution)/shard_map/ppermute | solution.py:443
  13.4 0.0 collective-permute-done.2.refs_2_
  13.4 0.9 %collective-permute-start.3 = (bf16[240,128]{1,0:T(8,128)(2,1)S(1)}, bf16[240,128]{1,0:T(8,128)(2,1)S(1)}, u32[]{:S(2)}, u32[]{:S(2)}) collective-permute-start(bf16[240,128]{1,0:T(8,128)(2,1)S(1)} %collective-permute-done.2.refs_2_), channel_id=1, source_target_pairs={{0,1},{1,0},{2,3},{3,2},{4,5},{5,4},{6,7},{7,6},{8,9},{9,8},{10,11... | collective-permute-start | bytes 184328 | tf_op jit(solution)/shard_map/ppermute | solution.py:443
  14.3 1.2 %collective-permute-start.5 = (bf16[240,128]{1,0:T(8,128)(2,1)S(1)}, bf16[240,128]{1,0:T(8,128)(2,1)S(1)}, u32[]{:S(2)}, u32[]{:S(2)}) collective-permute-start(bf16[240,128]{1,0:T(8,128)(2,1)S(1)} %join.3.refs_4_), channel_id=1, source_target_pairs={{0,1},{1,0},{2,3},{3,2},{4,5},{5,4},{6,7},{7,6},{8,9},{9,8},{10,11... | collective-permute-start | bytes 184328 | tf_op jit(solution)/shard_map/ppermute | solution.py:443
  15.5 0.0 collective-permute-done.6.refs_6_
  15.5 0.8 %collective-permute-start.7 = (bf16[240,128]{1,0:T(8,128)(2,1)S(1)}, bf16[240,128]{1,0:T(8,128)(2,1)S(1)}, u32[]{:S(2)}, u32[]{:S(2)}) collective-permute-start(bf16[240,128]{1,0:T(8,128)(2,1)S(1)} %collective-permute-done.6.refs_6_), channel_id=1, source_target_pairs={{0,1},{1,0},{2,3},{3,2},{4,5},{5,4},{6,7},{7,6},{8,9},{9,8},{10,11... | collective-permute-start | bytes 184328 | tf_op jit(solution)/shard_map/ppermute | solution.py:443
  16.3 0.4 collective-permute-done.1.refs_1_
  16.7 1.6 %collective-permute-done.3.refs_3_ = bf16[240,128]{1,0:T(8,128)(2,1)S(1)} collective-permute-done((bf16[240,128]{1,0:T(8,128)(2,1)S(1)}, bf16[240,128]{1,0:T(8,128)(2,1)S(1)}, u32[]{:S(2)}, u32[]{:S(2)}) %collective-permute-start.3) | collective-permute-done | bytes 61472 | tf_op jit(solution)/shard_map/ppermute | solution.py:443
  18.3 0.7 %collective-permute-done.5.refs_5_ = bf16[240,128]{1,0:T(8,128)(2,1)S(1)} collective-permute-done((bf16[240,128]{1,0:T(8,128)(2,1)S(1)}, bf16[240,128]{1,0:T(8,128)(2,1)S(1)}, u32[]{:S(2)}, u32[]{:S(2)}) %collective-permute-start.5) | collective-permute-done | bytes 61472 | tf_op jit(solution)/shard_map/ppermute | solution.py:443
  19.0 0.8 %collective-permute-done.7.refs_7_ = bf16[240,128]{1,0:T(8,128)(2,1)S(1)} collective-permute-done((bf16[240,128]{1,0:T(8,128)(2,1)S(1)}, bf16[240,128]{1,0:T(8,128)(2,1)S(1)}, u32[]{:S(2)}, u32[]{:S(2)}) %collective-permute-start.7) | collective-permute-done | bytes 61472 | tf_op jit(solution)/shard_map/ppermute | solution.py:443
  19.7 0.0 copy-done
  19.7 0.0 copy-done.1
  19.7 0.0 copy-done.2
  19.8 7.9 %expert_rows.1 = (bf16[80,1536]{1,0:T(8,128)(2,1)S(1)}, bf16[80,1536]{1,0:T(8,128)(2,1)S(1)}, bf16[80,2048]{1,0:T(8,128)(2,1)S(1)}, bf16[80,2048]{1,0:T(8,128)(2...) custom-call(bf16[240,128]{1,0:T(8,128)(2,1)S(1)} %join.2.refs_0_, ...), custom_call_target="tpu_custom_call" | custom-call | flops 10066329600 | bytes 18874368 | tf_op jit(solution)/shard_map/expert_rows/pallas_call | solution.py:287
  27.7 3.7 %collective-permute-start.10 = (bf16[240,128]{1,0:T(8,128)(2,1)S(1)}, bf16[240,128]{1,0:T(8,128)(2,1)S(1)}, u32[]{:S(2)}, u32[]{:S(2)}) collective-permute-start(bf16[240,128]{1,0:T(8,128)(2,1)S(1)} %get-tuple-element.32), channel_id=1, source_target_pairs={{0,3},{1,2},{2,1},{3,0},{4,7},{5,6},{6,5},{7,4},{8,11},{9,10},{10,... | collective-permute-start | bytes 184328 | tf_op jit(solution)/shard_map/ppermute | solution.py:443
  31.4 0.0 collective-permute-start.8
  31.4 0.7 %collective-permute-start.9 = (bf16[240,128]{1,0:T(8,128)(2,1)S(1)}, bf16[240,128]{1,0:T(8,128)(2,1)S(1)}, u32[]{:S(2)}, u32[]{:S(2)}) collective-permute-start(bf16[240,128]{1,0:T(8,128)(2,1)S(1)} %get-tuple-element.31), channel_id=1, source_target_pairs={{0,2},{1,3},{2,0},{3,1},{4,6},{5,7},{6,4},{7,5},{8,10},{9,11},{10,... | collective-permute-start | bytes 184328 | tf_op jit(solution)/shard_map/ppermute | solution.py:443
  32.1 0.0 copy-start.3
  32.1 0.0 copy-start.4
  32.1 5.1 %grads_in.1 = (bf16[1536,2048]{1,0:T(8,128)(2,1)}, bf16[1536,2048]{1,0:T(8,128)(2,1)}, f32[8,128]{1,0:T(8,128)S(1)}) custom-call(bf16[80,1536]{1,0:T(8,128)(2,1)S(1)} %get-tuple-element.33.left, bf16[80,2048]{1,0:T(8,128)(2,1)S(1)} %get-tuple-element.34.refs_0_, bf16[80,2048]{1,0:T(8,128)(2,1)S(1)} %get-tuple-element.35.refs_1_), custom_call_target="tpu_custom_call" | custom-call | flops 3221225472 | bytes 12582912 | tf_op jit(solution)/shard_map/grads_in/pallas_call | solution.py:334
  37.3 0.0 collective-permute-done.10.refs_3_
  37.3 0.0 collective-permute-done.8.refs_1_
  37.3 0.0 collective-permute-done.9.refs_2_
  37.3 0.1 collective-permute-start.11
  37.4 1.2 %collective-permute-done.11.received = bf16[128,128]{1,0:T(8,128)(2,1)S(1)} collective-permute-done((bf16[128,128]{1,0:T(8,128)(2,1)S(1)}, bf16[128,128]{1,0:T(8,128)(2,1)S(1)}, u32[]{:S(2)}, u32[]{:S(2)}) %collective-permute-start.11) | collective-permute-done | bytes 32800 | tf_op jit(solution)/shard_map/ppermute | solution.py:443
  38.6 1.5 %collective-permute-start.12 = (bf16[128,128]{1,0:T(8,128)(2,1)S(1)}, bf16[128,128]{1,0:T(8,128)(2,1)S(1)}, u32[]{:S(2)}, u32[]{:S(2)}) collective-permute-start(bf16[128,128]{1,0:T(8,128)(2,1)S(1)} %get-tuple-element.40), channel_id=1, source_target_pairs={{0,8},{4,12},{8,0},{12,4},{1,9},{5,13},{9,1},{13,5},{2,10},{6,14},... | collective-permute-start | bytes 98312 | tf_op jit(solution)/shard_map/ppermute | solution.py:443
  40.1 3.7 %grad_down.1 = (bf16[2048,1536]{1,0:T(8,128)(2,1)}, f32[8,128]{1,0:T(8,128)}) custom-call(bf16[80,2048]{1,0:T(8,128)(2,1)S(1)} %get-tuple-element.43.left, bf16[80,1536]{1,0:T(8,128)(2,1)S(1)} %get-tuple-element.44.refs_0_), custom_call_target="tpu_custom_call" | custom-call | flops 1610612736 | bytes 6291456 | tf_op jit(solution)/shard_map/grad_down/pallas_call | solution.py:334
  43.8 0.0 collective-permute-done.12.rest_1_
  43.8 0.0 copy-done.3
  43.8 0.0 copy-done.4
  43.8 1.6 %combine_rows.1 = bf16[8,3072]{1,0:T(8,128)(2,1)} custom-call(s32[2,8]{1,0:T(2,128)S(1)} %bitcast.3, s32[4,768]{1,0:T(4,128)S(1)} %copy-done.3, bf16[128,128]{1,0:T(8,128)(2,1)S(1)} %get-tuple-element.39.rest_0_, bf16[128,128]{1,0:T(8,128)(2,1)S(1)} %collective-permute-done.12.rest_1_), custom_call_target="tpu_custom_call" | custom-call | tf_op jit(solution)/shard_map/combine_rows/pallas_call | solution.py:424
  (5 shorter events, 0.1 us)
Async XLA Ops:
  0.6 19.1 %copy-start = (bf16[1536,2048]{1,0:T(8,128)(2,1)S(1)}, bf16[1536,2048]{1,0:T(8,128)(2,1)}, u32[]{:S(2)}) copy-start(bf16[1536,2048]{1,0:T(8,128)(2,1)} %refs_8_.1) | copy-start | bytes 18874372
  0.6 19.1 %copy-start.1 = (bf16[1536,2048]{1,0:T(8,128)(2,1)S(1)}, bf16[1536,2048]{1,0:T(8,128)(2,1)}, u32[]{:S(2)}) copy-start(bf16[1536,2048]{1,0:T(8,128)(2,1)} %refs_9_.1) | copy-start | bytes 18874372
  0.7 19.1 %copy-start.2 = (bf16[2048,1536]{1,0:T(8,128)(2,1)S(1)}, bf16[2048,1536]{1,0:T(8,128)(2,1)}, u32[]{:S(2)}) copy-start(bf16[2048,1536]{1,0:T(8,128)(2,1)} %refs_10_.1) | copy-start | bytes 18874372
  2.1 1.4 %collective-permute-start = (bf16[256,128]{1,0:T(8,128)(2,1)S(1)}, bf16[256,128]{1,0:T(8,128)(2,1)S(1)}, u32[]{:S(2)}, u32[]{:S(2)}) collective-permute-start(bf16[256,128]{1,0:T(8,128)(2,1)S(1)} %get-tuple-element.26), channel_id=1, source_target_pairs={{0,4},{4,0},{8,12},{12,8},{1,5},{5,1},{9,13},{13,9},{2,6},{6,2},{1... | collective-permute-start | bytes 196616 | tf_op jit(solution)/shard_map/ppermute | solution.py:443
  3.5 5.6 %collective-permute-start.4 = (bf16[256,128]{1,0:T(8,128)(2,1)S(1)}, bf16[256,128]{1,0:T(8,128)(2,1)S(1)}, u32[]{:S(2)}, u32[]{:S(2)}) collective-permute-start(bf16[256,128]{1,0:T(8,128)(2,1)S(1)} %get-tuple-element.28), channel_id=1, source_target_pairs={{0,8},{4,12},{8,0},{12,4},{1,9},{5,13},{9,1},{13,5},{2,10},{6,14},... | collective-permute-start | bytes 196616 | tf_op jit(solution)/shard_map/ppermute | solution.py:443
  6.5 7.0 %collective-permute-start.2 = (bf16[240,128]{1,0:T(8,128)(2,1)S(1)}, bf16[240,128]{1,0:T(8,128)(2,1)S(1)}, u32[]{:S(2)}, u32[]{:S(2)}) collective-permute-start(bf16[240,128]{1,0:T(8,128)(2,1)S(1)} %join.2.refs_0_), channel_id=1, source_target_pairs={{0,2},{1,3},{2,0},{3,1},{4,6},{5,7},{6,4},{7,5},{8,10},{9,11},{10,... | collective-permute-start | bytes 184328 | tf_op jit(solution)/shard_map/ppermute | solution.py:443
  9.1 6.4 %collective-permute-start.6 = (bf16[240,128]{1,0:T(8,128)(2,1)S(1)}, bf16[240,128]{1,0:T(8,128)(2,1)S(1)}, u32[]{:S(2)}, u32[]{:S(2)}) collective-permute-start(bf16[240,128]{1,0:T(8,128)(2,1)S(1)} %join.3.refs_4_), channel_id=1, source_target_pairs={{0,2},{1,3},{2,0},{3,1},{4,6},{5,7},{6,4},{7,5},{8,10},{9,11},{10,... | collective-permute-start | bytes 184328 | tf_op jit(solution)/shard_map/ppermute | solution.py:443
  11.9 4.9 %collective-permute-start.1 = (bf16[240,128]{1,0:T(8,128)(2,1)S(1)}, bf16[240,128]{1,0:T(8,128)(2,1)S(1)}, u32[]{:S(2)}, u32[]{:S(2)}) collective-permute-start(bf16[240,128]{1,0:T(8,128)(2,1)S(1)} %join.2.refs_0_), channel_id=1, source_target_pairs={{0,1},{1,0},{2,3},{3,2},{4,5},{5,4},{6,7},{7,6},{8,9},{9,8},{10,11... | collective-permute-start | bytes 184328 | tf_op jit(solution)/shard_map/ppermute | solution.py:443
  13.4 4.9 %collective-permute-start.3 = (bf16[240,128]{1,0:T(8,128)(2,1)S(1)}, bf16[240,128]{1,0:T(8,128)(2,1)S(1)}, u32[]{:S(2)}, u32[]{:S(2)}) collective-permute-start(bf16[240,128]{1,0:T(8,128)(2,1)S(1)} %collective-permute-done.2.refs_2_), channel_id=1, source_target_pairs={{0,1},{1,0},{2,3},{3,2},{4,5},{5,4},{6,7},{7,6},{8,9},{9,8},{10,11... | collective-permute-start | bytes 184328 | tf_op jit(solution)/shard_map/ppermute | solution.py:443
  14.3 4.7 %collective-permute-start.5 = (bf16[240,128]{1,0:T(8,128)(2,1)S(1)}, bf16[240,128]{1,0:T(8,128)(2,1)S(1)}, u32[]{:S(2)}, u32[]{:S(2)}) collective-permute-start(bf16[240,128]{1,0:T(8,128)(2,1)S(1)} %join.3.refs_4_), channel_id=1, source_target_pairs={{0,1},{1,0},{2,3},{3,2},{4,5},{5,4},{6,7},{7,6},{8,9},{9,8},{10,11... | collective-permute-start | bytes 184328 | tf_op jit(solution)/shard_map/ppermute | solution.py:443
  15.5 4.2 %collective-permute-start.7 = (bf16[240,128]{1,0:T(8,128)(2,1)S(1)}, bf16[240,128]{1,0:T(8,128)(2,1)S(1)}, u32[]{:S(2)}, u32[]{:S(2)}) collective-permute-start(bf16[240,128]{1,0:T(8,128)(2,1)S(1)} %collective-permute-done.6.refs_6_), channel_id=1, source_target_pairs={{0,1},{1,0},{2,3},{3,2},{4,5},{5,4},{6,7},{7,6},{8,9},{9,8},{10,11... | collective-permute-start | bytes 184328 | tf_op jit(solution)/shard_map/ppermute | solution.py:443
  27.7 9.6 %collective-permute-start.10 = (bf16[240,128]{1,0:T(8,128)(2,1)S(1)}, bf16[240,128]{1,0:T(8,128)(2,1)S(1)}, u32[]{:S(2)}, u32[]{:S(2)}) collective-permute-start(bf16[240,128]{1,0:T(8,128)(2,1)S(1)} %get-tuple-element.32), channel_id=1, source_target_pairs={{0,3},{1,2},{2,1},{3,0},{4,7},{5,6},{6,5},{7,4},{8,11},{9,10},{10,... | collective-permute-start | bytes 184328 | tf_op jit(solution)/shard_map/ppermute | solution.py:443
  31.4 5.9 %collective-permute-start.8 = (bf16[240,128]{1,0:T(8,128)(2,1)S(1)}, bf16[240,128]{1,0:T(8,128)(2,1)S(1)}, u32[]{:S(2)}, u32[]{:S(2)}) collective-permute-start(bf16[240,128]{1,0:T(8,128)(2,1)S(1)} %get-tuple-element.30), channel_id=1, source_target_pairs={{0,1},{1,0},{2,3},{3,2},{4,5},{5,4},{6,7},{7,6},{8,9},{9,8},{10,11... | collective-permute-start | bytes 184328 | tf_op jit(solution)/shard_map/ppermute | solution.py:443
  31.4 5.9 %collective-permute-start.9 = (bf16[240,128]{1,0:T(8,128)(2,1)S(1)}, bf16[240,128]{1,0:T(8,128)(2,1)S(1)}, u32[]{:S(2)}, u32[]{:S(2)}) collective-permute-start(bf16[240,128]{1,0:T(8,128)(2,1)S(1)} %get-tuple-element.31), channel_id=1, source_target_pairs={{0,2},{1,3},{2,0},{3,1},{4,6},{5,7},{6,4},{7,5},{8,10},{9,11},{10,... | collective-permute-start | bytes 184328 | tf_op jit(solution)/shard_map/ppermute | solution.py:443
  32.1 11.7 %copy-start.3 = (s32[4,768]{1,0:T(4,128)S(1)}, s32[4,768]{1,0:T(4,128)}, u32[]{:S(2)}) copy-start(s32[4,768]{1,0:T(4,128)} %pattern.1) | copy-start | bytes 36868
  32.1 11.7 %copy-start.4 = (s32[8,2]{0,1:T(2,128)S(1)}, s32[8,2]{0,1:T(2,128)}, u32[]{:S(2)}) copy-start(s32[8,2]{0,1:T(2,128)} %param.13) | copy-start | bytes 196
  37.3 1.3 %collective-permute-start.11 = (bf16[128,128]{1,0:T(8,128)(2,1)S(1)}, bf16[128,128]{1,0:T(8,128)(2,1)S(1)}, u32[]{:S(2)}, u32[]{:S(2)}) collective-permute-start(bf16[128,128]{1,0:T(8,128)(2,1)S(1)} %get-tuple-element.38), channel_id=1, source_target_pairs={{0,4},{4,0},{8,12},{12,8},{1,5},{5,1},{9,13},{13,9},{2,6},{6,2},{1... | collective-permute-start | bytes 98312 | tf_op jit(solution)/shard_map/ppermute | solution.py:443
  38.6 5.2 %collective-permute-start.12 = (bf16[128,128]{1,0:T(8,128)(2,1)S(1)}, bf16[128,128]{1,0:T(8,128)(2,1)S(1)}, u32[]{:S(2)}, u32[]{:S(2)}) collective-permute-start(bf16[128,128]{1,0:T(8,128)(2,1)S(1)} %get-tuple-element.40), channel_id=1, source_target_pairs={{0,8},{4,12},{8,0},{12,4},{1,9},{5,13},{9,1},{13,5},{2,10},{6,14},... | collective-permute-start | bytes 98312 | tf_op jit(solution)/shard_map/ppermute | solution.py:443

commit v5 on v4

--- a/solution.py
+++ b/solution.py
@@ -443,12 +443,21 @@
     return lax.ppermute(value, axis, [(i, i ^ k) for i in range(size)])
 
 
-def gather_line(value):
-    held = {0: value}
-    bit = lax.axis_size("tensor") // 2
+def cross(value, mask):
+    size = lax.axis_size("expert") * lax.axis_size("tensor")
+    return lax.ppermute(value, ("expert", "tensor"), [(i, i ^ mask) for i in range(size)])
+
+
+def gather_line(value, across):
+    far = lax.axis_size("tensor") // 2
+    start = across * lax.axis_size("tensor")
+    held = {0: cross(value, start) if across else value}
+    if far:
+        held[far] = cross(value, start + far)
+    bit = far // 2
     while bit:
         for k in list(held):
-            held[k ^ bit] = swap(held[k], "tensor", bit)
+            held[k ^ bit] = cross(held[k], bit)
         bit //= 2
     return [held[k] for k in range(len(held))]
 
@@ -467,7 +476,12 @@
     keep, send = dispatch(
         routes, combine, grad_scale, pattern, x_tokens, grad_values, (w_gate, w_up, w_down), n_e, holders, chunks
     )
-    near, far = (gather_line(join(b, block, dense)) for b in exchange(keep, send, 2 * block))
+    bit = 1
+    while 2 * bit < n_e:
+        keep, send = merge(keep, swap(send, "expert", bit), bit * 2 * block)
+        bit *= 2
+    near = gather_line(join(keep, block, dense), 0)
+    far = gather_line(join(send, block, dense), bit)
     rows_in, rows_grad, hidden, d_gate, d_up, *back = expert_rows(
         near, far, w_gate, w_up, w_down, n_e, dense, chunks
     )

time: 45.5 us -> 44.6 us (0.980)
  starting transfers between devices: 19.2 us -> 16.4 us
  waiting for transfers between devices: 5.56 us -> 7.48 us
    ppermute x13 -> x6, starting transfers between devices: 19.2 us -> 5.55 us  [swap(): return lax.ppermute(value, axis, [(i, i ^ k) for i in range(size)])]
    ppermute x0 -> x7, starting transfers between devices: none -> 10.8 us  [cross(): lax.ppermute(value, ('expert', 'tensor'), [(i, i ^ mask) for i in range(s...]
    ppermute x0 -> x7, waiting for transfers between devices: none -> 5.38 us  [cross(): lax.ppermute(value, ('expert', 'tensor'), [(i, i ^ mask) for i in range(s...]
    ppermute x13 -> x6, waiting for transfers between devices: 5.56 us -> 2.11 us  [swap(): return lax.ppermute(value, axis, [(i, i ^ k) for i in range(size)])]
where the time goes in v5:
time: 44.6 us; the launch traced here: 44.5 us
  Pallas kernels  19.8 us (44%)
  starting transfers between devices  16.4 us (37%)
  waiting for transfers between devices  7.48 us (17%)
  between operations  0.77 us (2%)
    ppermute x7, starting transfers between devices, cross(): lax.ppermute(value, ('expert', 'tensor'), [(i, i ^ mask) for i in range(s...  10.8 us
    pallas_call x2, Pallas kernels, outer(): pl.pallas_call(functools.partial(outer_kernel, count=count, tile=tile, wi...  8.84 us
    pallas_call x1, Pallas kernels, expert_rows(): pl.pallas_call(functools.partial(expert_kernel, n_t=n_t, n_e=n_e, dense=d...  7.9 us
    ppermute x6, starting transfers between devices, swap(): return lax.ppermute(value, axis, [(i, i ^ k) for i in range(size)])  5.55 us
    ppermute x7, waiting for transfers between devices, cross(): lax.ppermute(value, ('expert', 'tensor'), [(i, i ^ mask) for i in range(s...  5.38 us
    ppermute x6, waiting for transfers between devices, swap(): return lax.ppermute(value, axis, [(i, i ^ k) for i in range(size)])  2.11 us
    pallas_call x1, Pallas kernels, combine_rows(): pl.pallas_call(functools.partial(combine_kernel, n_e=n_e, holders=holders...  1.56 us
    pallas_call x1, Pallas kernels, dispatch(): pl.pallas_call(functools.partial(dispatch_kernel, n_e=n_e, holders=holder...  1.4 us
  transfers between devices with their start and end apart: 13, of which 6 were waited for; matrix products, arithmetic and copies ran while one was open for 0% of the time, Pallas kernels for 20%

profile of v5, /device:TPU:0, one launch (start us, length us, event | category | flops | bytes accessed | tf_op | source)
XLA Modules:
  0.0 44.5 jit_solution(4785357410459708313)
XLA Ops:
  0.6 0.0 copy-start
  0.6 0.0 copy-start.1
  0.7 0.0 copy-start.2
  0.7 1.4 %dispatch.1 = (bf16[256,128]{1,0:T(8,128)(2,1)S(1)}, bf16[256,128]{1,0:T(8,128)(2,1)S(1)}) custom-call(s32[2,8]{1,0:T(2,128)} %bitcast.2, f32[2,8]{1,0:T(2,128)} %bitcast.4, f32[8]{0:T(128)} %scale_any.1, s32[4,768]{1,0:T(4,128)} %pattern.1, bf16[8,3072]{1,0:T(8,128)(2,1)} %x_any.1, bf16[8,3072]{1,0:T(8,128)(2,1)} %g_any.1, bf16[1536,2048]{1,0:T(8,128)(2,1)} %refs_8_.1, ...), custom_call_target="tpu_custom_call" | custom-call | tf_op jit(solution)/shard_map/dispatch/pallas_call | solution.py:151
  2.1 0.5 %collective-permute-start = (bf16[256,128]{1,0:T(8,128)(2,1)S(1)}, bf16[256,128]{1,0:T(8,128)(2,1)S(1)}, u32[]{:S(2)}, u32[]{:S(2)}) collective-permute-start(bf16[256,128]{1,0:T(8,128)(2,1)S(1)} %get-tuple-element.26), channel_id=1, source_target_pairs={{0,4},{4,0},{8,12},{12,8},{1,5},{5,1},{9,13},{13,9},{2,6},{6,2},{1... | collective-permute-start | bytes 196616 | tf_op jit(solution)/shard_map/ppermute | solution.py:443
  2.6 0.9 %collective-permute-done.received = bf16[256,128]{1,0:T(8,128)(2,1)S(1)} collective-permute-done((bf16[256,128]{1,0:T(8,128)(2,1)S(1)}, bf16[256,128]{1,0:T(8,128)(2,1)S(1)}, u32[]{:S(2)}, u32[]{:S(2)}) %collective-permute-start) | collective-permute-done | bytes 65568 | tf_op jit(solution)/shard_map/ppermute | solution.py:443
  3.5 4.0 %collective-permute-start.2 = (bf16[240,128]{1,0:T(8,128)(2,1)S(1)}, bf16[240,128]{1,0:T(8,128)(2,1)S(1)}, u32[]{:S(2)}, u32[]{:S(2)}) collective-permute-start(bf16[240,128]{1,0:T(8,128)(2,1)S(1)} %join.2.refs_0_), channel_id=1, source_target_pairs={{0,2},{1,3},{2,0},{3,1},{4,6},{5,7},{6,4},{7,5},{8,10},{9,11},{10,... | collective-permute-start | bytes 184328 | tf_op jit(solution)/shard_map/ppermute | solution.py:448
  7.6 1.6 %collective-permute-start.4 = (bf16[240,128]{1,0:T(8,128)(2,1)S(1)}, bf16[240,128]{1,0:T(8,128)(2,1)S(1)}, u32[]{:S(2)}, u32[]{:S(2)}) collective-permute-start(bf16[240,128]{1,0:T(8,128)(2,1)S(1)} %join.3), channel_id=1, source_target_pairs={{0,8},{1,9},{2,10},{3,11},{4,12},{5,13},{6,14},{7,15},{8,0},{9,1},... | collective-permute-start | bytes 184328 | tf_op jit(solution)/shard_map/ppermute | solution.py:448
  9.1 0.0 collective-permute-start.6
  9.1 1.9 %collective-permute-start.1 = (bf16[240,128]{1,0:T(8,128)(2,1)S(1)}, bf16[240,128]{1,0:T(8,128)(2,1)S(1)}, u32[]{:S(2)}, u32[]{:S(2)}) collective-permute-start(bf16[240,128]{1,0:T(8,128)(2,1)S(1)} %join.2.refs_0_), channel_id=1, source_target_pairs={{0,1},{1,0},{2,3},{3,2},{4,5},{5,4},{6,7},{7,6},{8,9},{9,8},{10,11... | collective-permute-start | bytes 184328 | tf_op jit(solution)/shard_map/ppermute | solution.py:448
  11.0 0.2 collective-permute-done.2.refs_2_
  11.2 2.1 %collective-permute-start.3 = (bf16[240,128]{1,0:T(8,128)(2,1)S(1)}, bf16[240,128]{1,0:T(8,128)(2,1)S(1)}, u32[]{:S(2)}, u32[]{:S(2)}) collective-permute-start(bf16[240,128]{1,0:T(8,128)(2,1)S(1)} %collective-permute-done.2.refs_2_), channel_id=1, source_target_pairs={{0,1},{1,0},{2,3},{3,2},{4,5},{5,4},{6,7},{7,6},{8,9},{9,8},{10,11... | collective-permute-start | bytes 184328 | tf_op jit(solution)/shard_map/ppermute | solution.py:448
  13.3 0.0 collective-permute-done.4.refs_4_
  13.3 0.2 collective-permute-start.5
  13.4 2.1 %collective-permute-done.6.refs_6_ = bf16[240,128]{1,0:T(8,128)(2,1)S(1)} collective-permute-done((bf16[240,128]{1,0:T(8,128)(2,1)S(1)}, bf16[240,128]{1,0:T(8,128)(2,1)S(1)}, u32[]{:S(2)}, u32[]{:S(2)}) %collective-permute-start.6) | collective-permute-done | bytes 61472 | tf_op jit(solution)/shard_map/ppermute | solution.py:448
  15.6 1.2 %collective-permute-start.7 = (bf16[240,128]{1,0:T(8,128)(2,1)S(1)}, bf16[240,128]{1,0:T(8,128)(2,1)S(1)}, u32[]{:S(2)}, u32[]{:S(2)}) collective-permute-start(bf16[240,128]{1,0:T(8,128)(2,1)S(1)} %collective-permute-done.6.refs_6_), channel_id=1, source_target_pairs={{0,1},{1,0},{2,3},{3,2},{4,5},{5,4},{6,7},{7,6},{8,9},{9,8},{10,11... | collective-permute-start | bytes 184328 | tf_op jit(solution)/shard_map/ppermute | solution.py:448
  16.7 0.0 collective-permute-done.1.refs_1_
  16.7 0.0 collective-permute-done.3.refs_3_
  16.7 1.0 %collective-permute-done.5.refs_5_ = bf16[240,128]{1,0:T(8,128)(2,1)S(1)} collective-permute-done((bf16[240,128]{1,0:T(8,128)(2,1)S(1)}, bf16[240,128]{1,0:T(8,128)(2,1)S(1)}, u32[]{:S(2)}, u32[]{:S(2)}) %collective-permute-start.5) | collective-permute-done | bytes 61472 | tf_op jit(solution)/shard_map/ppermute | solution.py:448
  17.7 2.1 %collective-permute-done.7.refs_7_ = bf16[240,128]{1,0:T(8,128)(2,1)S(1)} collective-permute-done((bf16[240,128]{1,0:T(8,128)(2,1)S(1)}, bf16[240,128]{1,0:T(8,128)(2,1)S(1)}, u32[]{:S(2)}, u32[]{:S(2)}) %collective-permute-start.7) | collective-permute-done | bytes 61472 | tf_op jit(solution)/shard_map/ppermute | solution.py:448
  19.8 0.0 copy-done
  19.8 0.0 copy-done.1
  19.8 0.0 copy-done.2
  19.8 7.9 %expert_rows.1 = (bf16[80,1536]{1,0:T(8,128)(2,1)S(1)}, bf16[80,1536]{1,0:T(8,128)(2,1)S(1)}, bf16[80,2048]{1,0:T(8,128)(2,1)S(1)}, bf16[80,2048]{1,0:T(8,128)(2...) custom-call(bf16[240,128]{1,0:T(8,128)(2,1)S(1)} %join.2.refs_0_, ...), custom_call_target="tpu_custom_call" | custom-call | flops 10066329600 | bytes 18874368 | tf_op jit(solution)/shard_map/expert_rows/pallas_call | solution.py:287
  27.7 2.9 %collective-permute-start.10 = (bf16[240,128]{1,0:T(8,128)(2,1)S(1)}, bf16[240,128]{1,0:T(8,128)(2,1)S(1)}, u32[]{:S(2)}, u32[]{:S(2)}) collective-permute-start(bf16[240,128]{1,0:T(8,128)(2,1)S(1)} %get-tuple-element.32), channel_id=1, source_target_pairs={{0,3},{1,2},{2,1},{3,0},{4,7},{5,6},{6,5},{7,4},{8,11},{9,10},{10,... | collective-permute-start | bytes 184328 | tf_op jit(solution)/shard_map/ppermute | solution.py:443
  30.6 0.0 collective-permute-start.8
  30.6 1.6 %collective-permute-start.9 = (bf16[240,128]{1,0:T(8,128)(2,1)S(1)}, bf16[240,128]{1,0:T(8,128)(2,1)S(1)}, u32[]{:S(2)}, u32[]{:S(2)}) collective-permute-start(bf16[240,128]{1,0:T(8,128)(2,1)S(1)} %get-tuple-element.31), channel_id=1, source_target_pairs={{0,2},{1,3},{2,0},{3,1},{4,6},{5,7},{6,4},{7,5},{8,10},{9,11},{10,... | collective-permute-start | bytes 184328 | tf_op jit(solution)/shard_map/ppermute | solution.py:443
  32.2 0.0 copy-start.3
  32.2 0.0 copy-start.4
  32.2 5.1 %grads_in.1 = (bf16[1536,2048]{1,0:T(8,128)(2,1)}, bf16[1536,2048]{1,0:T(8,128)(2,1)}, f32[8,128]{1,0:T(8,128)S(1)}) custom-call(bf16[80,1536]{1,0:T(8,128)(2,1)S(1)} %get-tuple-element.33.left, bf16[80,2048]{1,0:T(8,128)(2,1)S(1)} %get-tuple-element.34.refs_0_, bf16[80,2048]{1,0:T(8,128)(2,1)S(1)} %get-tuple-element.35.refs_1_), custom_call_target="tpu_custom_call" | custom-call | flops 3221225472 | bytes 12582912 | tf_op jit(solution)/shard_map/grads_in/pallas_call | solution.py:334
  37.3 0.0 collective-permute-done.10.refs_3_
  37.3 0.0 collective-permute-done.8.refs_1_
  37.3 0.0 collective-permute-done.9.refs_2_
  37.4 0.1 collective-permute-start.11
  37.5 1.2 %collective-permute-done.11.received = bf16[128,128]{1,0:T(8,128)(2,1)S(1)} collective-permute-done((bf16[128,128]{1,0:T(8,128)(2,1)S(1)}, bf16[128,128]{1,0:T(8,128)(2,1)S(1)}, u32[]{:S(2)}, u32[]{:S(2)}) %collective-permute-start.11) | collective-permute-done | bytes 32800 | tf_op jit(solution)/shard_map/ppermute | solution.py:443
  38.7 0.5 %collective-permute-start.12 = (bf16[128,128]{1,0:T(8,128)(2,1)S(1)}, bf16[128,128]{1,0:T(8,128)(2,1)S(1)}, u32[]{:S(2)}, u32[]{:S(2)}) collective-permute-start(bf16[128,128]{1,0:T(8,128)(2,1)S(1)} %get-tuple-element.40), channel_id=1, source_target_pairs={{0,8},{4,12},{8,0},{12,4},{1,9},{5,13},{9,1},{13,5},{2,10},{6,14},... | collective-permute-start | bytes 98312 | tf_op jit(solution)/shard_map/ppermute | solution.py:443
  39.2 3.7 %grad_down.1 = (bf16[2048,1536]{1,0:T(8,128)(2,1)}, f32[8,128]{1,0:T(8,128)}) custom-call(bf16[80,2048]{1,0:T(8,128)(2,1)S(1)} %get-tuple-element.43.left, bf16[80,1536]{1,0:T(8,128)(2,1)S(1)} %get-tuple-element.44.refs_0_), custom_call_target="tpu_custom_call" | custom-call | flops 1610612736 | bytes 6291456 | tf_op jit(solution)/shard_map/grad_down/pallas_call | solution.py:334
  42.9 0.0 collective-permute-done.12.rest_1_
  42.9 0.0 copy-done.3
  42.9 0.0 copy-done.4
  42.9 1.6 %combine_rows.1 = bf16[8,3072]{1,0:T(8,128)(2,1)} custom-call(s32[2,8]{1,0:T(2,128)S(1)} %bitcast.3, s32[4,768]{1,0:T(4,128)S(1)} %copy-done.3, bf16[128,128]{1,0:T(8,128)(2,1)S(1)} %get-tuple-element.39.rest_0_, bf16[128,128]{1,0:T(8,128)(2,1)S(1)} %collective-permute-done.12.rest_1_), custom_call_target="tpu_custom_call" | custom-call | tf_op jit(solution)/shard_map/combine_rows/pallas_call | solution.py:424
  (5 shorter events, 0.1 us)
Async XLA Ops:
  0.6 19.2 %copy-start = (bf16[1536,2048]{1,0:T(8,128)(2,1)S(1)}, bf16[1536,2048]{1,0:T(8,128)(2,1)}, u32[]{:S(2)}) copy-start(bf16[1536,2048]{1,0:T(8,128)(2,1)} %refs_8_.1) | copy-start | bytes 18874372
  0.6 19.1 %copy-start.1 = (bf16[1536,2048]{1,0:T(8,128)(2,1)S(1)}, bf16[1536,2048]{1,0:T(8,128)(2,1)}, u32[]{:S(2)}) copy-start(bf16[1536,2048]{1,0:T(8,128)(2,1)} %refs_9_.1) | copy-start | bytes 18874372
  0.7 19.1 %copy-start.2 = (bf16[2048,1536]{1,0:T(8,128)(2,1)S(1)}, bf16[2048,1536]{1,0:T(8,128)(2,1)}, u32[]{:S(2)}) copy-start(bf16[2048,1536]{1,0:T(8,128)(2,1)} %refs_10_.1) | copy-start | bytes 18874372
  2.1 1.4 %collective-permute-start = (bf16[256,128]{1,0:T(8,128)(2,1)S(1)}, bf16[256,128]{1,0:T(8,128)(2,1)S(1)}, u32[]{:S(2)}, u32[]{:S(2)}) collective-permute-start(bf16[256,128]{1,0:T(8,128)(2,1)S(1)} %get-tuple-element.26), channel_id=1, source_target_pairs={{0,4},{4,0},{8,12},{12,8},{1,5},{5,1},{9,13},{13,9},{2,6},{6,2},{1... | collective-permute-start | bytes 196616 | tf_op jit(solution)/shard_map/ppermute | solution.py:443
  3.5 7.6 %collective-permute-start.2 = (bf16[240,128]{1,0:T(8,128)(2,1)S(1)}, bf16[240,128]{1,0:T(8,128)(2,1)S(1)}, u32[]{:S(2)}, u32[]{:S(2)}) collective-permute-start(bf16[240,128]{1,0:T(8,128)(2,1)S(1)} %join.2.refs_0_), channel_id=1, source_target_pairs={{0,2},{1,3},{2,0},{3,1},{4,6},{5,7},{6,4},{7,5},{8,10},{9,11},{10,... | collective-permute-start | bytes 184328 | tf_op jit(solution)/shard_map/ppermute | solution.py:448
  7.6 5.7 %collective-permute-start.4 = (bf16[240,128]{1,0:T(8,128)(2,1)S(1)}, bf16[240,128]{1,0:T(8,128)(2,1)S(1)}, u32[]{:S(2)}, u32[]{:S(2)}) collective-permute-start(bf16[240,128]{1,0:T(8,128)(2,1)S(1)} %join.3), channel_id=1, source_target_pairs={{0,8},{1,9},{2,10},{3,11},{4,12},{5,13},{6,14},{7,15},{8,0},{9,1},... | collective-permute-start | bytes 184328 | tf_op jit(solution)/shard_map/ppermute | solution.py:448
  9.1 6.4 %collective-permute-start.6 = (bf16[240,128]{1,0:T(8,128)(2,1)S(1)}, bf16[240,128]{1,0:T(8,128)(2,1)S(1)}, u32[]{:S(2)}, u32[]{:S(2)}) collective-permute-start(bf16[240,128]{1,0:T(8,128)(2,1)S(1)} %join.3), channel_id=1, source_target_pairs={{0,10},{1,11},{2,8},{3,9},{4,14},{5,15},{6,12},{7,13},{8,2},{9,3},... | collective-permute-start | bytes 184328 | tf_op jit(solution)/shard_map/ppermute | solution.py:448
  9.1 7.6 %collective-permute-start.1 = (bf16[240,128]{1,0:T(8,128)(2,1)S(1)}, bf16[240,128]{1,0:T(8,128)(2,1)S(1)}, u32[]{:S(2)}, u32[]{:S(2)}) collective-permute-start(bf16[240,128]{1,0:T(8,128)(2,1)S(1)} %join.2.refs_0_), channel_id=1, source_target_pairs={{0,1},{1,0},{2,3},{3,2},{4,5},{5,4},{6,7},{7,6},{8,9},{9,8},{10,11... | collective-permute-start | bytes 184328 | tf_op jit(solution)/shard_map/ppermute | solution.py:448
  11.2 5.6 %collective-permute-start.3 = (bf16[240,128]{1,0:T(8,128)(2,1)S(1)}, bf16[240,128]{1,0:T(8,128)(2,1)S(1)}, u32[]{:S(2)}, u32[]{:S(2)}) collective-permute-start(bf16[240,128]{1,0:T(8,128)(2,1)S(1)} %collective-permute-done.2.refs_2_), channel_id=1, source_target_pairs={{0,1},{1,0},{2,3},{3,2},{4,5},{5,4},{6,7},{7,6},{8,9},{9,8},{10,11... | collective-permute-start | bytes 184328 | tf_op jit(solution)/shard_map/ppermute | solution.py:448
  13.3 4.5 %collective-permute-start.5 = (bf16[240,128]{1,0:T(8,128)(2,1)S(1)}, bf16[240,128]{1,0:T(8,128)(2,1)S(1)}, u32[]{:S(2)}, u32[]{:S(2)}) collective-permute-start(bf16[240,128]{1,0:T(8,128)(2,1)S(1)} %collective-permute-done.4.refs_4_), channel_id=1, source_target_pairs={{0,1},{1,0},{2,3},{3,2},{4,5},{5,4},{6,7},{7,6},{8,9},{9,8},{10,11... | collective-permute-start | bytes 184328 | tf_op jit(solution)/shard_map/ppermute | solution.py:448
  15.6 4.2 %collective-permute-start.7 = (bf16[240,128]{1,0:T(8,128)(2,1)S(1)}, bf16[240,128]{1,0:T(8,128)(2,1)S(1)}, u32[]{:S(2)}, u32[]{:S(2)}) collective-permute-start(bf16[240,128]{1,0:T(8,128)(2,1)S(1)} %collective-permute-done.6.refs_6_), channel_id=1, source_target_pairs={{0,1},{1,0},{2,3},{3,2},{4,5},{5,4},{6,7},{7,6},{8,9},{9,8},{10,11... | collective-permute-start | bytes 184328 | tf_op jit(solution)/shard_map/ppermute | solution.py:448
  27.7 9.6 %collective-permute-start.10 = (bf16[240,128]{1,0:T(8,128)(2,1)S(1)}, bf16[240,128]{1,0:T(8,128)(2,1)S(1)}, u32[]{:S(2)}, u32[]{:S(2)}) collective-permute-start(bf16[240,128]{1,0:T(8,128)(2,1)S(1)} %get-tuple-element.32), channel_id=1, source_target_pairs={{0,3},{1,2},{2,1},{3,0},{4,7},{5,6},{6,5},{7,4},{8,11},{9,10},{10,... | collective-permute-start | bytes 184328 | tf_op jit(solution)/shard_map/ppermute | solution.py:443
  30.6 6.7 %collective-permute-start.8 = (bf16[240,128]{1,0:T(8,128)(2,1)S(1)}, bf16[240,128]{1,0:T(8,128)(2,1)S(1)}, u32[]{:S(2)}, u32[]{:S(2)}) collective-permute-start(bf16[240,128]{1,0:T(8,128)(2,1)S(1)} %get-tuple-element.30), channel_id=1, source_target_pairs={{0,1},{1,0},{2,3},{3,2},{4,5},{5,4},{6,7},{7,6},{8,9},{9,8},{10,11... | collective-permute-start | bytes 184328 | tf_op jit(solution)/shard_map/ppermute | solution.py:443
  30.6 6.7 %collective-permute-start.9 = (bf16[240,128]{1,0:T(8,128)(2,1)S(1)}, bf16[240,128]{1,0:T(8,128)(2,1)S(1)}, u32[]{:S(2)}, u32[]{:S(2)}) collective-permute-start(bf16[240,128]{1,0:T(8,128)(2,1)S(1)} %get-tuple-element.31), channel_id=1, source_target_pairs={{0,2},{1,3},{2,0},{3,1},{4,6},{5,7},{6,4},{7,5},{8,10},{9,11},{10,... | collective-permute-start | bytes 184328 | tf_op jit(solution)/shard_map/ppermute | solution.py:443
  32.2 10.7 %copy-start.3 = (s32[4,768]{1,0:T(4,128)S(1)}, s32[4,768]{1,0:T(4,128)}, u32[]{:S(2)}) copy-start(s32[4,768]{1,0:T(4,128)} %pattern.1) | copy-start | bytes 36868
  32.2 10.8 %copy-start.4 = (s32[8,2]{0,1:T(2,128)S(1)}, s32[8,2]{0,1:T(2,128)}, u32[]{:S(2)}) copy-start(s32[8,2]{0,1:T(2,128)} %param.13) | copy-start | bytes 196
  37.4 1.3 %collective-permute-start.11 = (bf16[128,128]{1,0:T(8,128)(2,1)S(1)}, bf16[128,128]{1,0:T(8,128)(2,1)S(1)}, u32[]{:S(2)}, u32[]{:S(2)}) collective-permute-start(bf16[128,128]{1,0:T(8,128)(2,1)S(1)} %get-tuple-element.38), channel_id=1, source_target_pairs={{0,4},{4,0},{8,12},{12,8},{1,5},{5,1},{9,13},{13,9},{2,6},{6,2},{1... | collective-permute-start | bytes 98312 | tf_op jit(solution)/shard_map/ppermute | solution.py:443
  38.7 4.2 %collective-permute-start.12 = (bf16[128,128]{1,0:T(8,128)(2,1)S(1)}, bf16[128,128]{1,0:T(8,128)(2,1)S(1)}, u32[]{:S(2)}, u32[]{:S(2)}) collective-permute-start(bf16[128,128]{1,0:T(8,128)(2,1)S(1)} %get-tuple-element.40), channel_id=1, source_target_pairs={{0,8},{4,12},{8,0},{12,4},{1,9},{5,13},{9,1},{13,5},{2,10},{6,14},... | collective-permute-start | bytes 98312 | tf_op jit(solution)/shard_map/ppermute | solution.py:443

commit v6 on v5

--- a/solution.py
+++ b/solution.py
@@ -449,17 +449,13 @@
 
 
 def gather_line(value, across):
-    far = lax.axis_size("tensor") // 2
-    start = across * lax.axis_size("tensor")
+    n_t = lax.axis_size("tensor")
+    start = across * n_t
     held = {0: cross(value, start) if across else value}
-    if far:
-        held[far] = cross(value, start + far)
-    bit = far // 2
-    while bit:
-        for k in list(held):
-            held[k ^ bit] = cross(held[k], bit)
-        bit //= 2
-    return [held[k] for k in range(len(held))]
+    for k in range(1, n_t):
+        rest = k & (k - 1)
+        held[k] = cross(held[rest], k - rest) if rest else cross(value, start + k)
+    return [held[k] for k in range(n_t)]
 
 
 def body(x_tokens, grad_values, grad_scale, combine, routes, pattern, w_gate, w_up, w_down):

time: 44.6 us -> 44.4 us (level)
  waiting for transfers between devices: 7.48 us -> 6.78 us
  starting transfers between devices: 16.4 us -> 17 us
    ppermute x7, waiting for transfers between devices: 5.38 us -> 4.67 us  [cross(): lax.ppermute(value, ('expert', 'tensor'), [(i, i ^ mask) for i in range(s...]
  transfers between devices with their start and end apart: 13 -> 13, of which waited for: 6 -> 7; matrix products, arithmetic and copies ran while one was open for 0% -> 0% of each run, Pallas kernels for 20% -> 20%
where the time goes in v6:
time: 44.4 us; the launch traced here: 44.3 us
  Pallas kernels  19.7 us (44%)
  starting transfers between devices  17 us (38%)
  waiting for transfers between devices  6.78 us (15%)
  between operations  0.77 us (2%)
    ppermute x7, starting transfers between devices, cross(): lax.ppermute(value, ('expert', 'tensor'), [(i, i ^ mask) for i in range(s...  11.1 us
    pallas_call x2, Pallas kernels, outer(): pl.pallas_call(functools.partial(outer_kernel, count=count, tile=tile, wi...  8.83 us
    pallas_call x1, Pallas kernels, expert_rows(): pl.pallas_call(functools.partial(expert_kernel, n_t=n_t, n_e=n_e, dense=d...  7.77 us
    ppermute x6, starting transfers between devices, swap(): return lax.ppermute(value, axis, [(i, i ^ k) for i in range(size)])  5.97 us
    ppermute x7, waiting for transfers between devices, cross(): lax.ppermute(value, ('expert', 'tensor'), [(i, i ^ mask) for i in range(s...  4.67 us
    ppermute x6, waiting for transfers between devices, swap(): return lax.ppermute(value, axis, [(i, i ^ k) for i in range(size)])  2.11 us
    pallas_call x1, Pallas kernels, combine_rows(): pl.pallas_call(functools.partial(combine_kernel, n_e=n_e, holders=holders...  1.55 us
    pallas_call x1, Pallas kernels, dispatch(): pl.pallas_call(functools.partial(dispatch_kernel, n_e=n_e, holders=holder...  1.41 us
  transfers between devices with their start and end apart: 13, of which 7 were waited for; matrix products, arithmetic and copies ran while one was open for 0% of the time, Pallas kernels for 20%

profile of v6, /device:TPU:0, one launch (start us, length us, event | category | flops | bytes accessed | tf_op | source)
XLA Modules:
  0.0 44.3 jit_solution(6423861422748303071)
XLA Ops:
  0.6 0.0 copy-start
  0.6 0.0 copy-start.1
  0.7 0.0 copy-start.2
  0.7 1.4 %dispatch.1 = (bf16[256,128]{1,0:T(8,128)(2,1)S(1)}, bf16[256,128]{1,0:T(8,128)(2,1)S(1)}) custom-call(s32[2,8]{1,0:T(2,128)} %bitcast.2, f32[2,8]{1,0:T(2,128)} %bitcast.4, f32[8]{0:T(128)} %scale_any.1, s32[4,768]{1,0:T(4,128)} %pattern.1, bf16[8,3072]{1,0:T(8,128)(2,1)} %x_any.1, bf16[8,3072]{1,0:T(8,128)(2,1)} %g_any.1, bf16[1536,2048]{1,0:T(8,128)(2,1)} %refs_8_.1, ...), custom_call_target="tpu_custom_call" | custom-call | tf_op jit(solution)/shard_map/dispatch/pallas_call | solution.py:151
  2.1 0.5 %collective-permute-start = (bf16[256,128]{1,0:T(8,128)(2,1)S(1)}, bf16[256,128]{1,0:T(8,128)(2,1)S(1)}, u32[]{:S(2)}, u32[]{:S(2)}) collective-permute-start(bf16[256,128]{1,0:T(8,128)(2,1)S(1)} %get-tuple-element.26), channel_id=1, source_target_pairs={{0,4},{4,0},{8,12},{12,8},{1,5},{5,1},{9,13},{13,9},{2,6},{6,2},{1... | collective-permute-start | bytes 196616 | tf_op jit(solution)/shard_map/ppermute | solution.py:443
  2.6 0.9 %collective-permute-done.received = bf16[256,128]{1,0:T(8,128)(2,1)S(1)} collective-permute-done((bf16[256,128]{1,0:T(8,128)(2,1)S(1)}, bf16[256,128]{1,0:T(8,128)(2,1)S(1)}, u32[]{:S(2)}, u32[]{:S(2)}) %collective-permute-start) | collective-permute-done | bytes 65568 | tf_op jit(solution)/shard_map/ppermute | solution.py:443
  3.5 4.0 %collective-permute-start.2 = (bf16[240,128]{1,0:T(8,128)(2,1)S(1)}, bf16[240,128]{1,0:T(8,128)(2,1)S(1)}, u32[]{:S(2)}, u32[]{:S(2)}) collective-permute-start(bf16[240,128]{1,0:T(8,128)(2,1)S(1)} %join.2.refs_0_), channel_id=1, source_target_pairs={{0,2},{1,3},{2,0},{3,1},{4,6},{5,7},{6,4},{7,5},{8,10},{9,11},{10,... | collective-permute-start | bytes 184328 | tf_op jit(solution)/shard_map/ppermute | solution.py:448
  7.6 1.4 %collective-permute-start.6 = (bf16[240,128]{1,0:T(8,128)(2,1)S(1)}, bf16[240,128]{1,0:T(8,128)(2,1)S(1)}, u32[]{:S(2)}, u32[]{:S(2)}) collective-permute-start(bf16[240,128]{1,0:T(8,128)(2,1)S(1)} %join.3), channel_id=1, source_target_pairs={{0,10},{1,11},{2,8},{3,9},{4,14},{5,15},{6,12},{7,13},{8,2},{9,3},... | collective-permute-start | bytes 184328 | tf_op jit(solution)/shard_map/ppermute | solution.py:448
  8.9 1.6 %collective-permute-start.1 = (bf16[240,128]{1,0:T(8,128)(2,1)S(1)}, bf16[240,128]{1,0:T(8,128)(2,1)S(1)}, u32[]{:S(2)}, u32[]{:S(2)}) collective-permute-start(bf16[240,128]{1,0:T(8,128)(2,1)S(1)} %join.2.refs_0_), channel_id=1, source_target_pairs={{0,1},{1,0},{2,3},{3,2},{4,5},{5,4},{6,7},{7,6},{8,9},{9,8},{10,11... | collective-permute-start | bytes 184328 | tf_op jit(solution)/shard_map/ppermute | solution.py:448
  10.5 0.5 %collective-permute-start.4 = (bf16[240,128]{1,0:T(8,128)(2,1)S(1)}, bf16[240,128]{1,0:T(8,128)(2,1)S(1)}, u32[]{:S(2)}, u32[]{:S(2)}) collective-permute-start(bf16[240,128]{1,0:T(8,128)(2,1)S(1)} %join.3), channel_id=1, source_target_pairs={{0,8},{1,9},{2,10},{3,11},{4,12},{5,13},{6,14},{7,15},{8,0},{9,1},... | collective-permute-start | bytes 184328 | tf_op jit(solution)/shard_map/ppermute | solution.py:448
  11.0 1.4 %collective-permute-start.5 = (bf16[240,128]{1,0:T(8,128)(2,1)S(1)}, bf16[240,128]{1,0:T(8,128)(2,1)S(1)}, u32[]{:S(2)}, u32[]{:S(2)}) collective-permute-start(bf16[240,128]{1,0:T(8,128)(2,1)S(1)} %join.3), channel_id=1, source_target_pairs={{0,9},{1,8},{2,11},{3,10},{4,13},{5,12},{6,15},{7,14},{8,1},{9,0},... | collective-permute-start | bytes 184328 | tf_op jit(solution)/shard_map/ppermute | solution.py:448
  12.4 0.0 collective-permute-done.2.refs_2_
  12.4 1.6 %collective-permute-start.3 = (bf16[240,128]{1,0:T(8,128)(2,1)S(1)}, bf16[240,128]{1,0:T(8,128)(2,1)S(1)}, u32[]{:S(2)}, u32[]{:S(2)}) collective-permute-start(bf16[240,128]{1,0:T(8,128)(2,1)S(1)} %collective-permute-done.2.refs_2_), channel_id=1, source_target_pairs={{0,1},{1,0},{2,3},{3,2},{4,5},{5,4},{6,7},{7,6},{8,9},{9,8},{10,11... | collective-permute-start | bytes 184328 | tf_op jit(solution)/shard_map/ppermute | solution.py:448
  14.0 1.1 %collective-permute-done.6.refs_6_ = bf16[240,128]{1,0:T(8,128)(2,1)S(1)} collective-permute-done((bf16[240,128]{1,0:T(8,128)(2,1)S(1)}, bf16[240,128]{1,0:T(8,128)(2,1)S(1)}, u32[]{:S(2)}, u32[]{:S(2)}) %collective-permute-start.6) | collective-permute-done | bytes 61472 | tf_op jit(solution)/shard_map/ppermute | solution.py:448
  15.1 0.6 %collective-permute-start.7 = (bf16[240,128]{1,0:T(8,128)(2,1)S(1)}, bf16[240,128]{1,0:T(8,128)(2,1)S(1)}, u32[]{:S(2)}, u32[]{:S(2)}) collective-permute-start(bf16[240,128]{1,0:T(8,128)(2,1)S(1)} %collective-permute-done.6.refs_6_), channel_id=1, source_target_pairs={{0,1},{1,0},{2,3},{3,2},{4,5},{5,4},{6,7},{7,6},{8,9},{9,8},{10,11... | collective-permute-start | bytes 184328 | tf_op jit(solution)/shard_map/ppermute | solution.py:448
  15.7 0.0 collective-permute-done.1.refs_1_
  15.7 0.2 collective-permute-done.4.refs_4_
  15.9 0.4 collective-permute-done.5.refs_5_
  16.3 1.0 %collective-permute-done.3.refs_3_ = bf16[240,128]{1,0:T(8,128)(2,1)S(1)} collective-permute-done((bf16[240,128]{1,0:T(8,128)(2,1)S(1)}, bf16[240,128]{1,0:T(8,128)(2,1)S(1)}, u32[]{:S(2)}, u32[]{:S(2)}) %collective-permute-start.3) | collective-permute-done | bytes 61472 | tf_op jit(solution)/shard_map/ppermute | solution.py:448
  17.3 2.0 %collective-permute-done.7.refs_7_ = bf16[240,128]{1,0:T(8,128)(2,1)S(1)} collective-permute-done((bf16[240,128]{1,0:T(8,128)(2,1)S(1)}, bf16[240,128]{1,0:T(8,128)(2,1)S(1)}, u32[]{:S(2)}, u32[]{:S(2)}) %collective-permute-start.7) | collective-permute-done | bytes 61472 | tf_op jit(solution)/shard_map/ppermute | solution.py:448
  19.3 0.0 copy-done
  19.3 0.0 copy-done.1
  19.3 0.0 copy-done.2
  19.3 7.8 %expert_rows.1 = (bf16[80,1536]{1,0:T(8,128)(2,1)S(1)}, bf16[80,1536]{1,0:T(8,128)(2,1)S(1)}, bf16[80,2048]{1,0:T(8,128)(2,1)S(1)}, bf16[80,2048]{1,0:T(8,128)(2...) custom-call(bf16[240,128]{1,0:T(8,128)(2,1)S(1)} %join.2.refs_0_, ...), custom_call_target="tpu_custom_call" | custom-call | flops 10066329600 | bytes 18874368 | tf_op jit(solution)/shard_map/expert_rows/pallas_call | solution.py:287
  27.1 3.5 %collective-permute-start.10 = (bf16[240,128]{1,0:T(8,128)(2,1)S(1)}, bf16[240,128]{1,0:T(8,128)(2,1)S(1)}, u32[]{:S(2)}, u32[]{:S(2)}) collective-permute-start(bf16[240,128]{1,0:T(8,128)(2,1)S(1)} %get-tuple-element.32), channel_id=1, source_target_pairs={{0,3},{1,2},{2,1},{3,0},{4,7},{5,6},{6,5},{7,4},{8,11},{9,10},{10,... | collective-permute-start | bytes 184328 | tf_op jit(solution)/shard_map/ppermute | solution.py:443
  30.6 0.0 collective-permute-start.8
  30.6 0.9 %collective-permute-start.9 = (bf16[240,128]{1,0:T(8,128)(2,1)S(1)}, bf16[240,128]{1,0:T(8,128)(2,1)S(1)}, u32[]{:S(2)}, u32[]{:S(2)}) collective-permute-start(bf16[240,128]{1,0:T(8,128)(2,1)S(1)} %get-tuple-element.31), channel_id=1, source_target_pairs={{0,2},{1,3},{2,0},{3,1},{4,6},{5,7},{6,4},{7,5},{8,10},{9,11},{10,... | collective-permute-start | bytes 184328 | tf_op jit(solution)/shard_map/ppermute | solution.py:443
  31.5 0.0 copy-start.3
  31.5 0.0 copy-start.4
  31.5 5.1 %grads_in.1 = (bf16[1536,2048]{1,0:T(8,128)(2,1)}, bf16[1536,2048]{1,0:T(8,128)(2,1)}, f32[8,128]{1,0:T(8,128)S(1)}) custom-call(bf16[80,1536]{1,0:T(8,128)(2,1)S(1)} %get-tuple-element.33.left, bf16[80,2048]{1,0:T(8,128)(2,1)S(1)} %get-tuple-element.34.refs_0_, bf16[80,2048]{1,0:T(8,128)(2,1)S(1)} %get-tuple-element.35.refs_1_), custom_call_target="tpu_custom_call" | custom-call | flops 3221225472 | bytes 12582912 | tf_op jit(solution)/shard_map/grads_in/pallas_call | solution.py:334
  36.7 0.0 collective-permute-done.10.refs_3_
  36.7 0.0 collective-permute-done.8.refs_1_
  36.7 0.0 collective-permute-done.9.refs_2_
  36.7 0.1 collective-permute-start.11
  36.8 1.2 %collective-permute-done.11.received = bf16[128,128]{1,0:T(8,128)(2,1)S(1)} collective-permute-done((bf16[128,128]{1,0:T(8,128)(2,1)S(1)}, bf16[128,128]{1,0:T(8,128)(2,1)S(1)}, u32[]{:S(2)}, u32[]{:S(2)}) %collective-permute-start.11) | collective-permute-done | bytes 32800 | tf_op jit(solution)/shard_map/ppermute | solution.py:443
  38.0 0.9 %collective-permute-start.12 = (bf16[128,128]{1,0:T(8,128)(2,1)S(1)}, bf16[128,128]{1,0:T(8,128)(2,1)S(1)}, u32[]{:S(2)}, u32[]{:S(2)}) collective-permute-start(bf16[128,128]{1,0:T(8,128)(2,1)S(1)} %get-tuple-element.40), channel_id=1, source_target_pairs={{0,8},{4,12},{8,0},{12,4},{1,9},{5,13},{9,1},{13,5},{2,10},{6,14},... | collective-permute-start | bytes 98312 | tf_op jit(solution)/shard_map/ppermute | solution.py:443
  39.0 3.7 %grad_down.1 = (bf16[2048,1536]{1,0:T(8,128)(2,1)}, f32[8,128]{1,0:T(8,128)}) custom-call(bf16[80,2048]{1,0:T(8,128)(2,1)S(1)} %get-tuple-element.43.left, bf16[80,1536]{1,0:T(8,128)(2,1)S(1)} %get-tuple-element.44.refs_0_), custom_call_target="tpu_custom_call" | custom-call | flops 1610612736 | bytes 6291456 | tf_op jit(solution)/shard_map/grad_down/pallas_call | solution.py:334
  42.7 0.0 collective-permute-done.12.rest_1_
  42.7 0.0 copy-done.3
  42.7 0.0 copy-done.4
  42.7 1.6 %combine_rows.1 = bf16[8,3072]{1,0:T(8,128)(2,1)} custom-call(s32[2,8]{1,0:T(2,128)S(1)} %bitcast.3, s32[4,768]{1,0:T(4,128)S(1)} %copy-done.3, bf16[128,128]{1,0:T(8,128)(2,1)S(1)} %get-tuple-element.39.rest_0_, bf16[128,128]{1,0:T(8,128)(2,1)S(1)} %collective-permute-done.12.rest_1_), custom_call_target="tpu_custom_call" | custom-call | tf_op jit(solution)/shard_map/combine_rows/pallas_call | solution.py:424
  (5 shorter events, 0.1 us)
Async XLA Ops:
  0.6 18.7 %copy-start = (bf16[1536,2048]{1,0:T(8,128)(2,1)S(1)}, bf16[1536,2048]{1,0:T(8,128)(2,1)}, u32[]{:S(2)}) copy-start(bf16[1536,2048]{1,0:T(8,128)(2,1)} %refs_8_.1) | copy-start | bytes 18874372
  0.6 18.7 %copy-start.1 = (bf16[1536,2048]{1,0:T(8,128)(2,1)S(1)}, bf16[1536,2048]{1,0:T(8,128)(2,1)}, u32[]{:S(2)}) copy-start(bf16[1536,2048]{1,0:T(8,128)(2,1)} %refs_9_.1) | copy-start | bytes 18874372
  0.7 18.7 %copy-start.2 = (bf16[2048,1536]{1,0:T(8,128)(2,1)S(1)}, bf16[2048,1536]{1,0:T(8,128)(2,1)}, u32[]{:S(2)}) copy-start(bf16[2048,1536]{1,0:T(8,128)(2,1)} %refs_10_.1) | copy-start | bytes 18874372
  2.1 1.4 %collective-permute-start = (bf16[256,128]{1,0:T(8,128)(2,1)S(1)}, bf16[256,128]{1,0:T(8,128)(2,1)S(1)}, u32[]{:S(2)}, u32[]{:S(2)}) collective-permute-start(bf16[256,128]{1,0:T(8,128)(2,1)S(1)} %get-tuple-element.26), channel_id=1, source_target_pairs={{0,4},{4,0},{8,12},{12,8},{1,5},{5,1},{9,13},{13,9},{2,6},{6,2},{1... | collective-permute-start | bytes 196616 | tf_op jit(solution)/shard_map/ppermute | solution.py:443
  3.5 8.9 %collective-permute-start.2 = (bf16[240,128]{1,0:T(8,128)(2,1)S(1)}, bf16[240,128]{1,0:T(8,128)(2,1)S(1)}, u32[]{:S(2)}, u32[]{:S(2)}) collective-permute-start(bf16[240,128]{1,0:T(8,128)(2,1)S(1)} %join.2.refs_0_), channel_id=1, source_target_pairs={{0,2},{1,3},{2,0},{3,1},{4,6},{5,7},{6,4},{7,5},{8,10},{9,11},{10,... | collective-permute-start | bytes 184328 | tf_op jit(solution)/shard_map/ppermute | solution.py:448
  7.6 7.5 %collective-permute-start.6 = (bf16[240,128]{1,0:T(8,128)(2,1)S(1)}, bf16[240,128]{1,0:T(8,128)(2,1)S(1)}, u32[]{:S(2)}, u32[]{:S(2)}) collective-permute-start(bf16[240,128]{1,0:T(8,128)(2,1)S(1)} %join.3), channel_id=1, source_target_pairs={{0,10},{1,11},{2,8},{3,9},{4,14},{5,15},{6,12},{7,13},{8,2},{9,3},... | collective-permute-start | bytes 184328 | tf_op jit(solution)/shard_map/ppermute | solution.py:448
  8.9 6.8 %collective-permute-start.1 = (bf16[240,128]{1,0:T(8,128)(2,1)S(1)}, bf16[240,128]{1,0:T(8,128)(2,1)S(1)}, u32[]{:S(2)}, u32[]{:S(2)}) collective-permute-start(bf16[240,128]{1,0:T(8,128)(2,1)S(1)} %join.2.refs_0_), channel_id=1, source_target_pairs={{0,1},{1,0},{2,3},{3,2},{4,5},{5,4},{6,7},{7,6},{8,9},{9,8},{10,11... | collective-permute-start | bytes 184328 | tf_op jit(solution)/shard_map/ppermute | solution.py:448
  10.5 5.4 %collective-permute-start.4 = (bf16[240,128]{1,0:T(8,128)(2,1)S(1)}, bf16[240,128]{1,0:T(8,128)(2,1)S(1)}, u32[]{:S(2)}, u32[]{:S(2)}) collective-permute-start(bf16[240,128]{1,0:T(8,128)(2,1)S(1)} %join.3), channel_id=1, source_target_pairs={{0,8},{1,9},{2,10},{3,11},{4,12},{5,13},{6,14},{7,15},{8,0},{9,1},... | collective-permute-start | bytes 184328 | tf_op jit(solution)/shard_map/ppermute | solution.py:448
  11.0 5.3 %collective-permute-start.5 = (bf16[240,128]{1,0:T(8,128)(2,1)S(1)}, bf16[240,128]{1,0:T(8,128)(2,1)S(1)}, u32[]{:S(2)}, u32[]{:S(2)}) collective-permute-start(bf16[240,128]{1,0:T(8,128)(2,1)S(1)} %join.3), channel_id=1, source_target_pairs={{0,9},{1,8},{2,11},{3,10},{4,13},{5,12},{6,15},{7,14},{8,1},{9,0},... | collective-permute-start | bytes 184328 | tf_op jit(solution)/shard_map/ppermute | solution.py:448
  12.4 4.9 %collective-permute-start.3 = (bf16[240,128]{1,0:T(8,128)(2,1)S(1)}, bf16[240,128]{1,0:T(8,128)(2,1)S(1)}, u32[]{:S(2)}, u32[]{:S(2)}) collective-permute-start(bf16[240,128]{1,0:T(8,128)(2,1)S(1)} %collective-permute-done.2.refs_2_), channel_id=1, source_target_pairs={{0,1},{1,0},{2,3},{3,2},{4,5},{5,4},{6,7},{7,6},{8,9},{9,8},{10,11... | collective-permute-start | bytes 184328 | tf_op jit(solution)/shard_map/ppermute | solution.py:448
  15.1 4.2 %collective-permute-start.7 = (bf16[240,128]{1,0:T(8,128)(2,1)S(1)}, bf16[240,128]{1,0:T(8,128)(2,1)S(1)}, u32[]{:S(2)}, u32[]{:S(2)}) collective-permute-start(bf16[240,128]{1,0:T(8,128)(2,1)S(1)} %collective-permute-done.6.refs_6_), channel_id=1, source_target_pairs={{0,1},{1,0},{2,3},{3,2},{4,5},{5,4},{6,7},{7,6},{8,9},{9,8},{10,11... | collective-permute-start | bytes 184328 | tf_op jit(solution)/shard_map/ppermute | solution.py:448
  27.1 9.6 %collective-permute-start.10 = (bf16[240,128]{1,0:T(8,128)(2,1)S(1)}, bf16[240,128]{1,0:T(8,128)(2,1)S(1)}, u32[]{:S(2)}, u32[]{:S(2)}) collective-permute-start(bf16[240,128]{1,0:T(8,128)(2,1)S(1)} %get-tuple-element.32), channel_id=1, source_target_pairs={{0,3},{1,2},{2,1},{3,0},{4,7},{5,6},{6,5},{7,4},{8,11},{9,10},{10,... | collective-permute-start | bytes 184328 | tf_op jit(solution)/shard_map/ppermute | solution.py:443
  30.6 6.1 %collective-permute-start.8 = (bf16[240,128]{1,0:T(8,128)(2,1)S(1)}, bf16[240,128]{1,0:T(8,128)(2,1)S(1)}, u32[]{:S(2)}, u32[]{:S(2)}) collective-permute-start(bf16[240,128]{1,0:T(8,128)(2,1)S(1)} %get-tuple-element.30), channel_id=1, source_target_pairs={{0,1},{1,0},{2,3},{3,2},{4,5},{5,4},{6,7},{7,6},{8,9},{9,8},{10,11... | collective-permute-start | bytes 184328 | tf_op jit(solution)/shard_map/ppermute | solution.py:443
  30.6 6.1 %collective-permute-start.9 = (bf16[240,128]{1,0:T(8,128)(2,1)S(1)}, bf16[240,128]{1,0:T(8,128)(2,1)S(1)}, u32[]{:S(2)}, u32[]{:S(2)}) collective-permute-start(bf16[240,128]{1,0:T(8,128)(2,1)S(1)} %get-tuple-element.31), channel_id=1, source_target_pairs={{0,2},{1,3},{2,0},{3,1},{4,6},{5,7},{6,4},{7,5},{8,10},{9,11},{10,... | collective-permute-start | bytes 184328 | tf_op jit(solution)/shard_map/ppermute | solution.py:443
  31.5 11.2 %copy-start.3 = (s32[4,768]{1,0:T(4,128)S(1)}, s32[4,768]{1,0:T(4,128)}, u32[]{:S(2)}) copy-start(s32[4,768]{1,0:T(4,128)} %pattern.1) | copy-start | bytes 36868
  31.5 11.2 %copy-start.4 = (s32[8,2]{0,1:T(2,128)S(1)}, s32[8,2]{0,1:T(2,128)}, u32[]{:S(2)}) copy-start(s32[8,2]{0,1:T(2,128)} %param.13) | copy-start | bytes 196
  36.7 1.3 %collective-permute-start.11 = (bf16[128,128]{1,0:T(8,128)(2,1)S(1)}, bf16[128,128]{1,0:T(8,128)(2,1)S(1)}, u32[]{:S(2)}, u32[]{:S(2)}) collective-permute-start(bf16[128,128]{1,0:T(8,128)(2,1)S(1)} %get-tuple-element.38), channel_id=1, source_target_pairs={{0,4},{4,0},{8,12},{12,8},{1,5},{5,1},{9,13},{13,9},{2,6},{6,2},{1... | collective-permute-start | bytes 98312 | tf_op jit(solution)/shard_map/ppermute | solution.py:443
  38.0 4.7 %collective-permute-start.12 = (bf16[128,128]{1,0:T(8,128)(2,1)S(1)}, bf16[128,128]{1,0:T(8,128)(2,1)S(1)}, u32[]{:S(2)}, u32[]{:S(2)}) collective-permute-start(bf16[128,128]{1,0:T(8,128)(2,1)S(1)} %get-tuple-element.40), channel_id=1, source_target_pairs={{0,8},{4,12},{8,0},{12,4},{1,9},{5,13},{9,1},{13,5},{2,10},{6,14},... | collective-permute-start | bytes 98312 | tf_op jit(solution)/shard_map/ppermute | solution.py:443
